TPU v7x, 256 devices: a whole 4x4x8 slice. The times are simulated.
256 devices in a mesh: section: 16 (over y, z_hi), ctx: 16 (over x, z_lo, core).
Axes of the slice: x: 4, y: 4, z: 8 (z_hi: 4, z_lo: 2; z = z_hi * 2 + z_lo), core: 2. Of those that a mesh axis runs over, the one named last changes fastest.
Arguments:
- queries: bfloat16 [16, 2048, 4096], P('section', 'ctx'), may hold values from -50 to 50, as said below
- keys: bfloat16 [16, 2048, 512], P('section', 'ctx'), may hold values from -5 to 5
- values: bfloat16 [16, 2048, 512], P('section', 'ctx'), may hold values from -12 to 12
- residual: bfloat16 [2048, 4096], P('ctx'), may hold values from -6 to 6
- span_map: int32 [16], replicated, may hold values from 0 to 15, as said below
Outputs:
- hidden_states: bfloat16 [16, 2048, 4096], P('section', 'ctx')
Inputs may be any that keep to these rules, and one draw needn't show every extreme that they name: `queries`: queries of some rows may be large multiples of a visible key. `span_map`: each of the 16 spans appears exactly once.
All inputs are finite; a program needn't handle non-finite values.
Results may differ from a plain program's by a relative error of at most 0.008.
Values may be sent and summed in bfloat16 or wider, within the bound.
No kernel may reach another device: no remote copies, remote signals or barrier semaphores. Data moves between devices by JAX's collectives and lax.ppermute only.
A program may use at most 128 MiB of HBM per device.

v0:
```python
import functools
import math

import jax
import jax.numpy as jnp
from jax import lax
from jax.experimental import pallas as pl
from jax.experimental.pallas import tpu as pltpu
from jax.sharding import PartitionSpec as P

KEY_VALUE_HEADS = 4
GROUP = 8
HEAD_SIZE = 128
TOK = 128
SPANS = 16
TRACE = SPANS * TOK
WIDTH = KEY_VALUE_HEADS * HEAD_SIZE
RING = 4
PAIR = 2 * HEAD_SIZE
EXP2_SCALE = math.log2(math.e) / math.sqrt(HEAD_SIZE)
HIDDEN = -1e30
VMEM_LIMIT = 24 * 2**20
CHUNKS = 2
PART = KEY_VALUE_HEADS // CHUNKS

SIDE = PART * HEAD_SIZE

UNITS = [(dx, dz, dc) for dc in range(2) for dz in range(2) for dx in range(4)]


def ctx_pairs(dx, dz, dc):
    pairs = []
    for i in range(SPANS):
        x, z, c = i // 4, i // 2 % 2, i % 2
        pairs.append((i, (x + dx) % 4 * 4 + (z ^ dz) * 2 + (c ^ dc)))
    return pairs


def ctx_move(unit, dx, dz, dc):
    return lax.ppermute(unit, "ctx", ctx_pairs(dx, dz, dc))


def turn_pairs(steps):
    return [(i, i // RING * RING + (i + steps) % RING) for i in range(RING * RING)]


def climb_pairs(steps):
    return [(i, (i + RING * steps) % (RING * RING)) for i in range(RING * RING)]


def pinned(x):
    return pltpu.with_memory_space_constraint(x, pltpu.HBM)


def join_kernel(k_ref, v_ref, o_ref, sems):
    copies = []
    for chunk in range(CHUNKS):
        for side, source in enumerate((k_ref, v_ref)):
            copies.append(
                pltpu.make_async_copy(
                    source.at[0, :, pl.ds(chunk * SIDE, SIDE)],
                    o_ref.at[:, pl.ds((2 * chunk + side) * SIDE, SIDE)],
                    sems.at[chunk, side],
                )
            )
    for copy in copies:
        copy.start()
    for copy in copies:
        copy.wait()


def join(keys, values):
    return pl.pallas_call(
        join_kernel,
        in_specs=[pl.BlockSpec(memory_space=pltpu.HBM)] * 2,
        out_specs=pl.BlockSpec(memory_space=pltpu.VMEM),
        out_shape=jax.ShapeDtypeStruct((TOK, 2 * WIDTH), jnp.bfloat16),
        scratch_shapes=[pltpu.SemaphoreType.DMA((CHUNKS, 2))],
        compiler_params=pltpu.CompilerParams(vmem_limit_bytes=2 * 2**20),
        name="join",
    )(pinned(keys), pinned(values))


def gather(keys, values):
    held = {(0, 0, 0): join(keys, values)}
    for dx, dz, source in (
        (0, 1, (0, 0, 0)),
        (1, 0, (0, 0, 0)),
        (3, 0, (0, 0, 0)),
        (0, 1, (1, 0, 0)),
        (1, 0, (1, 0, 0)),
        (3, 0, (0, 1, 0)),
        (0, 1, (2, 0, 0)),
    ):
        target = ((source[0] + dx) % 4, source[1] ^ dz, 0)
        held[target] = ctx_move(held[source], dx, dz, 0)
    for dz in range(2):
        for dx in range(4):
            held[dx, dz, 1] = ctx_move(held[dx, dz, 0], 0, 0, 1)
    return [held[unit] for unit in UNITS]


def attention_kernel(chunk, span_map, ctx, section, q_hbm, *refs):
    units, o_refs = refs[:SPANS], refs[SPANS : SPANS + RING]
    q_ref, keys, vals, sems = refs[SPANS + RING :]
    copies = []
    for part in range(PART):
        width = GROUP * HEAD_SIZE
        copies.append(
            pltpu.make_async_copy(
                q_hbm.at[:, pl.ds((chunk * PART + part) * width, width)],
                q_ref.at[part],
                sems.at[part],
            )
        )
        copies[-1].start()

    key_row = lax.broadcasted_iota(jnp.int32, (TOK, TOK), 0)
    query_row = lax.broadcasted_iota(jnp.int32, (TOK, TOK), 1)
    one_hot = jnp.where(key_row == query_row, 1.0, 0.0).astype(jnp.bfloat16)
    me = ctx[0]
    my_span = span_map[me]
    x, z, c = me // 4, me // 2 % 2, me % 2
    for block, (dx, dz, dc) in enumerate(UNITS):
        source = (x + 4 - dx) % 4 * 4 + (z + dz) % 2 * 2 + (c + dc) % 2
        ahead = (span_map[source] - my_span) * TOK + key_row - query_row
        mask = jnp.where(ahead > 0, HIDDEN, 0.0).astype(jnp.bfloat16)
        rows = slice(block * TOK, (block + 1) * TOK)
        for part in range(PART):
            first = chunk * 2 * SIDE + part * HEAD_SIZE
            keys[part, rows, :HEAD_SIZE] = units[block][:, first : first + HEAD_SIZE]
            keys[part, rows, HEAD_SIZE:] = mask
            first += SIDE
            vals[part, rows, :HEAD_SIZE] = units[block][:, first : first + HEAD_SIZE]
    for part in range(PART):
        vals[part, :, HEAD_SIZE:] = jnp.ones((TRACE, HEAD_SIZE), jnp.bfloat16)
    place = section[0] % RING

    def score(part, steps):
        first = pl.multiple_of((place + steps) % RING * PAIR, PAIR)
        q = q_ref[part, :, pl.ds(first, PAIR)]
        q = jnp.concatenate(
            [
                jnp.concatenate([q[:, :HEAD_SIZE], one_hot], axis=1),
                jnp.concatenate([q[:, HEAD_SIZE:], one_hot], axis=1),
            ],
            axis=0,
        )
        return lax.dot_general(
            q, keys[part], (((1,), (1,)), ((), ())), preferred_element_type=jnp.float32
        )

    def weigh(scores):
        peak = jnp.max(scores, axis=1, keepdims=True)
        return jnp.exp2((scores - peak) * EXP2_SCALE).astype(jnp.bfloat16)

    def mix(weights, part, steps):
        mixed = jnp.dot(weights, vals[part], preferred_element_type=jnp.float32)
        result = (mixed[:, :HEAD_SIZE] / mixed[:, HEAD_SIZE:]).astype(jnp.bfloat16)
        result = jnp.concatenate([result[:TOK], result[TOK:]], axis=1)
        o_refs[steps][:, pl.ds(pl.multiple_of(part * PAIR, PAIR), PAIR)] = result

    for copy in copies:
        copy.wait()

    @pl.loop(0, PART)
    def _(part):
        scores = weights = None
        for steps in range(RING + 2):
            upcoming = score(part, steps) if steps < RING else None
            if weights is not None:
                mix(weights, part, steps - 2)
            weights = None if scores is None else weigh(scores)
            scores = upcoming


def attention(span_map, ctx, section, queries, units, chunk):
    smem = pl.BlockSpec(memory_space=pltpu.SMEM)
    vmem = pl.BlockSpec(memory_space=pltpu.VMEM)
    return pl.pallas_call(
        functools.partial(attention_kernel, chunk),
        in_specs=[smem, smem, smem, pl.BlockSpec(memory_space=pltpu.HBM)] + [vmem] * SPANS,
        out_specs=[vmem] * RING,
        out_shape=[jax.ShapeDtypeStruct((TOK, PART * PAIR), jnp.bfloat16)] * RING,
        scratch_shapes=[
            pltpu.VMEM((PART, TOK, GROUP * HEAD_SIZE), jnp.bfloat16),
            pltpu.VMEM((PART, TRACE, PAIR), jnp.bfloat16),
            pltpu.VMEM((PART, TRACE, PAIR), jnp.bfloat16),
            pltpu.SemaphoreType.DMA((PART,)),
        ],
        compiler_params=pltpu.CompilerParams(vmem_limit_bytes=VMEM_LIMIT),
        cost_estimate=pl.CostEstimate(
            flops=PART * GROUP * TOK * TRACE * PAIR * 2 * 2,
            bytes_accessed=PART * (TRACE * PAIR + GROUP * TOK * PAIR) * 2,
            transcendentals=PART * GROUP * TOK * TRACE,
        ),
        name="attention",
    )(pinned(span_map), ctx, section, pinned(queries), *units)


def total_kernel(a, b, c, d, o_ref):
    f32 = jnp.float32
    o_ref[...] = (
        a[...].astype(f32) + b[...].astype(f32) + (c[...].astype(f32) + d[...].astype(f32))
    ).astype(jnp.bfloat16)


def row_total(slabs):
    return pl.pallas_call(
        total_kernel,
        in_specs=[pl.BlockSpec(memory_space=pltpu.VMEM)] * RING,
        out_specs=pl.BlockSpec(memory_space=pltpu.VMEM),
        out_shape=jax.ShapeDtypeStruct((TOK, PART * PAIR), jnp.bfloat16),
        compiler_params=pltpu.CompilerParams(vmem_limit_bytes=4 * 2**20),
        name="row_total",
    )(*slabs)


def prefix_kernel(chunk, section, residual_ref, *refs):
    slabs, below, outs = refs[:RING], refs[RING : 2 * RING - 1], refs[2 * RING - 1 : 3 * RING - 1]
    ordered, summed = refs[3 * RING - 1 :]
    place, row = section[0] % RING, section[0] // RING
    for steps in range(RING):
        ordered[(place + RING - steps) % RING] = slabs[steps][...]
    for part in range(PART):
        columns = slice(part * PAIR, (part + 1) * PAIR)
        first = (chunk * PART + part) * GROUP * HEAD_SIZE + place * PAIR
        state = residual_ref[:, pl.ds(pl.multiple_of(first, PAIR), PAIR)].astype(jnp.float32)
        for steps, rows in enumerate(below, 1):
            earlier = rows[:, columns].astype(jnp.float32)
            state = state + jnp.where(row >= steps, earlier, 0.0)
        for layer in range(RING):
            state = state + ordered[layer, :, columns].astype(jnp.float32)
            summed[layer, :, columns] = state.astype(jnp.bfloat16)
    for steps in range(RING):
        outs[steps][...] = summed[(place + steps) % RING]


def prefix(section, residual, slabs, below, chunk):
    slab = jax.ShapeDtypeStruct((TOK, PART * PAIR), jnp.bfloat16)
    whole = pl.BlockSpec(memory_space=pltpu.VMEM)
    return pl.pallas_call(
        functools.partial(prefix_kernel, chunk),
        in_specs=[pl.BlockSpec(memory_space=pltpu.SMEM)] + [whole] * (2 * RING),
        out_specs=[whole] * RING,
        out_shape=[slab] * RING,
        scratch_shapes=[
            pltpu.VMEM((RING, TOK, PART * PAIR), jnp.bfloat16),
            pltpu.VMEM((RING, TOK, PART * PAIR), jnp.bfloat16),
        ],
        compiler_params=pltpu.CompilerParams(vmem_limit_bytes=8 * 2**20),
        name="prefix",
    )(section, residual, *slabs, *below)


def assemble_kernel(section, *refs):
    slabs, o_ref = refs[:-1], refs[-1]
    place = section[0] % RING
    for chunk in range(CHUNKS):
        for steps in range(RING):
            column = (place + RING - steps) % RING * PAIR
            for part in range(PART):
                first = (chunk * PART + part) * GROUP * HEAD_SIZE + column
                o_ref[0, :, pl.ds(pl.multiple_of(first, PAIR), PAIR)] = slabs[
                    chunk * RING + steps
                ][:, part * PAIR : (part + 1) * PAIR]


def assemble(section, slabs):
    whole = pl.BlockSpec(memory_space=pltpu.VMEM)
    width = KEY_VALUE_HEADS * GROUP * HEAD_SIZE
    return pl.pallas_call(
        assemble_kernel,
        in_specs=[pl.BlockSpec(memory_space=pltpu.SMEM)] + [whole] * len(slabs),
        out_specs=whole,
        out_shape=jax.ShapeDtypeStruct((1, TOK, width), jnp.bfloat16),
        compiler_params=pltpu.CompilerParams(vmem_limit_bytes=8 * 2**20),
        name="assemble",
    )(section, *slabs)


def turn(slabs):
    return [slabs[0]] + [
        lax.ppermute(slabs[steps], "section", turn_pairs(steps)) for steps in range(1, RING)
    ]


def body(queries, keys, values, residual, span_map):
    ctx = lax.axis_index("ctx")[None]
    section = lax.axis_index("section")[None]
    units = gather(keys, values)
    slabs = [
        turn(attention(span_map, ctx, section, queries[0], units, chunk))
        for chunk in range(CHUNKS)
    ]
    finished, sums = [], None
    for chunk in range(CHUNKS):
        total = row_total(slabs[chunk])
        if sums is not None:
            total, *sums = lax.optimization_barrier((total, *sums))
            finished += turn(sums)
        below = [lax.ppermute(total, "section", climb_pairs(s)) for s in range(1, RING)]
        sums = prefix(section, residual, slabs[chunk], below, chunk)
    finished += turn(sums)
    return assemble(section, finished)


def solution(mesh):
    placed = (
        P("section", "ctx", None),
        P("section", "ctx", None),
        P("section", "ctx", None),
        P("ctx", None),
        P(),
    )
    return jax.shard_map(
        body, mesh=mesh, in_specs=placed, out_specs=P("section", "ctx", None), check_vma=False
    )
```

profile of v0, /device:TPU:1, one launch (start us, length us, event | category | flops | bytes accessed | tf_op | source)
XLA Modules:
  0.0 106.5 jit_solution(13057378699058908443)
XLA Ops:
  1.0 2.1 %collective-permute-start = (bf16[128,1024]{1,0:T(8,128)(2,1)S(1)}, bf16[128,1024]{1,0:T(8,128)(2,1)S(1)}, u32[]{:S(2)}, u32[]{:S(2)}) collective-permute-start(bf16[128,1024]{1,0:T(8,128)(2,1)S(1)} %join.1.refs_0_), channel_id=1, source_target_pairs={{0,4},{1,5},{2,6},{3,7},{4,8},{5,9},{6,10},{7,11},{8,12},{9,13},{1... | collective-permute-start | bytes 786440 | tf_op jit(solution)/shard_map/ppermute | solution.py:40
  10.0 2.1 %collective-permute-start.11 = (bf16[128,1024]{1,0:T(8,128)(2,1)S(1)}, bf16[128,1024]{1,0:T(8,128)(2,1)S(1)}, u32[]{:S(2)}, u32[]{:S(2)}) collective-permute-start(bf16[128,1024]{1,0:T(8,128)(2,1)S(1)} %collective-permute-done.3.refs_4_), channel_id=1, source_target_pairs={{0,1},{1,0},{2,3},{3,2},{4,5},{5,4},{6,7},{7,6},{8,9},{9,8},{10,11... | collective-permute-start | bytes 786440 | tf_op jit(solution)/shard_map/ppermute | solution.py:40
  12.1 2.7 %collective-permute-start.6 = (bf16[128,1024]{1,0:T(8,128)(2,1)S(1)}, bf16[128,1024]{1,0:T(8,128)(2,1)S(1)}, u32[]{:S(2)}, u32[]{:S(2)}) collective-permute-start(bf16[128,1024]{1,0:T(8,128)(2,1)S(1)} %collective-permute-done.3.refs_4_), channel_id=1, source_target_pairs={{0,12},{1,13},{2,14},{3,15},{4,0},{5,1},{6,2},{7,3},{8,4},{9,5},{1... | collective-permute-start | bytes 786440 | tf_op jit(solution)/shard_map/ppermute | solution.py:40
  16.7 2.7 %collective-permute-start.5 = (bf16[128,1024]{1,0:T(8,128)(2,1)S(1)}, bf16[128,1024]{1,0:T(8,128)(2,1)S(1)}, u32[]{:S(2)}, u32[]{:S(2)}) collective-permute-start(bf16[128,1024]{1,0:T(8,128)(2,1)S(1)} %collective-permute-done.1.refs_2_), channel_id=1, source_target_pairs={{0,2},{1,3},{2,0},{3,1},{4,6},{5,7},{6,4},{7,5},{8,10},{9,11},{10,... | collective-permute-start | bytes 786440 | tf_op jit(solution)/shard_map/ppermute | solution.py:40
  19.4 2.7 %collective-permute-start.8 = (bf16[128,1024]{1,0:T(8,128)(2,1)S(1)}, bf16[128,1024]{1,0:T(8,128)(2,1)S(1)}, u32[]{:S(2)}, u32[]{:S(2)}) collective-permute-start(bf16[128,1024]{1,0:T(8,128)(2,1)S(1)} %collective-permute-done.refs_1_), channel_id=1, source_target_pairs={{0,1},{1,0},{2,3},{3,2},{4,5},{5,4},{6,7},{7,6},{8,9},{9,8},{10,11... | collective-permute-start | bytes 786440 | tf_op jit(solution)/shard_map/ppermute | solution.py:40
  24.5 4.2 %collective-permute-done.5.refs_6_ = bf16[128,1024]{1,0:T(8,128)(2,1)S(1)} collective-permute-done((bf16[128,1024]{1,0:T(8,128)(2,1)S(1)}, bf16[128,1024]{1,0:T(8,128)(2,1)S(1)}, u32[]{:S(2)}, u32[]{:S(2)}) %collective-permute-start.5) | collective-permute-done | bytes 262176 | tf_op jit(solution)/shard_map/ppermute | solution.py:40
  30.9 7.6 %attention.3 = (bf16[128,512]{1,0:T(8,128)(2,1)S(1)}, bf16[128,512]{1,0:T(8,128)(2,1)S(1)}, bf16[128,512]{1,0:T(8,128)(2,1)S(1)}, bf16[128,512]{1,0:T(8,128)(2,1)S(1)}) custom-call(s32[16]{0:T(128)} %span_map.3, s32[1]{0:T(128)} %bitcast.1.ctx, s32[1]{0:T(128)} %bitcast.section, bf16[128,4096]{1,0:T(8,128)(2,1)} %bitcast.3, ...), custom_call_target="tpu_custom_call" | custom-call | flops 4294967296 | bytes 3145728 | tf_op jit(solution)/shard_map/attention/pallas_call | solution.py:180
  38.5 3.1 %collective-permute-start.18 = (bf16[128,512]{1,0:T(8,128)(2,1)S(1)}, bf16[128,512]{1,0:T(8,128)(2,1)S(1)}, u32[]{:S(2)}, u32[]{:S(2)}) collective-permute-start(bf16[128,512]{1,0:T(8,128)(2,1)S(1)} %get-tuple-element.31), channel_id=1, source_target_pairs={{0,16},{16,32},{32,48},{48,0},{64,80},{80,96},{96,112},{112,64},{1... | collective-permute-start | bytes 393224 | tf_op jit(solution)/shard_map/ppermute | solution.py:284
  41.5 4.9 %collective-permute-start.19 = (bf16[128,512]{1,0:T(8,128)(2,1)S(1)}, bf16[128,512]{1,0:T(8,128)(2,1)S(1)}, u32[]{:S(2)}, u32[]{:S(2)}) collective-permute-start(bf16[128,512]{1,0:T(8,128)(2,1)S(1)} %get-tuple-element.32), channel_id=1, source_target_pairs={{0,32},{16,48},{32,0},{48,16},{64,96},{80,112},{96,64},{112,80},{1... | collective-permute-start | bytes 393224 | tf_op jit(solution)/shard_map/ppermute | solution.py:284
  46.5 2.4 %collective-permute-start.20 = (bf16[128,512]{1,0:T(8,128)(2,1)S(1)}, bf16[128,512]{1,0:T(8,128)(2,1)S(1)}, u32[]{:S(2)}, u32[]{:S(2)}) collective-permute-start(bf16[128,512]{1,0:T(8,128)(2,1)S(1)} %get-tuple-element.33), channel_id=1, source_target_pairs={{0,48},{16,0},{32,16},{48,32},{64,112},{80,64},{96,80},{112,96},{1... | collective-permute-start | bytes 393224 | tf_op jit(solution)/shard_map/ppermute | solution.py:284
  48.8 7.6 %attention.2 = (bf16[128,512]{1,0:T(8,128)(2,1)S(1)}, bf16[128,512]{1,0:T(8,128)(2,1)S(1)}, bf16[128,512]{1,0:T(8,128)(2,1)S(1)}, bf16[128,512]{1,0:T(8,128)(2,1)S(1)}) custom-call(s32[16]{0:T(128)} %span_map.3, s32[1]{0:T(128)} %bitcast.1.ctx, s32[1]{0:T(128)} %bitcast.section, bf16[128,4096]{1,0:T(8,128)(2,1)} %bitcast.4, ...), custom_call_target="tpu_custom_call" | custom-call | flops 4294967296 | bytes 3145728 | tf_op jit(solution)/shard_map/attention/pallas_call | solution.py:180
  56.5 2.1 %collective-permute-start.16 = (bf16[128,512]{1,0:T(8,128)(2,1)S(1)}, bf16[128,512]{1,0:T(8,128)(2,1)S(1)}, u32[]{:S(2)}, u32[]{:S(2)}) collective-permute-start(bf16[128,512]{1,0:T(8,128)(2,1)S(1)} %get-tuple-element.28), channel_id=1, source_target_pairs={{0,32},{16,48},{32,0},{48,16},{64,96},{80,112},{96,64},{112,80},{1... | collective-permute-start | bytes 393224 | tf_op jit(solution)/shard_map/ppermute | solution.py:284
  58.6 2.5 %collective-permute-start.17 = (bf16[128,512]{1,0:T(8,128)(2,1)S(1)}, bf16[128,512]{1,0:T(8,128)(2,1)S(1)}, u32[]{:S(2)}, u32[]{:S(2)}) collective-permute-start(bf16[128,512]{1,0:T(8,128)(2,1)S(1)} %get-tuple-element.29), channel_id=1, source_target_pairs={{0,48},{16,0},{32,16},{48,32},{64,112},{80,64},{96,80},{112,96},{1... | collective-permute-start | bytes 393224 | tf_op jit(solution)/shard_map/ppermute | solution.py:284
  61.2 2.8 %collective-permute-start.23 = (bf16[128,512]{1,0:T(8,128)(2,1)S(1)}, bf16[128,512]{1,0:T(8,128)(2,1)S(1)}, u32[]{:S(2)}, u32[]{:S(2)}) collective-permute-start(bf16[128,512]{1,0:T(8,128)(2,1)S(1)} %row_total.3), channel_id=1, source_target_pairs={{0,192},{16,208},{32,224},{48,240},{64,0},{80,16},{96,32},{112,48}... | collective-permute-start | bytes 393224 | tf_op jit(solution)/shard_map/ppermute | solution.py:302
  65.4 4.0 %collective-permute-done.16.c.refs_2_ = bf16[128,512]{1,0:T(8,128)(2,1)S(1)} collective-permute-done((bf16[128,512]{1,0:T(8,128)(2,1)S(1)}, bf16[128,512]{1,0:T(8,128)(2,1)S(1)}, u32[]{:S(2)}, u32[]{:S(2)}) %collective-permute-start.16) | collective-permute-done | bytes 131104 | tf_op jit(solution)/shard_map/ppermute | solution.py:284
  69.4 4.8 %collective-permute-done.17.d.refs_3_ = bf16[128,512]{1,0:T(8,128)(2,1)S(1)} collective-permute-done((bf16[128,512]{1,0:T(8,128)(2,1)S(1)}, bf16[128,512]{1,0:T(8,128)(2,1)S(1)}, u32[]{:S(2)}, u32[]{:S(2)}) %collective-permute-start.17) | collective-permute-done | bytes 131104 | tf_op jit(solution)/shard_map/ppermute | solution.py:284
  74.6 2.8 %collective-permute-start.29 = (bf16[128,512]{1,0:T(8,128)(2,1)S(1)}, bf16[128,512]{1,0:T(8,128)(2,1)S(1)}, u32[]{:S(2)}, u32[]{:S(2)}) collective-permute-start(bf16[128,512]{1,0:T(8,128)(2,1)S(1)} %row_total.2), channel_id=1, source_target_pairs={{0,192},{16,208},{32,224},{48,240},{64,0},{80,16},{96,32},{112,48}... | collective-permute-start | bytes 393224 | tf_op jit(solution)/shard_map/ppermute | solution.py:302
  79.2 2.1 %collective-permute-start.25 = (bf16[128,512]{1,0:T(8,128)(2,1)S(1)}, bf16[128,512]{1,0:T(8,128)(2,1)S(1)}, u32[]{:S(2)}, u32[]{:S(2)}) collective-permute-start(bf16[128,512]{1,0:T(8,128)(2,1)S(1)} %get-tuple-element.40), channel_id=1, source_target_pairs={{0,32},{16,48},{32,0},{48,16},{64,96},{80,112},{96,64},{112,80},{1... | collective-permute-start | bytes 393224 | tf_op jit(solution)/shard_map/ppermute | solution.py:284
  81.3 2.5 %collective-permute-start.26 = (bf16[128,512]{1,0:T(8,128)(2,1)S(1)}, bf16[128,512]{1,0:T(8,128)(2,1)S(1)}, u32[]{:S(2)}, u32[]{:S(2)}) collective-permute-start(bf16[128,512]{1,0:T(8,128)(2,1)S(1)} %get-tuple-element.41), channel_id=1, source_target_pairs={{0,48},{16,0},{32,16},{48,32},{64,112},{80,64},{96,80},{112,96},{1... | collective-permute-start | bytes 393224 | tf_op jit(solution)/shard_map/ppermute | solution.py:284
  83.8 2.2 %collective-permute-done.27.refs_4_ = bf16[128,512]{1,0:T(8,128)(2,1)S(1)} collective-permute-done((bf16[128,512]{1,0:T(8,128)(2,1)S(1)}, bf16[128,512]{1,0:T(8,128)(2,1)S(1)}, u32[]{:S(2)}, u32[]{:S(2)}) %collective-permute-start.27) | collective-permute-done | bytes 131104 | tf_op jit(solution)/shard_map/ppermute | solution.py:302
  88.1 1.9 %collective-permute-start.31 = (bf16[128,512]{1,0:T(8,128)(2,1)S(1)}, bf16[128,512]{1,0:T(8,128)(2,1)S(1)}, u32[]{:S(2)}, u32[]{:S(2)}) collective-permute-start(bf16[128,512]{1,0:T(8,128)(2,1)S(1)} %get-tuple-element.45), channel_id=1, source_target_pairs={{0,32},{16,48},{32,0},{48,16},{64,96},{80,112},{96,64},{112,80},{1... | collective-permute-start | bytes 393224 | tf_op jit(solution)/shard_map/ppermute | solution.py:284
  90.0 2.9 %collective-permute-start.32 = (bf16[128,512]{1,0:T(8,128)(2,1)S(1)}, bf16[128,512]{1,0:T(8,128)(2,1)S(1)}, u32[]{:S(2)}, u32[]{:S(2)}) collective-permute-start(bf16[128,512]{1,0:T(8,128)(2,1)S(1)} %get-tuple-element.46), channel_id=1, source_target_pairs={{0,48},{16,0},{32,16},{48,32},{64,112},{80,64},{96,80},{112,96},{1... | collective-permute-start | bytes 393224 | tf_op jit(solution)/shard_map/ppermute | solution.py:284
  92.8 9.2 %collective-permute-done.26.refs_3_ = bf16[128,512]{1,0:T(8,128)(2,1)S(1)} collective-permute-done((bf16[128,512]{1,0:T(8,128)(2,1)S(1)}, bf16[128,512]{1,0:T(8,128)(2,1)S(1)}, u32[]{:S(2)}, u32[]{:S(2)}) %collective-permute-start.26) | collective-permute-done | bytes 131104 | tf_op jit(solution)/shard_map/ppermute | solution.py:284
  102.1 3.4 %collective-permute-done.32.refs_7_ = bf16[128,512]{1,0:T(8,128)(2,1)S(1)} collective-permute-done((bf16[128,512]{1,0:T(8,128)(2,1)S(1)}, bf16[128,512]{1,0:T(8,128)(2,1)S(1)}, u32[]{:S(2)}, u32[]{:S(2)}) %collective-permute-start.32) | collective-permute-done | bytes 131104 | tf_op jit(solution)/shard_map/ppermute | solution.py:284
  (52 shorter events, 21.2 us)
Async XLA Ops:
  4.7 10.1 %collective-permute-start.2 = (bf16[128,1024]{1,0:T(8,128)(2,1)S(1)}, bf16[128,1024]{1,0:T(8,128)(2,1)S(1)}, u32[]{:S(2)}, u32[]{:S(2)}) collective-permute-start(bf16[128,1024]{1,0:T(8,128)(2,1)S(1)} %join.1.refs_0_), channel_id=1, source_target_pairs={{0,12},{1,13},{2,14},{3,15},{4,0},{5,1},{6,2},{7,3},{8,4},{9,5},{1... | collective-permute-start | bytes 786440 | tf_op jit(solution)/shard_map/ppermute | solution.py:40
  6.2 8.9 %collective-permute-start.7 = (bf16[128,1024]{1,0:T(8,128)(2,1)S(1)}, bf16[128,1024]{1,0:T(8,128)(2,1)S(1)}, u32[]{:S(2)}, u32[]{:S(2)}) collective-permute-start(bf16[128,1024]{1,0:T(8,128)(2,1)S(1)} %join.1.refs_0_), channel_id=1, source_target_pairs={{0,1},{1,0},{2,3},{3,2},{4,5},{5,4},{6,7},{7,6},{8,9},{9,8},{10,11... | collective-permute-start | bytes 786440 | tf_op jit(solution)/shard_map/ppermute | solution.py:40
  8.1 8.6 %collective-permute-start.1 = (bf16[128,1024]{1,0:T(8,128)(2,1)S(1)}, bf16[128,1024]{1,0:T(8,128)(2,1)S(1)}, u32[]{:S(2)}, u32[]{:S(2)}) collective-permute-start(bf16[128,1024]{1,0:T(8,128)(2,1)S(1)} %collective-permute-done.refs_1_), channel_id=1, source_target_pairs={{0,4},{1,5},{2,6},{3,7},{4,8},{5,9},{6,10},{7,11},{8,12},{9,13},{1... | collective-permute-start | bytes 786440 | tf_op jit(solution)/shard_map/ppermute | solution.py:40
  10.0 9.4 %collective-permute-start.11 = (bf16[128,1024]{1,0:T(8,128)(2,1)S(1)}, bf16[128,1024]{1,0:T(8,128)(2,1)S(1)}, u32[]{:S(2)}, u32[]{:S(2)}) collective-permute-start(bf16[128,1024]{1,0:T(8,128)(2,1)S(1)} %collective-permute-done.3.refs_4_), channel_id=1, source_target_pairs={{0,1},{1,0},{2,3},{3,2},{4,5},{5,4},{6,7},{7,6},{8,9},{9,8},{10,11... | collective-permute-start | bytes 786440 | tf_op jit(solution)/shard_map/ppermute | solution.py:40
  12.1 10.0 %collective-permute-start.6 = (bf16[128,1024]{1,0:T(8,128)(2,1)S(1)}, bf16[128,1024]{1,0:T(8,128)(2,1)S(1)}, u32[]{:S(2)}, u32[]{:S(2)}) collective-permute-start(bf16[128,1024]{1,0:T(8,128)(2,1)S(1)} %collective-permute-done.3.refs_4_), channel_id=1, source_target_pairs={{0,12},{1,13},{2,14},{3,15},{4,0},{5,1},{6,2},{7,3},{8,4},{9,5},{1... | collective-permute-start | bytes 786440 | tf_op jit(solution)/shard_map/ppermute | solution.py:40
  15.1 7.9 %collective-permute-start.4 = (bf16[128,1024]{1,0:T(8,128)(2,1)S(1)}, bf16[128,1024]{1,0:T(8,128)(2,1)S(1)}, u32[]{:S(2)}, u32[]{:S(2)}) collective-permute-start(bf16[128,1024]{1,0:T(8,128)(2,1)S(1)} %collective-permute-done.refs_1_), channel_id=1, source_target_pairs={{0,2},{1,3},{2,0},{3,1},{4,6},{5,7},{6,4},{7,5},{8,10},{9,11},{10,... | collective-permute-start | bytes 786440 | tf_op jit(solution)/shard_map/ppermute | solution.py:40
  16.7 12.0 %collective-permute-start.5 = (bf16[128,1024]{1,0:T(8,128)(2,1)S(1)}, bf16[128,1024]{1,0:T(8,128)(2,1)S(1)}, u32[]{:S(2)}, u32[]{:S(2)}) collective-permute-start(bf16[128,1024]{1,0:T(8,128)(2,1)S(1)} %collective-permute-done.1.refs_2_), channel_id=1, source_target_pairs={{0,2},{1,3},{2,0},{3,1},{4,6},{5,7},{6,4},{7,5},{8,10},{9,11},{10,... | collective-permute-start | bytes 786440 | tf_op jit(solution)/shard_map/ppermute | solution.py:40
  19.4 10.2 %collective-permute-start.8 = (bf16[128,1024]{1,0:T(8,128)(2,1)S(1)}, bf16[128,1024]{1,0:T(8,128)(2,1)S(1)}, u32[]{:S(2)}, u32[]{:S(2)}) collective-permute-start(bf16[128,1024]{1,0:T(8,128)(2,1)S(1)} %collective-permute-done.refs_1_), channel_id=1, source_target_pairs={{0,1},{1,0},{2,3},{3,2},{4,5},{5,4},{6,7},{7,6},{8,9},{9,8},{10,11... | collective-permute-start | bytes 786440 | tf_op jit(solution)/shard_map/ppermute | solution.py:40
  38.5 20.1 %collective-permute-start.18 = (bf16[128,512]{1,0:T(8,128)(2,1)S(1)}, bf16[128,512]{1,0:T(8,128)(2,1)S(1)}, u32[]{:S(2)}, u32[]{:S(2)}) collective-permute-start(bf16[128,512]{1,0:T(8,128)(2,1)S(1)} %get-tuple-element.31), channel_id=1, source_target_pairs={{0,16},{16,32},{32,48},{48,0},{64,80},{80,96},{96,112},{112,64},{1... | collective-permute-start | bytes 393224 | tf_op jit(solution)/shard_map/ppermute | solution.py:284
  41.5 19.6 %collective-permute-start.19 = (bf16[128,512]{1,0:T(8,128)(2,1)S(1)}, bf16[128,512]{1,0:T(8,128)(2,1)S(1)}, u32[]{:S(2)}, u32[]{:S(2)}) collective-permute-start(bf16[128,512]{1,0:T(8,128)(2,1)S(1)} %get-tuple-element.32), channel_id=1, source_target_pairs={{0,32},{16,48},{32,0},{48,16},{64,96},{80,112},{96,64},{112,80},{1... | collective-permute-start | bytes 393224 | tf_op jit(solution)/shard_map/ppermute | solution.py:284
  46.5 14.6 %collective-permute-start.20 = (bf16[128,512]{1,0:T(8,128)(2,1)S(1)}, bf16[128,512]{1,0:T(8,128)(2,1)S(1)}, u32[]{:S(2)}, u32[]{:S(2)}) collective-permute-start(bf16[128,512]{1,0:T(8,128)(2,1)S(1)} %get-tuple-element.33), channel_id=1, source_target_pairs={{0,48},{16,0},{32,16},{48,32},{64,112},{80,64},{96,80},{112,96},{1... | collective-permute-start | bytes 393224 | tf_op jit(solution)/shard_map/ppermute | solution.py:284
  56.4 8.1 %collective-permute-start.15 = (bf16[128,512]{1,0:T(8,128)(2,1)S(1)}, bf16[128,512]{1,0:T(8,128)(2,1)S(1)}, u32[]{:S(2)}, u32[]{:S(2)}) collective-permute-start(bf16[128,512]{1,0:T(8,128)(2,1)S(1)} %get-tuple-element.27), channel_id=1, source_target_pairs={{0,16},{16,32},{32,48},{48,0},{64,80},{80,96},{96,112},{112,64},{1... | collective-permute-start | bytes 393224 | tf_op jit(solution)/shard_map/ppermute | solution.py:284
  56.5 12.9 %collective-permute-start.16 = (bf16[128,512]{1,0:T(8,128)(2,1)S(1)}, bf16[128,512]{1,0:T(8,128)(2,1)S(1)}, u32[]{:S(2)}, u32[]{:S(2)}) collective-permute-start(bf16[128,512]{1,0:T(8,128)(2,1)S(1)} %get-tuple-element.28), channel_id=1, source_target_pairs={{0,32},{16,48},{32,0},{48,16},{64,96},{80,112},{96,64},{112,80},{1... | collective-permute-start | bytes 393224 | tf_op jit(solution)/shard_map/ppermute | solution.py:284
  58.6 15.6 %collective-permute-start.17 = (bf16[128,512]{1,0:T(8,128)(2,1)S(1)}, bf16[128,512]{1,0:T(8,128)(2,1)S(1)}, u32[]{:S(2)}, u32[]{:S(2)}) collective-permute-start(bf16[128,512]{1,0:T(8,128)(2,1)S(1)} %get-tuple-element.29), channel_id=1, source_target_pairs={{0,48},{16,0},{32,16},{48,32},{64,112},{80,64},{96,80},{112,96},{1... | collective-permute-start | bytes 393224 | tf_op jit(solution)/shard_map/ppermute | solution.py:284
  61.2 13.1 %collective-permute-start.23 = (bf16[128,512]{1,0:T(8,128)(2,1)S(1)}, bf16[128,512]{1,0:T(8,128)(2,1)S(1)}, u32[]{:S(2)}, u32[]{:S(2)}) collective-permute-start(bf16[128,512]{1,0:T(8,128)(2,1)S(1)} %row_total.3), channel_id=1, source_target_pairs={{0,192},{16,208},{32,224},{48,240},{64,0},{80,16},{96,32},{112,48}... | collective-permute-start | bytes 393224 | tf_op jit(solution)/shard_map/ppermute | solution.py:302
  64.0 10.3 %collective-permute-start.22 = (bf16[128,512]{1,0:T(8,128)(2,1)S(1)}, bf16[128,512]{1,0:T(8,128)(2,1)S(1)}, u32[]{:S(2)}, u32[]{:S(2)}) collective-permute-start(bf16[128,512]{1,0:T(8,128)(2,1)S(1)} %row_total.3), channel_id=1, source_target_pairs={{0,128},{16,144},{32,160},{48,176},{64,192},{80,208},{96,224},{112... | collective-permute-start | bytes 393224 | tf_op jit(solution)/shard_map/ppermute | solution.py:302
  64.5 9.8 %collective-permute-start.21 = (bf16[128,512]{1,0:T(8,128)(2,1)S(1)}, bf16[128,512]{1,0:T(8,128)(2,1)S(1)}, u32[]{:S(2)}, u32[]{:S(2)}) collective-permute-start(bf16[128,512]{1,0:T(8,128)(2,1)S(1)} %row_total.3), channel_id=1, source_target_pairs={{0,64},{16,80},{32,96},{48,112},{64,128},{80,144},{96,160},{112,17... | collective-permute-start | bytes 393224 | tf_op jit(solution)/shard_map/ppermute | solution.py:302
  77.8 8.3 %collective-permute-start.27 = (bf16[128,512]{1,0:T(8,128)(2,1)S(1)}, bf16[128,512]{1,0:T(8,128)(2,1)S(1)}, u32[]{:S(2)}, u32[]{:S(2)}) collective-permute-start(bf16[128,512]{1,0:T(8,128)(2,1)S(1)} %row_total.2), channel_id=1, source_target_pairs={{0,64},{16,80},{32,96},{48,112},{64,128},{80,144},{96,160},{112,17... | collective-permute-start | bytes 393224 | tf_op jit(solution)/shard_map/ppermute | solution.py:302
  78.5 11.5 %collective-permute-start.24 = (bf16[128,512]{1,0:T(8,128)(2,1)S(1)}, bf16[128,512]{1,0:T(8,128)(2,1)S(1)}, u32[]{:S(2)}, u32[]{:S(2)}) collective-permute-start(bf16[128,512]{1,0:T(8,128)(2,1)S(1)} %get-tuple-element.39), channel_id=1, source_target_pairs={{0,16},{16,32},{32,48},{48,0},{64,80},{80,96},{96,112},{112,64},{1... | collective-permute-start | bytes 393224 | tf_op jit(solution)/shard_map/ppermute | solution.py:284
  79.2 13.6 %collective-permute-start.25 = (bf16[128,512]{1,0:T(8,128)(2,1)S(1)}, bf16[128,512]{1,0:T(8,128)(2,1)S(1)}, u32[]{:S(2)}, u32[]{:S(2)}) collective-permute-start(bf16[128,512]{1,0:T(8,128)(2,1)S(1)} %get-tuple-element.40), channel_id=1, source_target_pairs={{0,32},{16,48},{32,0},{48,16},{64,96},{80,112},{96,64},{112,80},{1... | collective-permute-start | bytes 393224 | tf_op jit(solution)/shard_map/ppermute | solution.py:284
  81.3 20.8 %collective-permute-start.26 = (bf16[128,512]{1,0:T(8,128)(2,1)S(1)}, bf16[128,512]{1,0:T(8,128)(2,1)S(1)}, u32[]{:S(2)}, u32[]{:S(2)}) collective-permute-start(bf16[128,512]{1,0:T(8,128)(2,1)S(1)} %get-tuple-element.41), channel_id=1, source_target_pairs={{0,48},{16,0},{32,16},{48,32},{64,112},{80,64},{96,80},{112,96},{1... | collective-permute-start | bytes 393224 | tf_op jit(solution)/shard_map/ppermute | solution.py:284
  86.3 15.8 %collective-permute-start.30 = (bf16[128,512]{1,0:T(8,128)(2,1)S(1)}, bf16[128,512]{1,0:T(8,128)(2,1)S(1)}, u32[]{:S(2)}, u32[]{:S(2)}) collective-permute-start(bf16[128,512]{1,0:T(8,128)(2,1)S(1)} %get-tuple-element.44), channel_id=1, source_target_pairs={{0,16},{16,32},{32,48},{48,0},{64,80},{80,96},{96,112},{112,64},{1... | collective-permute-start | bytes 393224 | tf_op jit(solution)/shard_map/ppermute | solution.py:284
  88.1 14.0 %collective-permute-start.31 = (bf16[128,512]{1,0:T(8,128)(2,1)S(1)}, bf16[128,512]{1,0:T(8,128)(2,1)S(1)}, u32[]{:S(2)}, u32[]{:S(2)}) collective-permute-start(bf16[128,512]{1,0:T(8,128)(2,1)S(1)} %get-tuple-element.45), channel_id=1, source_target_pairs={{0,32},{16,48},{32,0},{48,16},{64,96},{80,112},{96,64},{112,80},{1... | collective-permute-start | bytes 393224 | tf_op jit(solution)/shard_map/ppermute | solution.py:284
  90.0 15.5 %collective-permute-start.32 = (bf16[128,512]{1,0:T(8,128)(2,1)S(1)}, bf16[128,512]{1,0:T(8,128)(2,1)S(1)}, u32[]{:S(2)}, u32[]{:S(2)}) collective-permute-start(bf16[128,512]{1,0:T(8,128)(2,1)S(1)} %get-tuple-element.46), channel_id=1, source_target_pairs={{0,48},{16,0},{32,16},{48,32},{64,112},{80,64},{96,80},{112,96},{1... | collective-permute-start | bytes 393224 | tf_op jit(solution)/shard_map/ppermute | solution.py:284
  (10 other events, 76.0 us)
where the time goes:
time: 107 us
  starting transfers between devices  58.6 us (55%)
  waiting for transfers between devices  30 us (28%)
  Pallas kernels  17.9 us (17%)
    ppermute x12, starting transfers between devices, turn(): lax.ppermute(slabs[steps], 'section', turn_pairs(steps))  26.9 us
    ppermute x15, starting transfers between devices, ctx_move(): return lax.ppermute(unit, 'ctx', ctx_pairs(dx, dz, dc))  23.6 us
    ppermute x12, waiting for transfers between devices, turn(): lax.ppermute(slabs[steps], 'section', turn_pairs(steps))  21.4 us
    pallas_call x2, Pallas kernels, attention(): pl.pallas_call(functools.partial(attention_kernel, chunk), in_specs=[smem...  15.1 us
    ppermute x6, starting transfers between devices, body(): lax.ppermute(total, 'section', climb_pairs(s))  8.12 us
    ppermute x15, waiting for transfers between devices, ctx_move(): return lax.ppermute(unit, 'ctx', ctx_pairs(dx, dz, dc))  6.32 us
    ppermute x6, waiting for transfers between devices, body(): lax.ppermute(total, 'section', climb_pairs(s))  2.25 us
  transfers between devices with their start and end apart: 33, of which 9 were waited for; matrix products, arithmetic and copies ran while one was open for 0% of the time, Pallas kernels for 7%

commit v1 on v0

--- a/solution.py
+++ b/solution.py
@@ -19,7 +19,7 @@
 PAIR = 2 * HEAD_SIZE
 EXP2_SCALE = math.log2(math.e) / math.sqrt(HEAD_SIZE)
 HIDDEN = -1e30
-VMEM_LIMIT = 24 * 2**20
+VMEM_LIMIT = 20 * 2**20
 CHUNKS = 2
 PART = KEY_VALUE_HEADS // CHUNKS
 
@@ -100,9 +100,9 @@
     return [held[unit] for unit in UNITS]
 
 
-def attention_kernel(chunk, span_map, ctx, section, q_hbm, *refs):
-    units, o_refs = refs[:SPANS], refs[SPANS : SPANS + RING]
-    q_ref, keys, vals, sems = refs[SPANS + RING :]
+def attention_kernel(chunk, span_map, ctx, q_hbm, *refs):
+    units, o_ref = refs[:SPANS], refs[SPANS]
+    q_ref, keys, vals, sems = refs[SPANS + 1 :]
     copies = []
     for part in range(PART):
         width = GROUP * HEAD_SIZE
@@ -134,11 +134,9 @@
             vals[part, rows, :HEAD_SIZE] = units[block][:, first : first + HEAD_SIZE]
     for part in range(PART):
         vals[part, :, HEAD_SIZE:] = jnp.ones((TRACE, HEAD_SIZE), jnp.bfloat16)
-    place = section[0] % RING
-
-    def score(part, steps):
-        first = pl.multiple_of((place + steps) % RING * PAIR, PAIR)
-        q = q_ref[part, :, pl.ds(first, PAIR)]
+
+    def score(part, owner):
+        q = q_ref[part, :, owner * PAIR : (owner + 1) * PAIR]
         q = jnp.concatenate(
             [
                 jnp.concatenate([q[:, :HEAD_SIZE], one_hot], axis=1),
@@ -154,11 +152,11 @@
         peak = jnp.max(scores, axis=1, keepdims=True)
         return jnp.exp2((scores - peak) * EXP2_SCALE).astype(jnp.bfloat16)
 
-    def mix(weights, part, steps):
+    def mix(weights, part, owner):
         mixed = jnp.dot(weights, vals[part], preferred_element_type=jnp.float32)
         result = (mixed[:, :HEAD_SIZE] / mixed[:, HEAD_SIZE:]).astype(jnp.bfloat16)
         result = jnp.concatenate([result[:TOK], result[TOK:]], axis=1)
-        o_refs[steps][:, pl.ds(pl.multiple_of(part * PAIR, PAIR), PAIR)] = result
+        o_ref[owner, :, pl.ds(pl.multiple_of(part * PAIR, PAIR), PAIR)] = result
 
     for copy in copies:
         copy.wait()
@@ -166,22 +164,22 @@
     @pl.loop(0, PART)
     def _(part):
         scores = weights = None
-        for steps in range(RING + 2):
-            upcoming = score(part, steps) if steps < RING else None
+        for owner in range(RING + 2):
+            upcoming = score(part, owner) if owner < RING else None
             if weights is not None:
-                mix(weights, part, steps - 2)
+                mix(weights, part, owner - 2)
             weights = None if scores is None else weigh(scores)
             scores = upcoming
 
 
-def attention(span_map, ctx, section, queries, units, chunk):
+def attention(span_map, ctx, queries, units, chunk):
     smem = pl.BlockSpec(memory_space=pltpu.SMEM)
     vmem = pl.BlockSpec(memory_space=pltpu.VMEM)
     return pl.pallas_call(
         functools.partial(attention_kernel, chunk),
-        in_specs=[smem, smem, smem, pl.BlockSpec(memory_space=pltpu.HBM)] + [vmem] * SPANS,
-        out_specs=[vmem] * RING,
-        out_shape=[jax.ShapeDtypeStruct((TOK, PART * PAIR), jnp.bfloat16)] * RING,
+        in_specs=[smem, smem, pl.BlockSpec(memory_space=pltpu.HBM)] + [vmem] * SPANS,
+        out_specs=vmem,
+        out_shape=jax.ShapeDtypeStruct((RING, TOK, PART * PAIR), jnp.bfloat16),
         scratch_shapes=[
             pltpu.VMEM((PART, TOK, GROUP * HEAD_SIZE), jnp.bfloat16),
             pltpu.VMEM((PART, TRACE, PAIR), jnp.bfloat16),
@@ -195,33 +193,30 @@
             transcendentals=PART * GROUP * TOK * TRACE,
         ),
         name="attention",
-    )(pinned(span_map), ctx, section, pinned(queries), *units)
-
-
-def total_kernel(a, b, c, d, o_ref):
-    f32 = jnp.float32
-    o_ref[...] = (
-        a[...].astype(f32) + b[...].astype(f32) + (c[...].astype(f32) + d[...].astype(f32))
-    ).astype(jnp.bfloat16)
-
-
-def row_total(slabs):
+    )(pinned(span_map), ctx, pinned(queries), *units)
+
+
+def total_kernel(x_ref, o_ref):
+    layers = [x_ref[layer].astype(jnp.float32) for layer in range(RING)]
+    o_ref[...] = ((layers[0] + layers[1]) + (layers[2] + layers[3])).astype(jnp.bfloat16)
+
+
+def row_total(layers):
     return pl.pallas_call(
         total_kernel,
-        in_specs=[pl.BlockSpec(memory_space=pltpu.VMEM)] * RING,
+        in_specs=[pl.BlockSpec(memory_space=pltpu.VMEM)],
         out_specs=pl.BlockSpec(memory_space=pltpu.VMEM),
         out_shape=jax.ShapeDtypeStruct((TOK, PART * PAIR), jnp.bfloat16),
         compiler_params=pltpu.CompilerParams(vmem_limit_bytes=4 * 2**20),
         name="row_total",
-    )(*slabs)
-
-
-def prefix_kernel(chunk, section, residual_ref, *refs):
-    slabs, below, outs = refs[:RING], refs[RING : 2 * RING - 1], refs[2 * RING - 1 : 3 * RING - 1]
-    ordered, summed = refs[3 * RING - 1 :]
+    )(layers)
+
+
+def prefix_kernel(chunk, section, residual_ref, layers, *refs):
+    below, outs, summed = refs[: RING - 1], refs[RING - 1 : -1], refs[-1]
+    if len(outs) == 1:
+        summed = outs[0]
     place, row = section[0] % RING, section[0] // RING
-    for steps in range(RING):
-        ordered[(place + RING - steps) % RING] = slabs[steps][...]
     for part in range(PART):
         columns = slice(part * PAIR, (part + 1) * PAIR)
         first = (chunk * PART + part) * GROUP * HEAD_SIZE + place * PAIR
@@ -230,47 +225,51 @@
             earlier = rows[:, columns].astype(jnp.float32)
             state = state + jnp.where(row >= steps, earlier, 0.0)
         for layer in range(RING):
-            state = state + ordered[layer, :, columns].astype(jnp.float32)
+            state = state + layers[layer, :, columns].astype(jnp.float32)
             summed[layer, :, columns] = state.astype(jnp.bfloat16)
-    for steps in range(RING):
-        outs[steps][...] = summed[(place + steps) % RING]
-
-
-def prefix(section, residual, slabs, below, chunk):
-    slab = jax.ShapeDtypeStruct((TOK, PART * PAIR), jnp.bfloat16)
+    if len(outs) > 1:
+        for steps in range(RING):
+            outs[steps][...] = summed[(place + steps) % RING]
+
+
+def prefix(section, residual, layers, below, chunk, joint):
+    shape = (TOK, PART * PAIR)
     whole = pl.BlockSpec(memory_space=pltpu.VMEM)
+    outs = [(RING, *shape)] if joint else [shape] * RING
     return pl.pallas_call(
         functools.partial(prefix_kernel, chunk),
-        in_specs=[pl.BlockSpec(memory_space=pltpu.SMEM)] + [whole] * (2 * RING),
-        out_specs=[whole] * RING,
-        out_shape=[slab] * RING,
-        scratch_shapes=[
-            pltpu.VMEM((RING, TOK, PART * PAIR), jnp.bfloat16),
-            pltpu.VMEM((RING, TOK, PART * PAIR), jnp.bfloat16),
-        ],
+        in_specs=[pl.BlockSpec(memory_space=pltpu.SMEM)] + [whole] * (1 + RING),
+        out_specs=[whole] * len(outs),
+        out_shape=[jax.ShapeDtypeStruct(out, jnp.bfloat16) for out in outs],
+        scratch_shapes=[pltpu.VMEM((RING, *shape), jnp.bfloat16)],
         compiler_params=pltpu.CompilerParams(vmem_limit_bytes=8 * 2**20),
         name="prefix",
-    )(section, residual, *slabs, *below)
-
-
-def assemble_kernel(section, *refs):
-    slabs, o_ref = refs[:-1], refs[-1]
+    )(section, residual, layers, *below)
+
+
+def assemble_kernel(joint, section, *refs):
+    o_ref, refs = refs[-1], list(refs[:-1])
     place = section[0] % RING
     for chunk in range(CHUNKS):
         for steps in range(RING):
-            column = (place + RING - steps) % RING * PAIR
+            if joint[chunk]:
+                slab, owner = refs[0].at[steps], steps
+            else:
+                slab, owner = refs.pop(0), (place + RING - steps) % RING
             for part in range(PART):
-                first = (chunk * PART + part) * GROUP * HEAD_SIZE + column
-                o_ref[0, :, pl.ds(pl.multiple_of(first, PAIR), PAIR)] = slabs[
-                    chunk * RING + steps
-                ][:, part * PAIR : (part + 1) * PAIR]
-
-
-def assemble(section, slabs):
+                first = (chunk * PART + part) * GROUP * HEAD_SIZE + owner * PAIR
+                if not joint[chunk]:
+                    first = pl.multiple_of(first, PAIR)
+                o_ref[0, :, pl.ds(first, PAIR)] = slab[:, part * PAIR : (part + 1) * PAIR]
+        if joint[chunk]:
+            refs.pop(0)
+
+
+def assemble(section, slabs, joint):
     whole = pl.BlockSpec(memory_space=pltpu.VMEM)
     width = KEY_VALUE_HEADS * GROUP * HEAD_SIZE
     return pl.pallas_call(
-        assemble_kernel,
+        functools.partial(assemble_kernel, joint),
         in_specs=[pl.BlockSpec(memory_space=pltpu.SMEM)] + [whole] * len(slabs),
         out_specs=whole,
         out_shape=jax.ShapeDtypeStruct((1, TOK, width), jnp.bfloat16),
@@ -285,24 +284,29 @@
     ]
 
 
+def swap(slabs):
+    rows = [[y * RING + z for z in range(RING)] for y in range(RING)]
+    return lax.all_to_all(slabs, "section", 0, 0, axis_index_groups=rows, tiled=True)
+
+
+JOINT = (True, False)
+
+
 def body(queries, keys, values, residual, span_map):
     ctx = lax.axis_index("ctx")[None]
     section = lax.axis_index("section")[None]
     units = gather(keys, values)
-    slabs = [
-        turn(attention(span_map, ctx, section, queries[0], units, chunk))
-        for chunk in range(CHUNKS)
-    ]
+    layers = [swap(attention(span_map, ctx, queries[0], units, c)) for c in range(CHUNKS)]
     finished, sums = [], None
     for chunk in range(CHUNKS):
-        total = row_total(slabs[chunk])
+        total = row_total(layers[chunk])
         if sums is not None:
             total, *sums = lax.optimization_barrier((total, *sums))
-            finished += turn(sums)
+            finished += [swap(sums[0])] if JOINT[0] else turn(sums)
         below = [lax.ppermute(total, "section", climb_pairs(s)) for s in range(1, RING)]
-        sums = prefix(section, residual, slabs[chunk], below, chunk)
-    finished += turn(sums)
-    return assemble(section, finished)
+        sums = prefix(section, residual, layers[chunk], below, chunk, JOINT[chunk])
+    finished += [swap(sums[0])] if JOINT[1] else turn(sums)
+    return assemble(section, finished, JOINT)
 
 
 def solution(mesh):

time: 107 us -> 115 us (1.075)
  the two profiles are of different devices: /device:TPU:1 before, /device:TPU:64 now
where the time goes in v1:
time: 115 us
  waiting for transfers between devices  47.6 us (41%)
  starting transfers between devices  45.2 us (39%)
  Pallas kernels  20.1 us (17%)
  local copies, waits for them, and re-layouts  1.91 us (2%)
    pallas_call x2, Pallas kernels, attention(): pl.pallas_call(functools.partial(attention_kernel, chunk), in_specs=[smem...  16.7 us
    all_to_all x3, starting transfers between devices, swap(): lax.all_to_all(slabs, 'section', 0, 0, axis_index_groups=rows, tiled=True)  16.3 us
    ppermute x15, waiting for transfers between devices, ctx_move(): return lax.ppermute(unit, 'ctx', ctx_pairs(dx, dz, dc))  15.6 us
    all_to_all x3, waiting for transfers between devices, swap(): lax.all_to_all(slabs, 'section', 0, 0, axis_index_groups=rows, tiled=True)  14.6 us
    ppermute x15, starting transfers between devices, ctx_move(): return lax.ppermute(unit, 'ctx', ctx_pairs(dx, dz, dc))  13.1 us
    ppermute x3, waiting for transfers between devices, turn(): lax.ppermute(slabs[steps], 'section', turn_pairs(steps))  11.1 us
    ppermute x6, starting transfers between devices, body(): lax.ppermute(total, 'section', climb_pairs(s))  9.15 us
    ppermute x3, starting transfers between devices, turn(): lax.ppermute(slabs[steps], 'section', turn_pairs(steps))  6.58 us
  transfers between devices with their start and end apart: 27, of which 13 were waited for; matrix products, arithmetic and copies ran while one was open for 0% of the time, Pallas kernels for 8%

profile of v1, /device:TPU:64, one launch (start us, length us, event | category | flops | bytes accessed | tf_op | source)
XLA Modules:
  0.0 114.9 jit_solution(17098343746980433032)
XLA Ops:
  2.5 1.9 %collective-permute-start.3 = (bf16[128,1024]{1,0:T(8,128)(2,1)S(1)}, bf16[128,1024]{1,0:T(8,128)(2,1)S(1)}, u32[]{:S(2)}, u32[]{:S(2)}) collective-permute-start(bf16[128,1024]{1,0:T(8,128)(2,1)S(1)} %join.1.refs_0_), channel_id=1, source_target_pairs={{0,2},{1,3},{2,0},{3,1},{4,6},{5,7},{6,4},{7,5},{8,10},{9,11},{10,... | collective-permute-start | bytes 786440 | tf_op jit(solution)/shard_map/ppermute | solution.py:40
  4.5 1.7 %collective-permute-start.2 = (bf16[128,1024]{1,0:T(8,128)(2,1)S(1)}, bf16[128,1024]{1,0:T(8,128)(2,1)S(1)}, u32[]{:S(2)}, u32[]{:S(2)}) collective-permute-start(bf16[128,1024]{1,0:T(8,128)(2,1)S(1)} %join.1.refs_0_), channel_id=1, source_target_pairs={{0,12},{1,13},{2,14},{3,15},{4,0},{5,1},{6,2},{7,3},{8,4},{9,5},{1... | collective-permute-start | bytes 786440 | tf_op jit(solution)/shard_map/ppermute | solution.py:40
  6.2 4.1 %collective-permute-done.refs_1_ = bf16[128,1024]{1,0:T(8,128)(2,1)S(1)} collective-permute-done((bf16[128,1024]{1,0:T(8,128)(2,1)S(1)}, bf16[128,1024]{1,0:T(8,128)(2,1)S(1)}, u32[]{:S(2)}, u32[]{:S(2)}) %collective-permute-start) | collective-permute-done | bytes 262176 | tf_op jit(solution)/shard_map/ppermute | solution.py:40
  10.6 3.0 %collective-permute-start.6 = (bf16[128,1024]{1,0:T(8,128)(2,1)S(1)}, bf16[128,1024]{1,0:T(8,128)(2,1)S(1)}, u32[]{:S(2)}, u32[]{:S(2)}) collective-permute-start(bf16[128,1024]{1,0:T(8,128)(2,1)S(1)} %collective-permute-done.3.refs_4_), channel_id=1, source_target_pairs={{0,12},{1,13},{2,14},{3,15},{4,0},{5,1},{6,2},{7,3},{8,4},{9,5},{1... | collective-permute-start | bytes 786440 | tf_op jit(solution)/shard_map/ppermute | solution.py:40
  13.8 1.9 %collective-permute-start.4 = (bf16[128,1024]{1,0:T(8,128)(2,1)S(1)}, bf16[128,1024]{1,0:T(8,128)(2,1)S(1)}, u32[]{:S(2)}, u32[]{:S(2)}) collective-permute-start(bf16[128,1024]{1,0:T(8,128)(2,1)S(1)} %collective-permute-done.refs_1_), channel_id=1, source_target_pairs={{0,2},{1,3},{2,0},{3,1},{4,6},{5,7},{6,4},{7,5},{8,10},{9,11},{10,... | collective-permute-start | bytes 786440 | tf_op jit(solution)/shard_map/ppermute | solution.py:40
  15.7 3.0 %collective-permute-done.1.refs_2_ = bf16[128,1024]{1,0:T(8,128)(2,1)S(1)} collective-permute-done((bf16[128,1024]{1,0:T(8,128)(2,1)S(1)}, bf16[128,1024]{1,0:T(8,128)(2,1)S(1)}, u32[]{:S(2)}, u32[]{:S(2)}) %collective-permute-start.1) | collective-permute-done | bytes 262176 | tf_op jit(solution)/shard_map/ppermute | solution.py:40
  18.7 1.9 %collective-permute-start.5 = (bf16[128,1024]{1,0:T(8,128)(2,1)S(1)}, bf16[128,1024]{1,0:T(8,128)(2,1)S(1)}, u32[]{:S(2)}, u32[]{:S(2)}) collective-permute-start(bf16[128,1024]{1,0:T(8,128)(2,1)S(1)} %collective-permute-done.1.refs_2_), channel_id=1, source_target_pairs={{0,2},{1,3},{2,0},{3,1},{4,6},{5,7},{6,4},{7,5},{8,10},{9,11},{10,... | collective-permute-start | bytes 786440 | tf_op jit(solution)/shard_map/ppermute | solution.py:40
  21.2 1.7 %collective-permute-done.4.refs_5_ = bf16[128,1024]{1,0:T(8,128)(2,1)S(1)} collective-permute-done((bf16[128,1024]{1,0:T(8,128)(2,1)S(1)}, bf16[128,1024]{1,0:T(8,128)(2,1)S(1)}, u32[]{:S(2)}, u32[]{:S(2)}) %collective-permute-start.4) | collective-permute-done | bytes 262176 | tf_op jit(solution)/shard_map/ppermute | solution.py:40
  22.9 5.2 %collective-permute-done.5.refs_6_ = bf16[128,1024]{1,0:T(8,128)(2,1)S(1)} collective-permute-done((bf16[128,1024]{1,0:T(8,128)(2,1)S(1)}, bf16[128,1024]{1,0:T(8,128)(2,1)S(1)}, u32[]{:S(2)}, u32[]{:S(2)}) %collective-permute-start.5) | collective-permute-done | bytes 262176 | tf_op jit(solution)/shard_map/ppermute | solution.py:40
  29.7 8.3 %attention.3 = bf16[4,128,512]{2,1,0:T(8,128)(2,1)} custom-call(s32[16]{0:T(128)} %span_map.3, s32[1]{0:T(128)} %bitcast.1.ctx, bf16[128,4096]{1,0:T(8,128)(2,1)} %bitcast.3, bf16[128,1024]{1,0:T(8,128)(2,1)S(1)} %join.1.refs_0_, bf16[128,1024]{1,0:T(8,128)(2,1)S(1)} %collective-permute-done.refs_1_, bf16[128,1024]{1,0:T(8,128)(2,1)S(1)} %collective-permute-done.1.refs_2_, ...), custom_call_target="tpu_custom_call" | custom-call | flops 4294967296 | bytes 3145728 | tf_op jit(solution)/shard_map/attention/pallas_call | solution.py:178
  38.1 7.9 %all-to-all-start.1 = ((bf16[4,128,512]{2,1,0:T(8,128)(2,1)}), bf16[4,128,512]{2,1,0:T(8,128)(2,1)S(1)}, u32[]{:S(2)}, u32[]{:S(2)}) async-start(bf16[4,128,512]{2,1,0:T(8,128)(2,1)} %attention.3), calls=%async_computation.1 | async-start | bytes 1048576 | tf_op jit(solution)/shard_map/all_to_all | solution.py:289
  48.0 8.3 %attention.2 = bf16[4,128,512]{2,1,0:T(8,128)(2,1)} custom-call(s32[16]{0:T(128)} %span_map.3, s32[1]{0:T(128)} %bitcast.1.ctx, bf16[128,4096]{1,0:T(8,128)(2,1)} %bitcast.4, bf16[128,1024]{1,0:T(8,128)(2,1)S(1)} %join.1.refs_0_, bf16[128,1024]{1,0:T(8,128)(2,1)S(1)} %collective-permute-done.refs_1_, bf16[128,1024]{1,0:T(8,128)(2,1)S(1)} %collective-permute-done.1.refs_2_, ...), custom_call_target="tpu_custom_call" | custom-call | flops 4294967296 | bytes 3145728 | tf_op jit(solution)/shard_map/attention/pallas_call | solution.py:178
  56.3 5.2 %all-to-all-done.1.x_ref.layers = bf16[4,128,512]{2,1,0:T(8,128)(2,1)S(1)} async-done(((bf16[4,128,512]{2,1,0:T(8,128)(2,1)}), bf16[4,128,512]{2,1,0:T(8,128)(2,1)S(1)}, u32[]{:S(2)}, u32[]{:S(2)}) %all-to-all-start.1) | async-done | bytes 524320 | tf_op jit(solution)/shard_map/all_to_all | solution.py:289
  61.5 4.2 %all-to-all-start = ((bf16[4,128,512]{2,1,0:T(8,128)(2,1)}), bf16[4,128,512]{2,1,0:T(8,128)(2,1)S(1)}, u32[]{:S(2)}, u32[]{:S(2)}) async-start(bf16[4,128,512]{2,1,0:T(8,128)(2,1)} %attention.2), calls=%async_computation | async-start | bytes 1048576 | tf_op jit(solution)/shard_map/all_to_all | solution.py:289
  65.8 3.1 %collective-permute-start.17 = (bf16[128,512]{1,0:T(8,128)(2,1)S(1)}, bf16[128,512]{1,0:T(8,128)(2,1)S(1)}, u32[]{:S(2)}, u32[]{:S(2)}) collective-permute-start(bf16[128,512]{1,0:T(8,128)(2,1)S(1)} %row_total.3), channel_id=1, source_target_pairs={{0,192},{16,208},{32,224},{48,240},{64,0},{80,16},{96,32},{112,48}... | collective-permute-start | bytes 393224 | tf_op jit(solution)/shard_map/ppermute | solution.py:306
  70.5 9.4 %all-to-all-done.x_ref.layers = bf16[4,128,512]{2,1,0:T(8,128)(2,1)S(1)} async-done(((bf16[4,128,512]{2,1,0:T(8,128)(2,1)}), bf16[4,128,512]{2,1,0:T(8,128)(2,1)S(1)}, u32[]{:S(2)}, u32[]{:S(2)}) %all-to-all-start) | async-done | bytes 524320 | tf_op jit(solution)/shard_map/all_to_all | solution.py:289
  81.0 4.2 %all-to-all-start.2 = ((bf16[4,128,512]{2,1,0:T(8,128)(2,1)}), bf16[4,128,512]{2,1,0:T(8,128)(2,1)S(1)}, u32[]{:S(2)}, u32[]{:S(2)}) async-start(bf16[4,128,512]{2,1,0:T(8,128)(2,1)} %prefix.2), calls=%async_computation.2 | async-start | bytes 1048576 | tf_op jit(solution)/shard_map/all_to_all | solution.py:289
  85.2 2.9 %collective-permute-start.20 = (bf16[128,512]{1,0:T(8,128)(2,1)S(1)}, bf16[128,512]{1,0:T(8,128)(2,1)S(1)}, u32[]{:S(2)}, u32[]{:S(2)}) collective-permute-start(bf16[128,512]{1,0:T(8,128)(2,1)S(1)} %row_total.2), channel_id=1, source_target_pairs={{0,192},{16,208},{32,224},{48,240},{64,0},{80,16},{96,32},{112,48}... | collective-permute-start | bytes 393224 | tf_op jit(solution)/shard_map/ppermute | solution.py:306
  89.6 2.3 %collective-permute-done.20.refs_2_ = bf16[128,512]{1,0:T(8,128)(2,1)S(1)} collective-permute-done((bf16[128,512]{1,0:T(8,128)(2,1)S(1)}, bf16[128,512]{1,0:T(8,128)(2,1)S(1)}, u32[]{:S(2)}, u32[]{:S(2)}) %collective-permute-start.20) | collective-permute-done | bytes 131104 | tf_op jit(solution)/shard_map/ppermute | solution.py:306
  92.0 2.7 %collective-permute-done.19.refs_1_ = bf16[128,512]{1,0:T(8,128)(2,1)S(1)} collective-permute-done((bf16[128,512]{1,0:T(8,128)(2,1)S(1)}, bf16[128,512]{1,0:T(8,128)(2,1)S(1)}, u32[]{:S(2)}, u32[]{:S(2)}) %collective-permute-start.19) | collective-permute-done | bytes 131104 | tf_op jit(solution)/shard_map/ppermute | solution.py:306
  96.1 3.7 %collective-permute-start.21 = (bf16[128,512]{1,0:T(8,128)(2,1)S(1)}, bf16[128,512]{1,0:T(8,128)(2,1)S(1)}, u32[]{:S(2)}, u32[]{:S(2)}) collective-permute-start(bf16[128,512]{1,0:T(8,128)(2,1)S(1)} %get-tuple-element.14), channel_id=1, source_target_pairs={{0,16},{16,32},{32,48},{48,0},{64,80},{80,96},{96,112},{112,64},{1... | collective-permute-start | bytes 393224 | tf_op jit(solution)/shard_map/ppermute | solution.py:283
  99.9 2.8 %collective-permute-start.23 = (bf16[128,512]{1,0:T(8,128)(2,1)S(1)}, bf16[128,512]{1,0:T(8,128)(2,1)S(1)}, u32[]{:S(2)}, u32[]{:S(2)}) collective-permute-start(bf16[128,512]{1,0:T(8,128)(2,1)S(1)} %get-tuple-element.16), channel_id=1, source_target_pairs={{0,48},{16,0},{32,16},{48,32},{64,112},{80,64},{96,80},{112,96},{1... | collective-permute-start | bytes 393224 | tf_op jit(solution)/shard_map/ppermute | solution.py:283
  104.1 7.4 %collective-permute-done.22.refs_3_ = bf16[128,512]{1,0:T(8,128)(2,1)S(1)} collective-permute-done((bf16[128,512]{1,0:T(8,128)(2,1)S(1)}, bf16[128,512]{1,0:T(8,128)(2,1)S(1)}, u32[]{:S(2)}, u32[]{:S(2)}) %collective-permute-start.22) | collective-permute-done | bytes 131104 | tf_op jit(solution)/shard_map/ppermute | solution.py:283
  111.5 2.3 %collective-permute-done.23.refs_4_ = bf16[128,512]{1,0:T(8,128)(2,1)S(1)} collective-permute-done((bf16[128,512]{1,0:T(8,128)(2,1)S(1)}, bf16[128,512]{1,0:T(8,128)(2,1)S(1)}, u32[]{:S(2)}, u32[]{:S(2)}) %collective-permute-start.23) | collective-permute-done | bytes 131104 | tf_op jit(solution)/shard_map/ppermute | solution.py:283
  (48 shorter events, 15.7 us)
Async XLA Ops:
  1.0 9.3 %collective-permute-start = (bf16[128,1024]{1,0:T(8,128)(2,1)S(1)}, bf16[128,1024]{1,0:T(8,128)(2,1)S(1)}, u32[]{:S(2)}, u32[]{:S(2)}) collective-permute-start(bf16[128,1024]{1,0:T(8,128)(2,1)S(1)} %join.1.refs_0_), channel_id=1, source_target_pairs={{0,4},{1,5},{2,6},{3,7},{4,8},{5,9},{6,10},{7,11},{8,12},{9,13},{1... | collective-permute-start | bytes 786440 | tf_op jit(solution)/shard_map/ppermute | solution.py:40
  2.5 8.0 %collective-permute-start.3 = (bf16[128,1024]{1,0:T(8,128)(2,1)S(1)}, bf16[128,1024]{1,0:T(8,128)(2,1)S(1)}, u32[]{:S(2)}, u32[]{:S(2)}) collective-permute-start(bf16[128,1024]{1,0:T(8,128)(2,1)S(1)} %join.1.refs_0_), channel_id=1, source_target_pairs={{0,2},{1,3},{2,0},{3,1},{4,6},{5,7},{6,4},{7,5},{8,10},{9,11},{10,... | collective-permute-start | bytes 786440 | tf_op jit(solution)/shard_map/ppermute | solution.py:40
  4.5 9.1 %collective-permute-start.2 = (bf16[128,1024]{1,0:T(8,128)(2,1)S(1)}, bf16[128,1024]{1,0:T(8,128)(2,1)S(1)}, u32[]{:S(2)}, u32[]{:S(2)}) collective-permute-start(bf16[128,1024]{1,0:T(8,128)(2,1)S(1)} %join.1.refs_0_), channel_id=1, source_target_pairs={{0,12},{1,13},{2,14},{3,15},{4,0},{5,1},{6,2},{7,3},{8,4},{9,5},{1... | collective-permute-start | bytes 786440 | tf_op jit(solution)/shard_map/ppermute | solution.py:40
  6.2 7.6 %collective-permute-start.7 = (bf16[128,1024]{1,0:T(8,128)(2,1)S(1)}, bf16[128,1024]{1,0:T(8,128)(2,1)S(1)}, u32[]{:S(2)}, u32[]{:S(2)}) collective-permute-start(bf16[128,1024]{1,0:T(8,128)(2,1)S(1)} %join.1.refs_0_), channel_id=1, source_target_pairs={{0,1},{1,0},{2,3},{3,2},{4,5},{5,4},{6,7},{7,6},{8,9},{9,8},{10,11... | collective-permute-start | bytes 786440 | tf_op jit(solution)/shard_map/ppermute | solution.py:40
  10.3 8.4 %collective-permute-start.1 = (bf16[128,1024]{1,0:T(8,128)(2,1)S(1)}, bf16[128,1024]{1,0:T(8,128)(2,1)S(1)}, u32[]{:S(2)}, u32[]{:S(2)}) collective-permute-start(bf16[128,1024]{1,0:T(8,128)(2,1)S(1)} %collective-permute-done.refs_1_), channel_id=1, source_target_pairs={{0,4},{1,5},{2,6},{3,7},{4,8},{5,9},{6,10},{7,11},{8,12},{9,13},{1... | collective-permute-start | bytes 786440 | tf_op jit(solution)/shard_map/ppermute | solution.py:40
  10.6 10.0 %collective-permute-start.11 = (bf16[128,1024]{1,0:T(8,128)(2,1)S(1)}, bf16[128,1024]{1,0:T(8,128)(2,1)S(1)}, u32[]{:S(2)}, u32[]{:S(2)}) collective-permute-start(bf16[128,1024]{1,0:T(8,128)(2,1)S(1)} %collective-permute-done.3.refs_4_), channel_id=1, source_target_pairs={{0,1},{1,0},{2,3},{3,2},{4,5},{5,4},{6,7},{7,6},{8,9},{9,8},{10,11... | collective-permute-start | bytes 786440 | tf_op jit(solution)/shard_map/ppermute | solution.py:40
  10.6 10.0 %collective-permute-start.6 = (bf16[128,1024]{1,0:T(8,128)(2,1)S(1)}, bf16[128,1024]{1,0:T(8,128)(2,1)S(1)}, u32[]{:S(2)}, u32[]{:S(2)}) collective-permute-start(bf16[128,1024]{1,0:T(8,128)(2,1)S(1)} %collective-permute-done.3.refs_4_), channel_id=1, source_target_pairs={{0,12},{1,13},{2,14},{3,15},{4,0},{5,1},{6,2},{7,3},{8,4},{9,5},{1... | collective-permute-start | bytes 786440 | tf_op jit(solution)/shard_map/ppermute | solution.py:40
  13.6 7.6 %collective-permute-start.10 = (bf16[128,1024]{1,0:T(8,128)(2,1)S(1)}, bf16[128,1024]{1,0:T(8,128)(2,1)S(1)}, u32[]{:S(2)}, u32[]{:S(2)}) collective-permute-start(bf16[128,1024]{1,0:T(8,128)(2,1)S(1)} %collective-permute-done.2.refs_3_), channel_id=1, source_target_pairs={{0,1},{1,0},{2,3},{3,2},{4,5},{5,4},{6,7},{7,6},{8,9},{9,8},{10,11... | collective-permute-start | bytes 786440 | tf_op jit(solution)/shard_map/ppermute | solution.py:40
  13.8 9.1 %collective-permute-start.4 = (bf16[128,1024]{1,0:T(8,128)(2,1)S(1)}, bf16[128,1024]{1,0:T(8,128)(2,1)S(1)}, u32[]{:S(2)}, u32[]{:S(2)}) collective-permute-start(bf16[128,1024]{1,0:T(8,128)(2,1)S(1)} %collective-permute-done.refs_1_), channel_id=1, source_target_pairs={{0,2},{1,3},{2,0},{3,1},{4,6},{5,7},{6,4},{7,5},{8,10},{9,11},{10,... | collective-permute-start | bytes 786440 | tf_op jit(solution)/shard_map/ppermute | solution.py:40
  18.7 9.4 %collective-permute-start.5 = (bf16[128,1024]{1,0:T(8,128)(2,1)S(1)}, bf16[128,1024]{1,0:T(8,128)(2,1)S(1)}, u32[]{:S(2)}, u32[]{:S(2)}) collective-permute-start(bf16[128,1024]{1,0:T(8,128)(2,1)S(1)} %collective-permute-done.1.refs_2_), channel_id=1, source_target_pairs={{0,2},{1,3},{2,0},{3,1},{4,6},{5,7},{6,4},{7,5},{8,10},{9,11},{10,... | collective-permute-start | bytes 786440 | tf_op jit(solution)/shard_map/ppermute | solution.py:40
  20.6 7.5 %collective-permute-start.8 = (bf16[128,1024]{1,0:T(8,128)(2,1)S(1)}, bf16[128,1024]{1,0:T(8,128)(2,1)S(1)}, u32[]{:S(2)}, u32[]{:S(2)}) collective-permute-start(bf16[128,1024]{1,0:T(8,128)(2,1)S(1)} %collective-permute-done.refs_1_), channel_id=1, source_target_pairs={{0,1},{1,0},{2,3},{3,2},{4,5},{5,4},{6,7},{7,6},{8,9},{9,8},{10,11... | collective-permute-start | bytes 786440 | tf_op jit(solution)/shard_map/ppermute | solution.py:40
  20.6 7.5 %collective-permute-start.9 = (bf16[128,1024]{1,0:T(8,128)(2,1)S(1)}, bf16[128,1024]{1,0:T(8,128)(2,1)S(1)}, u32[]{:S(2)}, u32[]{:S(2)}) collective-permute-start(bf16[128,1024]{1,0:T(8,128)(2,1)S(1)} %collective-permute-done.1.refs_2_), channel_id=1, source_target_pairs={{0,1},{1,0},{2,3},{3,2},{4,5},{5,4},{6,7},{7,6},{8,9},{9,8},{10,11... | collective-permute-start | bytes 786440 | tf_op jit(solution)/shard_map/ppermute | solution.py:40
  21.1 7.0 %collective-permute-start.14 = (bf16[128,1024]{1,0:T(8,128)(2,1)S(1)}, bf16[128,1024]{1,0:T(8,128)(2,1)}, u32[]{:S(2)}, u32[]{:S(2)}) collective-permute-start(bf16[128,1024]{1,0:T(8,128)(2,1)S(1)} %collective-permute-done.6.refs_7_), channel_id=1, source_target_pairs={{0,1},{1,0},{2,3},{3,2},{4,5},{5,4},{6,7},{7,6},{8,9},{9,8},{10,11... | collective-permute-start | bytes 786440 | tf_op jit(solution)/shard_map/ppermute | solution.py:40
  38.1 23.4 %all-to-all-start.1 = ((bf16[4,128,512]{2,1,0:T(8,128)(2,1)}), bf16[4,128,512]{2,1,0:T(8,128)(2,1)S(1)}, u32[]{:S(2)}, u32[]{:S(2)}) async-start(bf16[4,128,512]{2,1,0:T(8,128)(2,1)} %attention.3), calls=%async_computation.1 | async-start | bytes 1048576 | tf_op jit(solution)/shard_map/all_to_all | solution.py:289
  61.5 18.4 %all-to-all-start = ((bf16[4,128,512]{2,1,0:T(8,128)(2,1)}), bf16[4,128,512]{2,1,0:T(8,128)(2,1)S(1)}, u32[]{:S(2)}, u32[]{:S(2)}) async-start(bf16[4,128,512]{2,1,0:T(8,128)(2,1)} %attention.2), calls=%async_computation | async-start | bytes 1048576 | tf_op jit(solution)/shard_map/all_to_all | solution.py:289
  65.8 14.2 %collective-permute-start.17 = (bf16[128,512]{1,0:T(8,128)(2,1)S(1)}, bf16[128,512]{1,0:T(8,128)(2,1)S(1)}, u32[]{:S(2)}, u32[]{:S(2)}) collective-permute-start(bf16[128,512]{1,0:T(8,128)(2,1)S(1)} %row_total.3), channel_id=1, source_target_pairs={{0,192},{16,208},{32,224},{48,240},{64,0},{80,16},{96,32},{112,48}... | collective-permute-start | bytes 393224 | tf_op jit(solution)/shard_map/ppermute | solution.py:306
  68.9 11.1 %collective-permute-start.16 = (bf16[128,512]{1,0:T(8,128)(2,1)S(1)}, bf16[128,512]{1,0:T(8,128)(2,1)S(1)}, u32[]{:S(2)}, u32[]{:S(2)}) collective-permute-start(bf16[128,512]{1,0:T(8,128)(2,1)S(1)} %row_total.3), channel_id=1, source_target_pairs={{0,128},{16,144},{32,160},{48,176},{64,192},{80,208},{96,224},{112... | collective-permute-start | bytes 393224 | tf_op jit(solution)/shard_map/ppermute | solution.py:306
  69.5 10.5 %collective-permute-start.15 = (bf16[128,512]{1,0:T(8,128)(2,1)S(1)}, bf16[128,512]{1,0:T(8,128)(2,1)S(1)}, u32[]{:S(2)}, u32[]{:S(2)}) collective-permute-start(bf16[128,512]{1,0:T(8,128)(2,1)S(1)} %row_total.3), channel_id=1, source_target_pairs={{0,64},{16,80},{32,96},{48,112},{64,128},{80,144},{96,160},{112,17... | collective-permute-start | bytes 393224 | tf_op jit(solution)/shard_map/ppermute | solution.py:306
  81.0 32.8 %all-to-all-start.2 = ((bf16[4,128,512]{2,1,0:T(8,128)(2,1)}), bf16[4,128,512]{2,1,0:T(8,128)(2,1)S(1)}, u32[]{:S(2)}, u32[]{:S(2)}) async-start(bf16[4,128,512]{2,1,0:T(8,128)(2,1)} %prefix.2), calls=%async_computation.2 | async-start | bytes 1048576 | tf_op jit(solution)/shard_map/all_to_all | solution.py:289
  85.2 6.8 %collective-permute-start.20 = (bf16[128,512]{1,0:T(8,128)(2,1)S(1)}, bf16[128,512]{1,0:T(8,128)(2,1)S(1)}, u32[]{:S(2)}, u32[]{:S(2)}) collective-permute-start(bf16[128,512]{1,0:T(8,128)(2,1)S(1)} %row_total.2), channel_id=1, source_target_pairs={{0,192},{16,208},{32,224},{48,240},{64,0},{80,16},{96,32},{112,48}... | collective-permute-start | bytes 393224 | tf_op jit(solution)/shard_map/ppermute | solution.py:306
  88.7 7.2 %collective-permute-start.18 = (bf16[128,512]{1,0:T(8,128)(2,1)S(1)}, bf16[128,512]{1,0:T(8,128)(2,1)S(1)}, u32[]{:S(2)}, u32[]{:S(2)}) collective-permute-start(bf16[128,512]{1,0:T(8,128)(2,1)S(1)} %row_total.2), channel_id=1, source_target_pairs={{0,64},{16,80},{32,96},{48,112},{64,128},{80,144},{96,160},{112,17... | collective-permute-start | bytes 393224 | tf_op jit(solution)/shard_map/ppermute | solution.py:306
  96.1 8.0 %collective-permute-start.21 = (bf16[128,512]{1,0:T(8,128)(2,1)S(1)}, bf16[128,512]{1,0:T(8,128)(2,1)S(1)}, u32[]{:S(2)}, u32[]{:S(2)}) collective-permute-start(bf16[128,512]{1,0:T(8,128)(2,1)S(1)} %get-tuple-element.14), channel_id=1, source_target_pairs={{0,16},{16,32},{32,48},{48,0},{64,80},{80,96},{96,112},{112,64},{1... | collective-permute-start | bytes 393224 | tf_op jit(solution)/shard_map/ppermute | solution.py:283
  99.8 11.7 %collective-permute-start.22 = (bf16[128,512]{1,0:T(8,128)(2,1)S(1)}, bf16[128,512]{1,0:T(8,128)(2,1)S(1)}, u32[]{:S(2)}, u32[]{:S(2)}) collective-permute-start(bf16[128,512]{1,0:T(8,128)(2,1)S(1)} %get-tuple-element.15), channel_id=1, source_target_pairs={{0,32},{16,48},{32,0},{48,16},{64,96},{80,112},{96,64},{112,80},{1... | collective-permute-start | bytes 393224 | tf_op jit(solution)/shard_map/ppermute | solution.py:283
  99.9 13.9 %collective-permute-start.23 = (bf16[128,512]{1,0:T(8,128)(2,1)S(1)}, bf16[128,512]{1,0:T(8,128)(2,1)S(1)}, u32[]{:S(2)}, u32[]{:S(2)}) collective-permute-start(bf16[128,512]{1,0:T(8,128)(2,1)S(1)} %get-tuple-element.16), channel_id=1, source_target_pairs={{0,48},{16,0},{32,16},{48,32},{64,112},{80,64},{96,80},{112,96},{1... | collective-permute-start | bytes 393224 | tf_op jit(solution)/shard_map/ppermute | solution.py:283
  (8 other events, 59.0 us)

commit v2 on v0

--- a/solution.py
+++ b/solution.py
@@ -25,7 +25,9 @@
 
 SIDE = PART * HEAD_SIZE
 
-UNITS = [(dx, dz, dc) for dc in range(2) for dz in range(2) for dx in range(4)]
+NEAR = [(0, 0), (0, 1), (1, 0), (3, 0), (2, 0), (3, 1), (1, 1)]
+WHOLE = 2 * len(NEAR)
+UNITS = [(dx, dz, dc) for dc in range(2) for dx, dz in NEAR] + [(2, 1, 0), (2, 1, 1)]
 
 
 def ctx_pairs(dx, dz, dc):
@@ -81,28 +83,49 @@
     )(pinned(keys), pinned(values))
 
 
+def pack_kernel(*refs):
+    for place, ref in enumerate(refs[:-1]):
+        refs[-1][place] = ref[...]
+
+
+def pack(units):
+    vmem = pl.BlockSpec(memory_space=pltpu.VMEM)
+    return pl.pallas_call(
+        pack_kernel,
+        in_specs=[vmem] * len(units),
+        out_specs=vmem,
+        out_shape=jax.ShapeDtypeStruct((len(units), *units[0].shape), jnp.bfloat16),
+        compiler_params=pltpu.CompilerParams(vmem_limit_bytes=4 * 2**20),
+        name="pack",
+    )(*units)
+
+
 def gather(keys, values):
-    held = {(0, 0, 0): join(keys, values)}
-    for dx, dz, source in (
-        (0, 1, (0, 0, 0)),
-        (1, 0, (0, 0, 0)),
-        (3, 0, (0, 0, 0)),
-        (0, 1, (1, 0, 0)),
-        (1, 0, (1, 0, 0)),
-        (3, 0, (0, 1, 0)),
-        (0, 1, (2, 0, 0)),
-    ):
-        target = ((source[0] + dx) % 4, source[1] ^ dz, 0)
-        held[target] = ctx_move(held[source], dx, dz, 0)
-    for dz in range(2):
-        for dx in range(4):
-            held[dx, dz, 1] = ctx_move(held[dx, dz, 0], 0, 0, 1)
-    return [held[unit] for unit in UNITS]
+    own = join(keys, values)
+    back1 = ctx_move(own, 1, 0, 0)
+    other = ctx_move(own, 0, 1, 0)
+    back3 = ctx_move(own, 3, 0, 0)
+    back2 = ctx_move(back1, 1, 0, 0)
+    other1 = ctx_move(back1, 0, 1, 0)
+    other3 = ctx_move(other, 3, 0, 0)
+    farthest = [
+        ctx_move(back2[:, :WIDTH], 0, 1, 0),
+        ctx_move(other1[:, WIDTH:], 1, 0, 0),
+    ]
+    shared = [own, pack([other, back1, back3]), pack([back2, other3, other1])]
+    shared += [ctx_move(x, 0, 0, 1) for x in shared]
+    halves = [[part, ctx_move(part, 0, 0, 1)] for part in farthest]
+    return shared, halves
 
 
 def attention_kernel(chunk, span_map, ctx, section, q_hbm, *refs):
-    units, o_refs = refs[:SPANS], refs[SPANS : SPANS + RING]
-    q_ref, keys, vals, sems = refs[SPANS + RING :]
+    held, o_refs = refs[:8], refs[8 : 8 + RING]
+    q_ref, keys, vals, sems = refs[8 + RING :]
+    units = []
+    for side in range(2):
+        own, near, later = held[3 * side : 3 * side + 3]
+        units += [own] + [x.at[i] for x in (near, later) for i in range(3)]
+    units += held[6:]
     copies = []
     for part in range(PART):
         width = GROUP * HEAD_SIZE
@@ -127,7 +150,7 @@
         mask = jnp.where(ahead > 0, HIDDEN, 0.0).astype(jnp.bfloat16)
         rows = slice(block * TOK, (block + 1) * TOK)
         for part in range(PART):
-            first = chunk * 2 * SIDE + part * HEAD_SIZE
+            first = part * HEAD_SIZE + (chunk * 2 * SIDE if block < WHOLE else 0)
             keys[part, rows, :HEAD_SIZE] = units[block][:, first : first + HEAD_SIZE]
             keys[part, rows, HEAD_SIZE:] = mask
             first += SIDE
@@ -175,11 +198,13 @@
 
 
 def attention(span_map, ctx, section, queries, units, chunk):
+    shared, halves = units
+    units = [*shared, *halves[chunk]]
     smem = pl.BlockSpec(memory_space=pltpu.SMEM)
     vmem = pl.BlockSpec(memory_space=pltpu.VMEM)
     return pl.pallas_call(
         functools.partial(attention_kernel, chunk),
-        in_specs=[smem, smem, smem, pl.BlockSpec(memory_space=pltpu.HBM)] + [vmem] * SPANS,
+        in_specs=[smem, smem, smem, pl.BlockSpec(memory_space=pltpu.HBM)] + [vmem] * 8,
         out_specs=[vmem] * RING,
         out_shape=[jax.ShapeDtypeStruct((TOK, PART * PAIR), jnp.bfloat16)] * RING,
         scratch_shapes=[
@@ -288,7 +313,7 @@
 def body(queries, keys, values, residual, span_map):
     ctx = lax.axis_index("ctx")[None]
     section = lax.axis_index("section")[None]
-    units = gather(keys, values)
+    units = lax.optimization_barrier(gather(keys, values))
     slabs = [
         turn(attention(span_map, ctx, section, queries[0], units, chunk))
         for chunk in range(CHUNKS)

time: 107 us -> 107 us (level)
  waiting for transfers between devices: 30 us -> 36.3 us
  starting transfers between devices: 58.6 us -> 52.4 us
    ppermute x15 -> x13, starting transfers between devices: 23.6 us -> 18.5 us  [ctx_move(): return lax.ppermute(unit, 'ctx', ctx_pairs(dx, dz, dc))]
    ppermute x15 -> x13, waiting for transfers between devices: 6.32 us -> 11.3 us  [ctx_move(): return lax.ppermute(unit, 'ctx', ctx_pairs(dx, dz, dc))]
    ppermute x12, starting transfers between devices: 26.9 us -> 25.5 us  [turn(): lax.ppermute(slabs[steps], 'section', turn_pairs(steps))]
  transfers between devices with their start and end apart: 33 -> 31, of which waited for: 9 -> 12; matrix products, arithmetic and copies ran while one was open for 0% -> 0% of each run, Pallas kernels for 7% -> 7%
where the time goes in v2:
time: 107 us
  starting transfers between devices  52.4 us (49%)
  waiting for transfers between devices  36.3 us (34%)
  Pallas kernels  17.8 us (17%)
    ppermute x12, starting transfers between devices, turn(): lax.ppermute(slabs[steps], 'section', turn_pairs(steps))  25.5 us
    ppermute x12, waiting for transfers between devices, turn(): lax.ppermute(slabs[steps], 'section', turn_pairs(steps))  21.8 us
    ppermute x13, starting transfers between devices, ctx_move(): return lax.ppermute(unit, 'ctx', ctx_pairs(dx, dz, dc))  18.5 us
    pallas_call x2, Pallas kernels, attention(): pl.pallas_call(functools.partial(attention_kernel, chunk), in_specs=[smem...  14.9 us
    ppermute x13, waiting for transfers between devices, ctx_move(): return lax.ppermute(unit, 'ctx', ctx_pairs(dx, dz, dc))  11.3 us
    ppermute x6, starting transfers between devices, body(): lax.ppermute(total, 'section', climb_pairs(s))  8.43 us
    ppermute x6, waiting for transfers between devices, body(): lax.ppermute(total, 'section', climb_pairs(s))  3.12 us
  transfers between devices with their start and end apart: 31, of which 12 were waited for; matrix products, arithmetic and copies ran while one was open for 0% of the time, Pallas kernels for 7%

profile of v2, /device:TPU:1, one launch (start us, length us, event | category | flops | bytes accessed | tf_op | source)
XLA Modules:
  0.0 106.7 jit_solution(2903060005411291402)
XLA Ops:
  1.0 2.1 %collective-permute-start.1 = (bf16[128,1024]{1,0:T(8,128)(2,1)S(1)}, bf16[128,1024]{1,0:T(8,128)(2,1)S(1)}, u32[]{:S(2)}, u32[]{:S(2)}) collective-permute-start(bf16[128,1024]{1,0:T(8,128)(2,1)S(1)} %join.1.refs_0_), channel_id=1, source_target_pairs={{0,4},{1,5},{2,6},{3,7},{4,8},{5,9},{6,10},{7,11},{8,12},{9,13},{1... | collective-permute-start | bytes 786440 | tf_op jit(solution)/shard_map/ppermute | solution.py:42
  8.1 3.8 %collective-permute-start.5 = (bf16[128,1024]{1,0:T(8,128)(2,1)S(1)}, bf16[128,1024]{1,0:T(8,128)(2,1)S(1)}, u32[]{:S(2)}, u32[]{:S(2)}) collective-permute-start(bf16[128,1024]{1,0:T(8,128)(2,1)S(1)} %collective-permute-done.1.refs_1_), channel_id=1, source_target_pairs={{0,2},{1,3},{2,0},{3,1},{4,6},{5,7},{6,4},{7,5},{8,10},{9,11},{10,... | collective-permute-start | bytes 786440 | tf_op jit(solution)/shard_map/ppermute | solution.py:42
  11.9 2.7 %collective-permute-start.4 = (bf16[128,1024]{1,0:T(8,128)(2,1)S(1)}, bf16[128,1024]{1,0:T(8,128)(2,1)S(1)}, u32[]{:S(2)}, u32[]{:S(2)}) collective-permute-start(bf16[128,1024]{1,0:T(8,128)(2,1)S(1)} %collective-permute-done.refs_0_), channel_id=1, source_target_pairs={{0,12},{1,13},{2,14},{3,15},{4,0},{5,1},{6,2},{7,3},{8,4},{9,5},{1... | collective-permute-start | bytes 786440 | tf_op jit(solution)/shard_map/ppermute | solution.py:42
  14.6 2.5 %collective-permute-start.7 = (bf16[3,128,1024]{2,1,0:T(8,128)(2,1)S(1)}, bf16[3,128,1024]{2,1,0:T(8,128)(2,1)S(1)}, u32[]{:S(2)}, u32[]{:S(2)}) collective-permute-start(bf16[3,128,1024]{2,1,0:T(8,128)(2,1)S(1)} %pack.2.refs_1_), channel_id=1, source_target_pairs={{0,1},{1,0},{2,3},{3,2},{4,5},{5,4},{6,7},{7,6},{8,9},{9,8},{10,11... | collective-permute-start | bytes 2359304 | tf_op jit(solution)/shard_map/ppermute | solution.py:42
  17.1 2.0 %collective-permute-done.3.refs_0_ = bf16[128,1024]{1,0:T(8,128)(2,1)S(1)} collective-permute-done((bf16[128,1024]{1,0:T(8,128)(2,1)S(1)}, bf16[128,1024]{1,0:T(8,128)(2,1)S(1)}, u32[]{:S(2)}, u32[]{:S(2)}) %collective-permute-start.3) | collective-permute-done | bytes 262176 | tf_op jit(solution)/shard_map/ppermute | solution.py:42
  19.1 2.8 %collective-permute-start.8 = (bf16[3,128,1024]{2,1,0:T(8,128)(2,1)S(1)}, bf16[3,128,1024]{2,1,0:T(8,128)(2,1)S(1)}, u32[]{:S(2)}, u32[]{:S(2)}) collective-permute-start(bf16[3,128,1024]{2,1,0:T(8,128)(2,1)S(1)} %pack.3.refs_2_), channel_id=1, source_target_pairs={{0,1},{1,0},{2,3},{3,2},{4,5},{5,4},{6,7},{7,6},{8,9},{9,8},{10,11... | collective-permute-start | bytes 2359304 | tf_op jit(solution)/shard_map/ppermute | solution.py:42
  22.3 5.8 %collective-permute-done.11.refs_6_ = bf16[128,512]{1,0:T(8,128)(2,1)S(1)} collective-permute-done((bf16[128,512]{1,0:T(8,128)(2,1)S(1)}, bf16[128,512]{1,0:T(8,128)(2,1)S(1)}, u32[]{:S(2)}, u32[]{:S(2)}) %collective-permute-start.11) | collective-permute-done | bytes 131104 | tf_op jit(solution)/shard_map/ppermute | solution.py:42
  31.0 7.5 %attention.3 = (bf16[128,512]{1,0:T(8,128)(2,1)S(1)}, bf16[128,512]{1,0:T(8,128)(2,1)S(1)}, bf16[128,512]{1,0:T(8,128)(2,1)S(1)}, bf16[128,512]{1,0:T(8,128)(2,1)S(1)}) custom-call(s32[16]{0:T(128)} %span_map.3, s32[1]{0:T(128)} %bitcast.1.ctx, s32[1]{0:T(128)} %bitcast.section, bf16[128,4096]{1,0:T(8,128)(2,1)} %bitcast.3, ...), custom_call_target="tpu_custom_call" | custom-call | flops 4294967296 | bytes 3145728 | tf_op jit(solution)/shard_map/attention/pallas_call | solution.py:205
  38.5 3.2 %collective-permute-start.16 = (bf16[128,512]{1,0:T(8,128)(2,1)S(1)}, bf16[128,512]{1,0:T(8,128)(2,1)S(1)}, u32[]{:S(2)}, u32[]{:S(2)}) collective-permute-start(bf16[128,512]{1,0:T(8,128)(2,1)S(1)} %get-tuple-element.51), channel_id=1, source_target_pairs={{0,16},{16,32},{32,48},{48,0},{64,80},{80,96},{96,112},{112,64},{1... | collective-permute-start | bytes 393224 | tf_op jit(solution)/shard_map/ppermute | solution.py:309
  41.8 4.2 %collective-permute-start.17 = (bf16[128,512]{1,0:T(8,128)(2,1)S(1)}, bf16[128,512]{1,0:T(8,128)(2,1)S(1)}, u32[]{:S(2)}, u32[]{:S(2)}) collective-permute-start(bf16[128,512]{1,0:T(8,128)(2,1)S(1)} %get-tuple-element.52), channel_id=1, source_target_pairs={{0,32},{16,48},{32,0},{48,16},{64,96},{80,112},{96,64},{112,80},{1... | collective-permute-start | bytes 393224 | tf_op jit(solution)/shard_map/ppermute | solution.py:309
  46.0 2.4 %collective-permute-start.18 = (bf16[128,512]{1,0:T(8,128)(2,1)S(1)}, bf16[128,512]{1,0:T(8,128)(2,1)S(1)}, u32[]{:S(2)}, u32[]{:S(2)}) collective-permute-start(bf16[128,512]{1,0:T(8,128)(2,1)S(1)} %get-tuple-element.53), channel_id=1, source_target_pairs={{0,48},{16,0},{32,16},{48,32},{64,112},{80,64},{96,80},{112,96},{1... | collective-permute-start | bytes 393224 | tf_op jit(solution)/shard_map/ppermute | solution.py:309
  48.4 7.4 %attention.2 = (bf16[128,512]{1,0:T(8,128)(2,1)S(1)}, bf16[128,512]{1,0:T(8,128)(2,1)S(1)}, bf16[128,512]{1,0:T(8,128)(2,1)S(1)}, bf16[128,512]{1,0:T(8,128)(2,1)S(1)}) custom-call(s32[16]{0:T(128)} %span_map.3, s32[1]{0:T(128)} %bitcast.1.ctx, s32[1]{0:T(128)} %bitcast.section, bf16[128,4096]{1,0:T(8,128)(2,1)} %bitcast.4, ...), custom_call_target="tpu_custom_call" | custom-call | flops 4294967296 | bytes 3145728 | tf_op jit(solution)/shard_map/attention/pallas_call | solution.py:205
  55.9 2.1 %collective-permute-start.14 = (bf16[128,512]{1,0:T(8,128)(2,1)S(1)}, bf16[128,512]{1,0:T(8,128)(2,1)S(1)}, u32[]{:S(2)}, u32[]{:S(2)}) collective-permute-start(bf16[128,512]{1,0:T(8,128)(2,1)S(1)} %get-tuple-element.46), channel_id=1, source_target_pairs={{0,32},{16,48},{32,0},{48,16},{64,96},{80,112},{96,64},{112,80},{1... | collective-permute-start | bytes 393224 | tf_op jit(solution)/shard_map/ppermute | solution.py:309
  58.0 2.5 %collective-permute-start.15 = (bf16[128,512]{1,0:T(8,128)(2,1)S(1)}, bf16[128,512]{1,0:T(8,128)(2,1)S(1)}, u32[]{:S(2)}, u32[]{:S(2)}) collective-permute-start(bf16[128,512]{1,0:T(8,128)(2,1)S(1)} %get-tuple-element.47), channel_id=1, source_target_pairs={{0,48},{16,0},{32,16},{48,32},{64,112},{80,64},{96,80},{112,96},{1... | collective-permute-start | bytes 393224 | tf_op jit(solution)/shard_map/ppermute | solution.py:309
  60.6 2.8 %collective-permute-start.21 = (bf16[128,512]{1,0:T(8,128)(2,1)S(1)}, bf16[128,512]{1,0:T(8,128)(2,1)S(1)}, u32[]{:S(2)}, u32[]{:S(2)}) collective-permute-start(bf16[128,512]{1,0:T(8,128)(2,1)S(1)} %row_total.3), channel_id=1, source_target_pairs={{0,192},{16,208},{32,224},{48,240},{64,0},{80,16},{96,32},{112,48}... | collective-permute-start | bytes 393224 | tf_op jit(solution)/shard_map/ppermute | solution.py:327
  65.2 2.8 %collective-permute-done.14.c.refs_2_ = bf16[128,512]{1,0:T(8,128)(2,1)S(1)} collective-permute-done((bf16[128,512]{1,0:T(8,128)(2,1)S(1)}, bf16[128,512]{1,0:T(8,128)(2,1)S(1)}, u32[]{:S(2)}, u32[]{:S(2)}) %collective-permute-start.14) | collective-permute-done | bytes 131104 | tf_op jit(solution)/shard_map/ppermute | solution.py:309
  68.0 5.6 %collective-permute-done.15.d.refs_3_ = bf16[128,512]{1,0:T(8,128)(2,1)S(1)} collective-permute-done((bf16[128,512]{1,0:T(8,128)(2,1)S(1)}, bf16[128,512]{1,0:T(8,128)(2,1)S(1)}, u32[]{:S(2)}, u32[]{:S(2)}) %collective-permute-start.15) | collective-permute-done | bytes 131104 | tf_op jit(solution)/shard_map/ppermute | solution.py:309
  74.0 2.8 %collective-permute-start.27 = (bf16[128,512]{1,0:T(8,128)(2,1)S(1)}, bf16[128,512]{1,0:T(8,128)(2,1)S(1)}, u32[]{:S(2)}, u32[]{:S(2)}) collective-permute-start(bf16[128,512]{1,0:T(8,128)(2,1)S(1)} %row_total.2), channel_id=1, source_target_pairs={{0,192},{16,208},{32,224},{48,240},{64,0},{80,16},{96,32},{112,48}... | collective-permute-start | bytes 393224 | tf_op jit(solution)/shard_map/ppermute | solution.py:327
  80.5 2.7 %collective-permute-start.24 = (bf16[128,512]{1,0:T(8,128)(2,1)S(1)}, bf16[128,512]{1,0:T(8,128)(2,1)S(1)}, u32[]{:S(2)}, u32[]{:S(2)}) collective-permute-start(bf16[128,512]{1,0:T(8,128)(2,1)S(1)} %get-tuple-element.61), channel_id=1, source_target_pairs={{0,48},{16,0},{32,16},{48,32},{64,112},{80,64},{96,80},{112,96},{1... | collective-permute-start | bytes 393224 | tf_op jit(solution)/shard_map/ppermute | solution.py:309
  83.2 3.1 %collective-permute-done.25.refs_4_ = bf16[128,512]{1,0:T(8,128)(2,1)S(1)} collective-permute-done((bf16[128,512]{1,0:T(8,128)(2,1)S(1)}, bf16[128,512]{1,0:T(8,128)(2,1)S(1)}, u32[]{:S(2)}, u32[]{:S(2)}) %collective-permute-start.25) | collective-permute-done | bytes 131104 | tf_op jit(solution)/shard_map/ppermute | solution.py:327
  89.2 3.1 %collective-permute-start.30 = (bf16[128,512]{1,0:T(8,128)(2,1)S(1)}, bf16[128,512]{1,0:T(8,128)(2,1)S(1)}, u32[]{:S(2)}, u32[]{:S(2)}) collective-permute-start(bf16[128,512]{1,0:T(8,128)(2,1)S(1)} %get-tuple-element.66), channel_id=1, source_target_pairs={{0,48},{16,0},{32,16},{48,32},{64,112},{80,64},{96,80},{112,96},{1... | collective-permute-start | bytes 393224 | tf_op jit(solution)/shard_map/ppermute | solution.py:309
  92.2 4.2 %collective-permute-done.28.refs_5_ = bf16[128,512]{1,0:T(8,128)(2,1)S(1)} collective-permute-done((bf16[128,512]{1,0:T(8,128)(2,1)S(1)}, bf16[128,512]{1,0:T(8,128)(2,1)S(1)}, u32[]{:S(2)}, u32[]{:S(2)}) %collective-permute-start.28) | collective-permute-done | bytes 131104 | tf_op jit(solution)/shard_map/ppermute | solution.py:309
  96.4 2.9 %collective-permute-done.29.refs_6_ = bf16[128,512]{1,0:T(8,128)(2,1)S(1)} collective-permute-done((bf16[128,512]{1,0:T(8,128)(2,1)S(1)}, bf16[128,512]{1,0:T(8,128)(2,1)S(1)}, u32[]{:S(2)}, u32[]{:S(2)}) %collective-permute-start.29) | collective-permute-done | bytes 131104 | tf_op jit(solution)/shard_map/ppermute | solution.py:309
  99.3 6.3 %collective-permute-done.30.refs_7_ = bf16[128,512]{1,0:T(8,128)(2,1)S(1)} collective-permute-done((bf16[128,512]{1,0:T(8,128)(2,1)S(1)}, bf16[128,512]{1,0:T(8,128)(2,1)S(1)}, u32[]{:S(2)}, u32[]{:S(2)}) %collective-permute-start.30) | collective-permute-done | bytes 131104 | tf_op jit(solution)/shard_map/ppermute | solution.py:309
  (52 shorter events, 19.3 us)
Async XLA Ops:
  3.1 8.8 %collective-permute-start = (bf16[128,1024]{1,0:T(8,128)(2,1)S(1)}, bf16[128,1024]{1,0:T(8,128)(2,1)S(1)}, u32[]{:S(2)}, u32[]{:S(2)}) collective-permute-start(bf16[128,1024]{1,0:T(8,128)(2,1)S(1)} %join.1.refs_0_), channel_id=1, source_target_pairs={{0,2},{1,3},{2,0},{3,1},{4,6},{5,7},{6,4},{7,5},{8,10},{9,11},{10,... | collective-permute-start | bytes 786440 | tf_op jit(solution)/shard_map/ppermute | solution.py:42
  4.7 9.9 %collective-permute-start.2 = (bf16[128,1024]{1,0:T(8,128)(2,1)S(1)}, bf16[128,1024]{1,0:T(8,128)(2,1)S(1)}, u32[]{:S(2)}, u32[]{:S(2)}) collective-permute-start(bf16[128,1024]{1,0:T(8,128)(2,1)S(1)} %join.1.refs_0_), channel_id=1, source_target_pairs={{0,12},{1,13},{2,14},{3,15},{4,0},{5,1},{6,2},{7,3},{8,4},{9,5},{1... | collective-permute-start | bytes 786440 | tf_op jit(solution)/shard_map/ppermute | solution.py:42
  8.1 9.0 %collective-permute-start.5 = (bf16[128,1024]{1,0:T(8,128)(2,1)S(1)}, bf16[128,1024]{1,0:T(8,128)(2,1)S(1)}, u32[]{:S(2)}, u32[]{:S(2)}) collective-permute-start(bf16[128,1024]{1,0:T(8,128)(2,1)S(1)} %collective-permute-done.1.refs_1_), channel_id=1, source_target_pairs={{0,2},{1,3},{2,0},{3,1},{4,6},{5,7},{6,4},{7,5},{8,10},{9,11},{10,... | collective-permute-start | bytes 786440 | tf_op jit(solution)/shard_map/ppermute | solution.py:42
  11.9 7.2 %collective-permute-start.3 = (bf16[128,1024]{1,0:T(8,128)(2,1)S(1)}, bf16[128,1024]{1,0:T(8,128)(2,1)S(1)}, u32[]{:S(2)}, u32[]{:S(2)}) collective-permute-start(bf16[128,1024]{1,0:T(8,128)(2,1)S(1)} %collective-permute-done.1.refs_1_), channel_id=1, source_target_pairs={{0,4},{1,5},{2,6},{3,7},{4,8},{5,9},{6,10},{7,11},{8,12},{9,13},{1... | collective-permute-start | bytes 786440 | tf_op jit(solution)/shard_map/ppermute | solution.py:42
  11.9 7.2 %collective-permute-start.4 = (bf16[128,1024]{1,0:T(8,128)(2,1)S(1)}, bf16[128,1024]{1,0:T(8,128)(2,1)S(1)}, u32[]{:S(2)}, u32[]{:S(2)}) collective-permute-start(bf16[128,1024]{1,0:T(8,128)(2,1)S(1)} %collective-permute-done.refs_0_), channel_id=1, source_target_pairs={{0,12},{1,13},{2,14},{3,15},{4,0},{5,1},{6,2},{7,3},{8,4},{9,5},{1... | collective-permute-start | bytes 786440 | tf_op jit(solution)/shard_map/ppermute | solution.py:42
  14.6 16.4 %collective-permute-start.7 = (bf16[3,128,1024]{2,1,0:T(8,128)(2,1)S(1)}, bf16[3,128,1024]{2,1,0:T(8,128)(2,1)S(1)}, u32[]{:S(2)}, u32[]{:S(2)}) collective-permute-start(bf16[3,128,1024]{2,1,0:T(8,128)(2,1)S(1)} %pack.2.refs_1_), channel_id=1, source_target_pairs={{0,1},{1,0},{2,3},{3,2},{4,5},{5,4},{6,7},{7,6},{8,9},{9,8},{10,11... | collective-permute-start | bytes 2359304 | tf_op jit(solution)/shard_map/ppermute | solution.py:42
  19.1 11.9 %collective-permute-start.8 = (bf16[3,128,1024]{2,1,0:T(8,128)(2,1)S(1)}, bf16[3,128,1024]{2,1,0:T(8,128)(2,1)S(1)}, u32[]{:S(2)}, u32[]{:S(2)}) collective-permute-start(bf16[3,128,1024]{2,1,0:T(8,128)(2,1)S(1)} %pack.3.refs_2_), channel_id=1, source_target_pairs={{0,1},{1,0},{2,3},{3,2},{4,5},{5,4},{6,7},{7,6},{8,9},{9,8},{10,11... | collective-permute-start | bytes 2359304 | tf_op jit(solution)/shard_map/ppermute | solution.py:42
  22.0 7.3 %collective-permute-start.6 = (bf16[128,1024]{1,0:T(8,128)(2,1)S(1)}, bf16[128,1024]{1,0:T(8,128)(2,1)}, u32[]{:S(2)}, u32[]{:S(2)}) collective-permute-start(bf16[128,1024]{1,0:T(8,128)(2,1)S(1)} %join.1.refs_0_), channel_id=1, source_target_pairs={{0,1},{1,0},{2,3},{3,2},{4,5},{5,4},{6,7},{7,6},{8,9},{9,8},{10,11... | collective-permute-start | bytes 786440 | tf_op jit(solution)/shard_map/ppermute | solution.py:42
  38.5 19.5 %collective-permute-start.16 = (bf16[128,512]{1,0:T(8,128)(2,1)S(1)}, bf16[128,512]{1,0:T(8,128)(2,1)S(1)}, u32[]{:S(2)}, u32[]{:S(2)}) collective-permute-start(bf16[128,512]{1,0:T(8,128)(2,1)S(1)} %get-tuple-element.51), channel_id=1, source_target_pairs={{0,16},{16,32},{32,48},{48,0},{64,80},{80,96},{96,112},{112,64},{1... | collective-permute-start | bytes 393224 | tf_op jit(solution)/shard_map/ppermute | solution.py:309
  41.8 18.7 %collective-permute-start.17 = (bf16[128,512]{1,0:T(8,128)(2,1)S(1)}, bf16[128,512]{1,0:T(8,128)(2,1)S(1)}, u32[]{:S(2)}, u32[]{:S(2)}) collective-permute-start(bf16[128,512]{1,0:T(8,128)(2,1)S(1)} %get-tuple-element.52), channel_id=1, source_target_pairs={{0,32},{16,48},{32,0},{48,16},{64,96},{80,112},{96,64},{112,80},{1... | collective-permute-start | bytes 393224 | tf_op jit(solution)/shard_map/ppermute | solution.py:309
  46.0 14.5 %collective-permute-start.18 = (bf16[128,512]{1,0:T(8,128)(2,1)S(1)}, bf16[128,512]{1,0:T(8,128)(2,1)S(1)}, u32[]{:S(2)}, u32[]{:S(2)}) collective-permute-start(bf16[128,512]{1,0:T(8,128)(2,1)S(1)} %get-tuple-element.53), channel_id=1, source_target_pairs={{0,48},{16,0},{32,16},{48,32},{64,112},{80,64},{96,80},{112,96},{1... | collective-permute-start | bytes 393224 | tf_op jit(solution)/shard_map/ppermute | solution.py:309
  55.8 8.0 %collective-permute-start.13 = (bf16[128,512]{1,0:T(8,128)(2,1)S(1)}, bf16[128,512]{1,0:T(8,128)(2,1)S(1)}, u32[]{:S(2)}, u32[]{:S(2)}) collective-permute-start(bf16[128,512]{1,0:T(8,128)(2,1)S(1)} %get-tuple-element.45), channel_id=1, source_target_pairs={{0,16},{16,32},{32,48},{48,0},{64,80},{80,96},{96,112},{112,64},{1... | collective-permute-start | bytes 393224 | tf_op jit(solution)/shard_map/ppermute | solution.py:309
  55.9 12.1 %collective-permute-start.14 = (bf16[128,512]{1,0:T(8,128)(2,1)S(1)}, bf16[128,512]{1,0:T(8,128)(2,1)S(1)}, u32[]{:S(2)}, u32[]{:S(2)}) collective-permute-start(bf16[128,512]{1,0:T(8,128)(2,1)S(1)} %get-tuple-element.46), channel_id=1, source_target_pairs={{0,32},{16,48},{32,0},{48,16},{64,96},{80,112},{96,64},{112,80},{1... | collective-permute-start | bytes 393224 | tf_op jit(solution)/shard_map/ppermute | solution.py:309
  58.0 15.6 %collective-permute-start.15 = (bf16[128,512]{1,0:T(8,128)(2,1)S(1)}, bf16[128,512]{1,0:T(8,128)(2,1)S(1)}, u32[]{:S(2)}, u32[]{:S(2)}) collective-permute-start(bf16[128,512]{1,0:T(8,128)(2,1)S(1)} %get-tuple-element.47), channel_id=1, source_target_pairs={{0,48},{16,0},{32,16},{48,32},{64,112},{80,64},{96,80},{112,96},{1... | collective-permute-start | bytes 393224 | tf_op jit(solution)/shard_map/ppermute | solution.py:309
  60.6 13.1 %collective-permute-start.21 = (bf16[128,512]{1,0:T(8,128)(2,1)S(1)}, bf16[128,512]{1,0:T(8,128)(2,1)S(1)}, u32[]{:S(2)}, u32[]{:S(2)}) collective-permute-start(bf16[128,512]{1,0:T(8,128)(2,1)S(1)} %row_total.3), channel_id=1, source_target_pairs={{0,192},{16,208},{32,224},{48,240},{64,0},{80,16},{96,32},{112,48}... | collective-permute-start | bytes 393224 | tf_op jit(solution)/shard_map/ppermute | solution.py:327
  63.4 10.3 %collective-permute-start.20 = (bf16[128,512]{1,0:T(8,128)(2,1)S(1)}, bf16[128,512]{1,0:T(8,128)(2,1)S(1)}, u32[]{:S(2)}, u32[]{:S(2)}) collective-permute-start(bf16[128,512]{1,0:T(8,128)(2,1)S(1)} %row_total.3), channel_id=1, source_target_pairs={{0,128},{16,144},{32,160},{48,176},{64,192},{80,208},{96,224},{112... | collective-permute-start | bytes 393224 | tf_op jit(solution)/shard_map/ppermute | solution.py:327
  63.8 9.9 %collective-permute-start.19 = (bf16[128,512]{1,0:T(8,128)(2,1)S(1)}, bf16[128,512]{1,0:T(8,128)(2,1)S(1)}, u32[]{:S(2)}, u32[]{:S(2)}) collective-permute-start(bf16[128,512]{1,0:T(8,128)(2,1)S(1)} %row_total.3), channel_id=1, source_target_pairs={{0,64},{16,80},{32,96},{48,112},{64,128},{80,144},{96,160},{112,17... | collective-permute-start | bytes 393224 | tf_op jit(solution)/shard_map/ppermute | solution.py:327
  77.2 9.2 %collective-permute-start.25 = (bf16[128,512]{1,0:T(8,128)(2,1)S(1)}, bf16[128,512]{1,0:T(8,128)(2,1)S(1)}, u32[]{:S(2)}, u32[]{:S(2)}) collective-permute-start(bf16[128,512]{1,0:T(8,128)(2,1)S(1)} %row_total.2), channel_id=1, source_target_pairs={{0,64},{16,80},{32,96},{48,112},{64,128},{80,144},{96,160},{112,17... | collective-permute-start | bytes 393224 | tf_op jit(solution)/shard_map/ppermute | solution.py:327
  77.9 11.3 %collective-permute-start.22 = (bf16[128,512]{1,0:T(8,128)(2,1)S(1)}, bf16[128,512]{1,0:T(8,128)(2,1)S(1)}, u32[]{:S(2)}, u32[]{:S(2)}) collective-permute-start(bf16[128,512]{1,0:T(8,128)(2,1)S(1)} %get-tuple-element.59), channel_id=1, source_target_pairs={{0,16},{16,32},{32,48},{48,0},{64,80},{80,96},{96,112},{112,64},{1... | collective-permute-start | bytes 393224 | tf_op jit(solution)/shard_map/ppermute | solution.py:309
  78.6 13.6 %collective-permute-start.23 = (bf16[128,512]{1,0:T(8,128)(2,1)S(1)}, bf16[128,512]{1,0:T(8,128)(2,1)S(1)}, u32[]{:S(2)}, u32[]{:S(2)}) collective-permute-start(bf16[128,512]{1,0:T(8,128)(2,1)S(1)} %get-tuple-element.60), channel_id=1, source_target_pairs={{0,32},{16,48},{32,0},{48,16},{64,96},{80,112},{96,64},{112,80},{1... | collective-permute-start | bytes 393224 | tf_op jit(solution)/shard_map/ppermute | solution.py:309
  80.5 11.8 %collective-permute-start.24 = (bf16[128,512]{1,0:T(8,128)(2,1)S(1)}, bf16[128,512]{1,0:T(8,128)(2,1)S(1)}, u32[]{:S(2)}, u32[]{:S(2)}) collective-permute-start(bf16[128,512]{1,0:T(8,128)(2,1)S(1)} %get-tuple-element.61), channel_id=1, source_target_pairs={{0,48},{16,0},{32,16},{48,32},{64,112},{80,64},{96,80},{112,96},{1... | collective-permute-start | bytes 393224 | tf_op jit(solution)/shard_map/ppermute | solution.py:309
  86.6 9.8 %collective-permute-start.28 = (bf16[128,512]{1,0:T(8,128)(2,1)S(1)}, bf16[128,512]{1,0:T(8,128)(2,1)S(1)}, u32[]{:S(2)}, u32[]{:S(2)}) collective-permute-start(bf16[128,512]{1,0:T(8,128)(2,1)S(1)} %get-tuple-element.64), channel_id=1, source_target_pairs={{0,16},{16,32},{32,48},{48,0},{64,80},{80,96},{96,112},{112,64},{1... | collective-permute-start | bytes 393224 | tf_op jit(solution)/shard_map/ppermute | solution.py:309
  87.5 11.7 %collective-permute-start.29 = (bf16[128,512]{1,0:T(8,128)(2,1)S(1)}, bf16[128,512]{1,0:T(8,128)(2,1)S(1)}, u32[]{:S(2)}, u32[]{:S(2)}) collective-permute-start(bf16[128,512]{1,0:T(8,128)(2,1)S(1)} %get-tuple-element.65), channel_id=1, source_target_pairs={{0,32},{16,48},{32,0},{48,16},{64,96},{80,112},{96,64},{112,80},{1... | collective-permute-start | bytes 393224 | tf_op jit(solution)/shard_map/ppermute | solution.py:309
  89.2 16.4 %collective-permute-start.30 = (bf16[128,512]{1,0:T(8,128)(2,1)S(1)}, bf16[128,512]{1,0:T(8,128)(2,1)S(1)}, u32[]{:S(2)}, u32[]{:S(2)}) collective-permute-start(bf16[128,512]{1,0:T(8,128)(2,1)S(1)} %get-tuple-element.66), channel_id=1, source_target_pairs={{0,48},{16,0},{32,16},{48,32},{64,112},{80,64},{96,80},{112,96},{1... | collective-permute-start | bytes 393224 | tf_op jit(solution)/shard_map/ppermute | solution.py:309
  (8 other events, 55.1 us)

commit v3 on v0

--- a/solution.py
+++ b/solution.py
@@ -21,9 +21,8 @@
 HIDDEN = -1e30
 VMEM_LIMIT = 24 * 2**20
 CHUNKS = 2
-PART = KEY_VALUE_HEADS // CHUNKS
-
-SIDE = PART * HEAD_SIZE
+PARTS = (3, 1)
+BASES = (0, 3)
 
 UNITS = [(dx, dz, dc) for dc in range(2) for dz in range(2) for dx in range(4)]
 
@@ -55,11 +54,12 @@
 def join_kernel(k_ref, v_ref, o_ref, sems):
     copies = []
     for chunk in range(CHUNKS):
+        base, width = BASES[chunk] * HEAD_SIZE, PARTS[chunk] * HEAD_SIZE
         for side, source in enumerate((k_ref, v_ref)):
             copies.append(
                 pltpu.make_async_copy(
-                    source.at[0, :, pl.ds(chunk * SIDE, SIDE)],
-                    o_ref.at[:, pl.ds((2 * chunk + side) * SIDE, SIDE)],
+                    source.at[0, :, pl.ds(base, width)],
+                    o_ref.at[:, pl.ds(2 * base + side * width, width)],
                     sems.at[chunk, side],
                 )
             )
@@ -103,12 +103,13 @@
 def attention_kernel(chunk, span_map, ctx, section, q_hbm, *refs):
     units, o_refs = refs[:SPANS], refs[SPANS : SPANS + RING]
     q_ref, keys, vals, sems = refs[SPANS + RING :]
+    base, parts = BASES[chunk], PARTS[chunk]
     copies = []
-    for part in range(PART):
+    for part in range(parts):
         width = GROUP * HEAD_SIZE
         copies.append(
             pltpu.make_async_copy(
-                q_hbm.at[:, pl.ds((chunk * PART + part) * width, width)],
+                q_hbm.at[:, pl.ds((base + part) * width, width)],
                 q_ref.at[part],
                 sems.at[part],
             )
@@ -126,13 +127,13 @@
         ahead = (span_map[source] - my_span) * TOK + key_row - query_row
         mask = jnp.where(ahead > 0, HIDDEN, 0.0).astype(jnp.bfloat16)
         rows = slice(block * TOK, (block + 1) * TOK)
-        for part in range(PART):
-            first = chunk * 2 * SIDE + part * HEAD_SIZE
+        for part in range(parts):
+            first = (2 * base + part) * HEAD_SIZE
             keys[part, rows, :HEAD_SIZE] = units[block][:, first : first + HEAD_SIZE]
             keys[part, rows, HEAD_SIZE:] = mask
-            first += SIDE
+            first += parts * HEAD_SIZE
             vals[part, rows, :HEAD_SIZE] = units[block][:, first : first + HEAD_SIZE]
-    for part in range(PART):
+    for part in range(parts):
         vals[part, :, HEAD_SIZE:] = jnp.ones((TRACE, HEAD_SIZE), jnp.bfloat16)
     place = section[0] % RING
 
@@ -163,7 +164,7 @@
     for copy in copies:
         copy.wait()
 
-    @pl.loop(0, PART)
+    @pl.loop(0, parts)
     def _(part):
         scores = weights = None
         for steps in range(RING + 2):
@@ -177,22 +178,23 @@
 def attention(span_map, ctx, section, queries, units, chunk):
     smem = pl.BlockSpec(memory_space=pltpu.SMEM)
     vmem = pl.BlockSpec(memory_space=pltpu.VMEM)
+    parts = PARTS[chunk]
     return pl.pallas_call(
         functools.partial(attention_kernel, chunk),
         in_specs=[smem, smem, smem, pl.BlockSpec(memory_space=pltpu.HBM)] + [vmem] * SPANS,
         out_specs=[vmem] * RING,
-        out_shape=[jax.ShapeDtypeStruct((TOK, PART * PAIR), jnp.bfloat16)] * RING,
+        out_shape=[jax.ShapeDtypeStruct((TOK, parts * PAIR), jnp.bfloat16)] * RING,
         scratch_shapes=[
-            pltpu.VMEM((PART, TOK, GROUP * HEAD_SIZE), jnp.bfloat16),
-            pltpu.VMEM((PART, TRACE, PAIR), jnp.bfloat16),
-            pltpu.VMEM((PART, TRACE, PAIR), jnp.bfloat16),
-            pltpu.SemaphoreType.DMA((PART,)),
+            pltpu.VMEM((parts, TOK, GROUP * HEAD_SIZE), jnp.bfloat16),
+            pltpu.VMEM((parts, TRACE, PAIR), jnp.bfloat16),
+            pltpu.VMEM((parts, TRACE, PAIR), jnp.bfloat16),
+            pltpu.SemaphoreType.DMA((parts,)),
         ],
         compiler_params=pltpu.CompilerParams(vmem_limit_bytes=VMEM_LIMIT),
         cost_estimate=pl.CostEstimate(
-            flops=PART * GROUP * TOK * TRACE * PAIR * 2 * 2,
-            bytes_accessed=PART * (TRACE * PAIR + GROUP * TOK * PAIR) * 2,
-            transcendentals=PART * GROUP * TOK * TRACE,
+            flops=parts * GROUP * TOK * TRACE * PAIR * 2 * 2,
+            bytes_accessed=parts * (TRACE * PAIR + GROUP * TOK * PAIR) * 2,
+            transcendentals=parts * GROUP * TOK * TRACE,
         ),
         name="attention",
     )(pinned(span_map), ctx, section, pinned(queries), *units)
@@ -210,7 +212,7 @@
         total_kernel,
         in_specs=[pl.BlockSpec(memory_space=pltpu.VMEM)] * RING,
         out_specs=pl.BlockSpec(memory_space=pltpu.VMEM),
-        out_shape=jax.ShapeDtypeStruct((TOK, PART * PAIR), jnp.bfloat16),
+        out_shape=jax.ShapeDtypeStruct(slabs[0].shape, jnp.bfloat16),
         compiler_params=pltpu.CompilerParams(vmem_limit_bytes=4 * 2**20),
         name="row_total",
     )(*slabs)
@@ -222,9 +224,9 @@
     place, row = section[0] % RING, section[0] // RING
     for steps in range(RING):
         ordered[(place + RING - steps) % RING] = slabs[steps][...]
-    for part in range(PART):
+    for part in range(PARTS[chunk]):
         columns = slice(part * PAIR, (part + 1) * PAIR)
-        first = (chunk * PART + part) * GROUP * HEAD_SIZE + place * PAIR
+        first = (BASES[chunk] + part) * GROUP * HEAD_SIZE + place * PAIR
         state = residual_ref[:, pl.ds(pl.multiple_of(first, PAIR), PAIR)].astype(jnp.float32)
         for steps, rows in enumerate(below, 1):
             earlier = rows[:, columns].astype(jnp.float32)
@@ -237,7 +239,7 @@
 
 
 def prefix(section, residual, slabs, below, chunk):
-    slab = jax.ShapeDtypeStruct((TOK, PART * PAIR), jnp.bfloat16)
+    slab = jax.ShapeDtypeStruct(slabs[0].shape, jnp.bfloat16)
     whole = pl.BlockSpec(memory_space=pltpu.VMEM)
     return pl.pallas_call(
         functools.partial(prefix_kernel, chunk),
@@ -245,8 +247,8 @@
         out_specs=[whole] * RING,
         out_shape=[slab] * RING,
         scratch_shapes=[
-            pltpu.VMEM((RING, TOK, PART * PAIR), jnp.bfloat16),
-            pltpu.VMEM((RING, TOK, PART * PAIR), jnp.bfloat16),
+            pltpu.VMEM((RING, *slab.shape), jnp.bfloat16),
+            pltpu.VMEM((RING, *slab.shape), jnp.bfloat16),
         ],
         compiler_params=pltpu.CompilerParams(vmem_limit_bytes=8 * 2**20),
         name="prefix",
@@ -259,8 +261,8 @@
     for chunk in range(CHUNKS):
         for steps in range(RING):
             column = (place + RING - steps) % RING * PAIR
-            for part in range(PART):
-                first = (chunk * PART + part) * GROUP * HEAD_SIZE + column
+            for part in range(PARTS[chunk]):
+                first = (BASES[chunk] + part) * GROUP * HEAD_SIZE + column
                 o_ref[0, :, pl.ds(pl.multiple_of(first, PAIR), PAIR)] = slabs[
                     chunk * RING + steps
                 ][:, part * PAIR : (part + 1) * PAIR]
@@ -289,10 +291,9 @@
     ctx = lax.axis_index("ctx")[None]
     section = lax.axis_index("section")[None]
     units = gather(keys, values)
-    slabs = [
-        turn(attention(span_map, ctx, section, queries[0], units, chunk))
-        for chunk in range(CHUNKS)
-    ]
+    raw = [attention(span_map, ctx, section, queries[0], units, c) for c in range(CHUNKS)]
+    slabs = [turn(r) for r in raw]
+    slabs[0], _ = lax.optimization_barrier((slabs[0], raw[1]))
     finished, sums = [], None
     for chunk in range(CHUNKS):
         total = row_total(slabs[chunk])

time: 107 us -> 115 us (1.075)
  the two profiles are of different devices: /device:TPU:1 before, /device:TPU:16 now
where the time goes in v3:
time: 115 us; the launch traced here: 114 us
  starting transfers between devices  54 us (47%)
  waiting for transfers between devices  42.4 us (37%)
  Pallas kernels  17.9 us (16%)
    ppermute x12, starting transfers between devices, turn(): lax.ppermute(slabs[steps], 'section', turn_pairs(steps))  31.2 us
    ppermute x12, waiting for transfers between devices, turn(): lax.ppermute(slabs[steps], 'section', turn_pairs(steps))  30.5 us
    pallas_call x2, Pallas kernels, attention(): pl.pallas_call(functools.partial(attention_kernel, chunk), in_specs=[smem...  15.2 us
    ppermute x15, starting transfers between devices, ctx_move(): return lax.ppermute(unit, 'ctx', ctx_pairs(dx, dz, dc))  13.8 us
    ppermute x15, waiting for transfers between devices, ctx_move(): return lax.ppermute(unit, 'ctx', ctx_pairs(dx, dz, dc))  11.9 us
    ppermute x6, starting transfers between devices, body(): lax.ppermute(total, 'section', climb_pairs(s))  8.95 us
  transfers between devices with their start and end apart: 33, of which 11 were waited for; matrix products, arithmetic and copies ran while one was open for 0% of the time, Pallas kernels for 4%

profile of v3, /device:TPU:16, one launch (start us, length us, event | category | flops | bytes accessed | tf_op | source)
XLA Modules:
  0.0 114.4 jit_solution(7982537538264206176)
XLA Ops:
  2.6 1.9 %collective-permute-start.3 = (bf16[128,1024]{1,0:T(8,128)(2,1)S(1)}, bf16[128,1024]{1,0:T(8,128)(2,1)S(1)}, u32[]{:S(2)}, u32[]{:S(2)}) collective-permute-start(bf16[128,1024]{1,0:T(8,128)(2,1)S(1)} %join.1.refs_0_), channel_id=1, source_target_pairs={{0,2},{1,3},{2,0},{3,1},{4,6},{5,7},{6,4},{7,5},{8,10},{9,11},{10,... | collective-permute-start | bytes 786440 | tf_op jit(solution)/shard_map/ppermute | solution.py:39
  6.2 4.1 %collective-permute-done.refs_1_ = bf16[128,1024]{1,0:T(8,128)(2,1)S(1)} collective-permute-done((bf16[128,1024]{1,0:T(8,128)(2,1)S(1)}, bf16[128,1024]{1,0:T(8,128)(2,1)S(1)}, u32[]{:S(2)}, u32[]{:S(2)}) %collective-permute-start) | collective-permute-done | bytes 262176 | tf_op jit(solution)/shard_map/ppermute | solution.py:39
  10.6 1.9 %collective-permute-start.4 = (bf16[128,1024]{1,0:T(8,128)(2,1)S(1)}, bf16[128,1024]{1,0:T(8,128)(2,1)S(1)}, u32[]{:S(2)}, u32[]{:S(2)}) collective-permute-start(bf16[128,1024]{1,0:T(8,128)(2,1)S(1)} %collective-permute-done.refs_1_), channel_id=1, source_target_pairs={{0,2},{1,3},{2,0},{3,1},{4,6},{5,7},{6,4},{7,5},{8,10},{9,11},{10,... | collective-permute-start | bytes 786440 | tf_op jit(solution)/shard_map/ppermute | solution.py:39
  12.5 3.0 %collective-permute-start.6 = (bf16[128,1024]{1,0:T(8,128)(2,1)S(1)}, bf16[128,1024]{1,0:T(8,128)(2,1)S(1)}, u32[]{:S(2)}, u32[]{:S(2)}) collective-permute-start(bf16[128,1024]{1,0:T(8,128)(2,1)S(1)} %collective-permute-done.3.refs_4_), channel_id=1, source_target_pairs={{0,12},{1,13},{2,14},{3,15},{4,0},{5,1},{6,2},{7,3},{8,4},{9,5},{1... | collective-permute-start | bytes 786440 | tf_op jit(solution)/shard_map/ppermute | solution.py:39
  16.0 2.7 %collective-permute-done.1.refs_2_ = bf16[128,1024]{1,0:T(8,128)(2,1)S(1)} collective-permute-done((bf16[128,1024]{1,0:T(8,128)(2,1)S(1)}, bf16[128,1024]{1,0:T(8,128)(2,1)S(1)}, u32[]{:S(2)}, u32[]{:S(2)}) %collective-permute-start.1) | collective-permute-done | bytes 262176 | tf_op jit(solution)/shard_map/ppermute | solution.py:39
  18.7 1.9 %collective-permute-start.5 = (bf16[128,1024]{1,0:T(8,128)(2,1)S(1)}, bf16[128,1024]{1,0:T(8,128)(2,1)S(1)}, u32[]{:S(2)}, u32[]{:S(2)}) collective-permute-start(bf16[128,1024]{1,0:T(8,128)(2,1)S(1)} %collective-permute-done.1.refs_2_), channel_id=1, source_target_pairs={{0,2},{1,3},{2,0},{3,1},{4,6},{5,7},{6,4},{7,5},{8,10},{9,11},{10,... | collective-permute-start | bytes 786440 | tf_op jit(solution)/shard_map/ppermute | solution.py:39
  21.7 3.5 %collective-permute-done.5.refs_6_ = bf16[128,1024]{1,0:T(8,128)(2,1)S(1)} collective-permute-done((bf16[128,1024]{1,0:T(8,128)(2,1)S(1)}, bf16[128,1024]{1,0:T(8,128)(2,1)S(1)}, u32[]{:S(2)}, u32[]{:S(2)}) %collective-permute-start.5) | collective-permute-done | bytes 262176 | tf_op jit(solution)/shard_map/ppermute | solution.py:39
  26.8 10.4 %attention.3 = (bf16[128,768]{1,0:T(8,128)(2,1)S(1)}, bf16[128,768]{1,0:T(8,128)(2,1)S(1)}, bf16[128,768]{1,0:T(8,128)(2,1)S(1)}, bf16[128,768]{1,0:T(8,128)(2,1)S(1)}) custom-call(s32[16]{0:T(128)} %span_map.3, s32[1]{0:T(128)} %bitcast.1.ctx, s32[1]{0:T(128)} %bitcast.section, bf16[128,4096]{1,0:T(8,128)(2,1)} %bitcast.3, ...), custom_call_target="tpu_custom_call" | custom-call | flops 6442450944 | bytes 4718592 | tf_op jit(solution)/shard_map/attention/pallas_call | solution.py:182
  37.2 3.3 %collective-permute-start.18 = (bf16[128,768]{1,0:T(8,128)(2,1)S(1)}, bf16[128,768]{1,0:T(8,128)(2,1)S(1)}, u32[]{:S(2)}, u32[]{:S(2)}) collective-permute-start(bf16[128,768]{1,0:T(8,128)(2,1)S(1)} %get-tuple-element.35), channel_id=1, source_target_pairs={{0,16},{16,32},{32,48},{48,0},{64,80},{80,96},{96,112},{112,64},{1... | collective-permute-start | bytes 589832 | tf_op jit(solution)/shard_map/ppermute | solution.py:286
  40.5 5.4 %collective-permute-start.19 = (bf16[128,768]{1,0:T(8,128)(2,1)S(1)}, bf16[128,768]{1,0:T(8,128)(2,1)S(1)}, u32[]{:S(2)}, u32[]{:S(2)}) collective-permute-start(bf16[128,768]{1,0:T(8,128)(2,1)S(1)} %get-tuple-element.36), channel_id=1, source_target_pairs={{0,32},{16,48},{32,0},{48,16},{64,96},{80,112},{96,64},{112,80},{1... | collective-permute-start | bytes 589832 | tf_op jit(solution)/shard_map/ppermute | solution.py:286
  45.9 2.6 %collective-permute-start.20 = (bf16[128,768]{1,0:T(8,128)(2,1)S(1)}, bf16[128,768]{1,0:T(8,128)(2,1)S(1)}, u32[]{:S(2)}, u32[]{:S(2)}) collective-permute-start(bf16[128,768]{1,0:T(8,128)(2,1)S(1)} %get-tuple-element.37), channel_id=1, source_target_pairs={{0,48},{16,0},{32,16},{48,32},{64,112},{80,64},{96,80},{112,96},{1... | collective-permute-start | bytes 589832 | tf_op jit(solution)/shard_map/ppermute | solution.py:286
  48.5 4.8 %attention.2 = (bf16[128,256]{1,0:T(8,128)(2,1)S(1)}, bf16[128,256]{1,0:T(8,128)(2,1)S(1)}, bf16[128,256]{1,0:T(8,128)(2,1)S(1)}, bf16[128,256]{1,0:T(8,128)(2,1)S(1)}) custom-call(s32[16]{0:T(128)} %span_map.3, s32[1]{0:T(128)} %bitcast.1.ctx, s32[1]{0:T(128)} %bitcast.section, bf16[128,4096]{1,0:T(8,128)(2,1)} %bitcast.4, ...), custom_call_target="tpu_custom_call" | custom-call | flops 2147483648 | bytes 1572864 | tf_op jit(solution)/shard_map/attention/pallas_call | solution.py:182
  53.3 5.2 %collective-permute-done.19.c.refs_2_ = bf16[128,768]{1,0:T(8,128)(2,1)S(1)} collective-permute-done((bf16[128,768]{1,0:T(8,128)(2,1)S(1)}, bf16[128,768]{1,0:T(8,128)(2,1)S(1)}, u32[]{:S(2)}, u32[]{:S(2)}) %collective-permute-start.19) | collective-permute-done | bytes 196640 | tf_op jit(solution)/shard_map/ppermute | solution.py:286
  58.5 5.5 %collective-permute-done.20.d.refs_3_ = bf16[128,768]{1,0:T(8,128)(2,1)S(1)} collective-permute-done((bf16[128,768]{1,0:T(8,128)(2,1)S(1)}, bf16[128,768]{1,0:T(8,128)(2,1)S(1)}, u32[]{:S(2)}, u32[]{:S(2)}) %collective-permute-start.20) | collective-permute-done | bytes 196640 | tf_op jit(solution)/shard_map/ppermute | solution.py:286
  68.7 4.4 %collective-permute-start.16 = (bf16[128,256]{1,0:T(8,128)(2,1)S(1)}, bf16[128,256]{1,0:T(8,128)(2,1)S(1)}, u32[]{:S(2)}, u32[]{:S(2)}) collective-permute-start(bf16[128,256]{1,0:T(8,128)(2,1)S(1)} %get-tuple-element.32), channel_id=1, source_target_pairs={{0,32},{16,48},{32,0},{48,16},{64,96},{80,112},{96,64},{112,80},{1... | collective-permute-start | bytes 196616 | tf_op jit(solution)/shard_map/ppermute | solution.py:286
  73.5 2.8 %collective-permute-start.17 = (bf16[128,256]{1,0:T(8,128)(2,1)S(1)}, bf16[128,256]{1,0:T(8,128)(2,1)S(1)}, u32[]{:S(2)}, u32[]{:S(2)}) collective-permute-start(bf16[128,256]{1,0:T(8,128)(2,1)S(1)} %get-tuple-element.33), channel_id=1, source_target_pairs={{0,48},{16,0},{32,16},{48,32},{64,112},{80,64},{96,80},{112,96},{1... | collective-permute-start | bytes 196616 | tf_op jit(solution)/shard_map/ppermute | solution.py:286
  80.4 2.7 %collective-permute-start.28 = (bf16[128,256]{1,0:T(8,128)(2,1)S(1)}, bf16[128,256]{1,0:T(8,128)(2,1)S(1)}, u32[]{:S(2)}, u32[]{:S(2)}) collective-permute-start(bf16[128,256]{1,0:T(8,128)(2,1)S(1)} %row_total.2), channel_id=1, source_target_pairs={{0,128},{16,144},{32,160},{48,176},{64,192},{80,208},{96,224},{112... | collective-permute-start | bytes 196616 | tf_op jit(solution)/shard_map/ppermute | solution.py:303
  83.1 2.0 %collective-permute-start.29 = (bf16[128,256]{1,0:T(8,128)(2,1)S(1)}, bf16[128,256]{1,0:T(8,128)(2,1)S(1)}, u32[]{:S(2)}, u32[]{:S(2)}) collective-permute-start(bf16[128,256]{1,0:T(8,128)(2,1)S(1)} %row_total.2), channel_id=1, source_target_pairs={{0,192},{16,208},{32,224},{48,240},{64,0},{80,16},{96,32},{112,48}... | collective-permute-start | bytes 196616 | tf_op jit(solution)/shard_map/ppermute | solution.py:303
  85.1 2.2 %collective-permute-start.24 = (bf16[128,768]{1,0:T(8,128)(2,1)S(1)}, bf16[128,768]{1,0:T(8,128)(2,1)S(1)}, u32[]{:S(2)}, u32[]{:S(2)}) collective-permute-start(bf16[128,768]{1,0:T(8,128)(2,1)S(1)} %get-tuple-element.47), channel_id=1, source_target_pairs={{0,16},{16,32},{32,48},{48,0},{64,80},{80,96},{96,112},{112,64},{1... | collective-permute-start | bytes 589832 | tf_op jit(solution)/shard_map/ppermute | solution.py:286
  87.3 4.0 %collective-permute-start.25 = (bf16[128,768]{1,0:T(8,128)(2,1)S(1)}, bf16[128,768]{1,0:T(8,128)(2,1)S(1)}, u32[]{:S(2)}, u32[]{:S(2)}) collective-permute-start(bf16[128,768]{1,0:T(8,128)(2,1)S(1)} %get-tuple-element.48), channel_id=1, source_target_pairs={{0,32},{16,48},{32,0},{48,16},{64,96},{80,112},{96,64},{112,80},{1... | collective-permute-start | bytes 589832 | tf_op jit(solution)/shard_map/ppermute | solution.py:286
  91.3 2.5 %collective-permute-start.26 = (bf16[128,768]{1,0:T(8,128)(2,1)S(1)}, bf16[128,768]{1,0:T(8,128)(2,1)S(1)}, u32[]{:S(2)}, u32[]{:S(2)}) collective-permute-start(bf16[128,768]{1,0:T(8,128)(2,1)S(1)} %get-tuple-element.49), channel_id=1, source_target_pairs={{0,48},{16,0},{32,16},{48,32},{64,112},{80,64},{96,80},{112,96},{1... | collective-permute-start | bytes 589832 | tf_op jit(solution)/shard_map/ppermute | solution.py:286
  94.4 1.9 %collective-permute-start.31 = (bf16[128,256]{1,0:T(8,128)(2,1)S(1)}, bf16[128,256]{1,0:T(8,128)(2,1)S(1)}, u32[]{:S(2)}, u32[]{:S(2)}) collective-permute-start(bf16[128,256]{1,0:T(8,128)(2,1)S(1)} %get-tuple-element.53), channel_id=1, source_target_pairs={{0,32},{16,48},{32,0},{48,16},{64,96},{80,112},{96,64},{112,80},{1... | collective-permute-start | bytes 196616 | tf_op jit(solution)/shard_map/ppermute | solution.py:286
  96.4 11.8 %collective-permute-done.30.refs_5_ = bf16[128,256]{1,0:T(8,128)(2,1)S(1)} collective-permute-done((bf16[128,256]{1,0:T(8,128)(2,1)S(1)}, bf16[128,256]{1,0:T(8,128)(2,1)S(1)}, u32[]{:S(2)}, u32[]{:S(2)}) %collective-permute-start.30) | collective-permute-done | bytes 65568 | tf_op jit(solution)/shard_map/ppermute | solution.py:286
  108.2 5.2 %collective-permute-done.32.refs_7_ = bf16[128,256]{1,0:T(8,128)(2,1)S(1)} collective-permute-done((bf16[128,256]{1,0:T(8,128)(2,1)S(1)}, bf16[128,256]{1,0:T(8,128)(2,1)S(1)}, u32[]{:S(2)}, u32[]{:S(2)}) %collective-permute-start.32) | collective-permute-done | bytes 65568 | tf_op jit(solution)/shard_map/ppermute | solution.py:286
  (52 shorter events, 18.8 us)
Async XLA Ops:
  1.0 9.3 %collective-permute-start = (bf16[128,1024]{1,0:T(8,128)(2,1)S(1)}, bf16[128,1024]{1,0:T(8,128)(2,1)S(1)}, u32[]{:S(2)}, u32[]{:S(2)}) collective-permute-start(bf16[128,1024]{1,0:T(8,128)(2,1)S(1)} %join.1.refs_0_), channel_id=1, source_target_pairs={{0,4},{1,5},{2,6},{3,7},{4,8},{5,9},{6,10},{7,11},{8,12},{9,13},{1... | collective-permute-start | bytes 786440 | tf_op jit(solution)/shard_map/ppermute | solution.py:39
  2.6 10.0 %collective-permute-start.3 = (bf16[128,1024]{1,0:T(8,128)(2,1)S(1)}, bf16[128,1024]{1,0:T(8,128)(2,1)S(1)}, u32[]{:S(2)}, u32[]{:S(2)}) collective-permute-start(bf16[128,1024]{1,0:T(8,128)(2,1)S(1)} %join.1.refs_0_), channel_id=1, source_target_pairs={{0,2},{1,3},{2,0},{3,1},{4,6},{5,7},{6,4},{7,5},{8,10},{9,11},{10,... | collective-permute-start | bytes 786440 | tf_op jit(solution)/shard_map/ppermute | solution.py:39
  4.5 11.0 %collective-permute-start.2 = (bf16[128,1024]{1,0:T(8,128)(2,1)S(1)}, bf16[128,1024]{1,0:T(8,128)(2,1)S(1)}, u32[]{:S(2)}, u32[]{:S(2)}) collective-permute-start(bf16[128,1024]{1,0:T(8,128)(2,1)S(1)} %join.1.refs_0_), channel_id=1, source_target_pairs={{0,12},{1,13},{2,14},{3,15},{4,0},{5,1},{6,2},{7,3},{8,4},{9,5},{1... | collective-permute-start | bytes 786440 | tf_op jit(solution)/shard_map/ppermute | solution.py:39
  6.2 9.3 %collective-permute-start.7 = (bf16[128,1024]{1,0:T(8,128)(2,1)S(1)}, bf16[128,1024]{1,0:T(8,128)(2,1)S(1)}, u32[]{:S(2)}, u32[]{:S(2)}) collective-permute-start(bf16[128,1024]{1,0:T(8,128)(2,1)S(1)} %join.1.refs_0_), channel_id=1, source_target_pairs={{0,1},{1,0},{2,3},{3,2},{4,5},{5,4},{6,7},{7,6},{8,9},{9,8},{10,11... | collective-permute-start | bytes 786440 | tf_op jit(solution)/shard_map/ppermute | solution.py:39
  10.3 8.4 %collective-permute-start.1 = (bf16[128,1024]{1,0:T(8,128)(2,1)S(1)}, bf16[128,1024]{1,0:T(8,128)(2,1)S(1)}, u32[]{:S(2)}, u32[]{:S(2)}) collective-permute-start(bf16[128,1024]{1,0:T(8,128)(2,1)S(1)} %collective-permute-done.refs_1_), channel_id=1, source_target_pairs={{0,4},{1,5},{2,6},{3,7},{4,8},{5,9},{6,10},{7,11},{8,12},{9,13},{1... | collective-permute-start | bytes 786440 | tf_op jit(solution)/shard_map/ppermute | solution.py:39
  10.6 10.0 %collective-permute-start.4 = (bf16[128,1024]{1,0:T(8,128)(2,1)S(1)}, bf16[128,1024]{1,0:T(8,128)(2,1)S(1)}, u32[]{:S(2)}, u32[]{:S(2)}) collective-permute-start(bf16[128,1024]{1,0:T(8,128)(2,1)S(1)} %collective-permute-done.refs_1_), channel_id=1, source_target_pairs={{0,2},{1,3},{2,0},{3,1},{4,6},{5,7},{6,4},{7,5},{8,10},{9,11},{10,... | collective-permute-start | bytes 786440 | tf_op jit(solution)/shard_map/ppermute | solution.py:39
  12.5 8.1 %collective-permute-start.6 = (bf16[128,1024]{1,0:T(8,128)(2,1)S(1)}, bf16[128,1024]{1,0:T(8,128)(2,1)S(1)}, u32[]{:S(2)}, u32[]{:S(2)}) collective-permute-start(bf16[128,1024]{1,0:T(8,128)(2,1)S(1)} %collective-permute-done.3.refs_4_), channel_id=1, source_target_pairs={{0,12},{1,13},{2,14},{3,15},{4,0},{5,1},{6,2},{7,3},{8,4},{9,5},{1... | collective-permute-start | bytes 786440 | tf_op jit(solution)/shard_map/ppermute | solution.py:39
  18.7 6.4 %collective-permute-start.5 = (bf16[128,1024]{1,0:T(8,128)(2,1)S(1)}, bf16[128,1024]{1,0:T(8,128)(2,1)S(1)}, u32[]{:S(2)}, u32[]{:S(2)}) collective-permute-start(bf16[128,1024]{1,0:T(8,128)(2,1)S(1)} %collective-permute-done.1.refs_2_), channel_id=1, source_target_pairs={{0,2},{1,3},{2,0},{3,1},{4,6},{5,7},{6,4},{7,5},{8,10},{9,11},{10,... | collective-permute-start | bytes 786440 | tf_op jit(solution)/shard_map/ppermute | solution.py:39
  37.2 16.1 %collective-permute-start.18 = (bf16[128,768]{1,0:T(8,128)(2,1)S(1)}, bf16[128,768]{1,0:T(8,128)(2,1)S(1)}, u32[]{:S(2)}, u32[]{:S(2)}) collective-permute-start(bf16[128,768]{1,0:T(8,128)(2,1)S(1)} %get-tuple-element.35), channel_id=1, source_target_pairs={{0,16},{16,32},{32,48},{48,0},{64,80},{80,96},{96,112},{112,64},{1... | collective-permute-start | bytes 589832 | tf_op jit(solution)/shard_map/ppermute | solution.py:286
  40.5 18.0 %collective-permute-start.19 = (bf16[128,768]{1,0:T(8,128)(2,1)S(1)}, bf16[128,768]{1,0:T(8,128)(2,1)S(1)}, u32[]{:S(2)}, u32[]{:S(2)}) collective-permute-start(bf16[128,768]{1,0:T(8,128)(2,1)S(1)} %get-tuple-element.36), channel_id=1, source_target_pairs={{0,32},{16,48},{32,0},{48,16},{64,96},{80,112},{96,64},{112,80},{1... | collective-permute-start | bytes 589832 | tf_op jit(solution)/shard_map/ppermute | solution.py:286
  45.9 18.1 %collective-permute-start.20 = (bf16[128,768]{1,0:T(8,128)(2,1)S(1)}, bf16[128,768]{1,0:T(8,128)(2,1)S(1)}, u32[]{:S(2)}, u32[]{:S(2)}) collective-permute-start(bf16[128,768]{1,0:T(8,128)(2,1)S(1)} %get-tuple-element.37), channel_id=1, source_target_pairs={{0,48},{16,0},{32,16},{48,32},{64,112},{80,64},{96,80},{112,96},{1... | collective-permute-start | bytes 589832 | tf_op jit(solution)/shard_map/ppermute | solution.py:286
  64.1 14.7 %collective-permute-start.21 = (bf16[128,768]{1,0:T(8,128)(2,1)S(1)}, bf16[128,768]{1,0:T(8,128)(2,1)S(1)}, u32[]{:S(2)}, u32[]{:S(2)}) collective-permute-start(bf16[128,768]{1,0:T(8,128)(2,1)S(1)} %row_total.3), channel_id=1, source_target_pairs={{0,64},{16,80},{32,96},{48,112},{64,128},{80,144},{96,160},{112,17... | collective-permute-start | bytes 589832 | tf_op jit(solution)/shard_map/ppermute | solution.py:303
  65.5 13.3 %collective-permute-start.22 = (bf16[128,768]{1,0:T(8,128)(2,1)S(1)}, bf16[128,768]{1,0:T(8,128)(2,1)S(1)}, u32[]{:S(2)}, u32[]{:S(2)}) collective-permute-start(bf16[128,768]{1,0:T(8,128)(2,1)S(1)} %row_total.3), channel_id=1, source_target_pairs={{0,128},{16,144},{32,160},{48,176},{64,192},{80,208},{96,224},{112... | collective-permute-start | bytes 589832 | tf_op jit(solution)/shard_map/ppermute | solution.py:303
  66.1 12.7 %collective-permute-start.23 = (bf16[128,768]{1,0:T(8,128)(2,1)S(1)}, bf16[128,768]{1,0:T(8,128)(2,1)S(1)}, u32[]{:S(2)}, u32[]{:S(2)}) collective-permute-start(bf16[128,768]{1,0:T(8,128)(2,1)S(1)} %row_total.3), channel_id=1, source_target_pairs={{0,192},{16,208},{32,224},{48,240},{64,0},{80,16},{96,32},{112,48}... | collective-permute-start | bytes 589832 | tf_op jit(solution)/shard_map/ppermute | solution.py:303
  67.2 6.4 %collective-permute-start.15 = (bf16[128,256]{1,0:T(8,128)(2,1)S(1)}, bf16[128,256]{1,0:T(8,128)(2,1)S(1)}, u32[]{:S(2)}, u32[]{:S(2)}) collective-permute-start(bf16[128,256]{1,0:T(8,128)(2,1)S(1)} %get-tuple-element.31), channel_id=1, source_target_pairs={{0,16},{16,32},{32,48},{48,0},{64,80},{80,96},{96,112},{112,64},{1... | collective-permute-start | bytes 196616 | tf_op jit(solution)/shard_map/ppermute | solution.py:286
  68.7 9.0 %collective-permute-start.16 = (bf16[128,256]{1,0:T(8,128)(2,1)S(1)}, bf16[128,256]{1,0:T(8,128)(2,1)S(1)}, u32[]{:S(2)}, u32[]{:S(2)}) collective-permute-start(bf16[128,256]{1,0:T(8,128)(2,1)S(1)} %get-tuple-element.32), channel_id=1, source_target_pairs={{0,32},{16,48},{32,0},{48,16},{64,96},{80,112},{96,64},{112,80},{1... | collective-permute-start | bytes 196616 | tf_op jit(solution)/shard_map/ppermute | solution.py:286
  79.2 12.1 %collective-permute-start.27 = (bf16[128,256]{1,0:T(8,128)(2,1)S(1)}, bf16[128,256]{1,0:T(8,128)(2,1)S(1)}, u32[]{:S(2)}, u32[]{:S(2)}) collective-permute-start(bf16[128,256]{1,0:T(8,128)(2,1)S(1)} %row_total.2), channel_id=1, source_target_pairs={{0,64},{16,80},{32,96},{48,112},{64,128},{80,144},{96,160},{112,17... | collective-permute-start | bytes 196616 | tf_op jit(solution)/shard_map/ppermute | solution.py:303
  80.4 13.4 %collective-permute-start.28 = (bf16[128,256]{1,0:T(8,128)(2,1)S(1)}, bf16[128,256]{1,0:T(8,128)(2,1)S(1)}, u32[]{:S(2)}, u32[]{:S(2)}) collective-permute-start(bf16[128,256]{1,0:T(8,128)(2,1)S(1)} %row_total.2), channel_id=1, source_target_pairs={{0,128},{16,144},{32,160},{48,176},{64,192},{80,208},{96,224},{112... | collective-permute-start | bytes 196616 | tf_op jit(solution)/shard_map/ppermute | solution.py:303
  83.1 10.7 %collective-permute-start.29 = (bf16[128,256]{1,0:T(8,128)(2,1)S(1)}, bf16[128,256]{1,0:T(8,128)(2,1)S(1)}, u32[]{:S(2)}, u32[]{:S(2)}) collective-permute-start(bf16[128,256]{1,0:T(8,128)(2,1)S(1)} %row_total.2), channel_id=1, source_target_pairs={{0,192},{16,208},{32,224},{48,240},{64,0},{80,16},{96,32},{112,48}... | collective-permute-start | bytes 196616 | tf_op jit(solution)/shard_map/ppermute | solution.py:303
  85.1 28.3 %collective-permute-start.24 = (bf16[128,768]{1,0:T(8,128)(2,1)S(1)}, bf16[128,768]{1,0:T(8,128)(2,1)S(1)}, u32[]{:S(2)}, u32[]{:S(2)}) collective-permute-start(bf16[128,768]{1,0:T(8,128)(2,1)S(1)} %get-tuple-element.47), channel_id=1, source_target_pairs={{0,16},{16,32},{32,48},{48,0},{64,80},{80,96},{96,112},{112,64},{1... | collective-permute-start | bytes 589832 | tf_op jit(solution)/shard_map/ppermute | solution.py:286
  87.3 26.1 %collective-permute-start.25 = (bf16[128,768]{1,0:T(8,128)(2,1)S(1)}, bf16[128,768]{1,0:T(8,128)(2,1)S(1)}, u32[]{:S(2)}, u32[]{:S(2)}) collective-permute-start(bf16[128,768]{1,0:T(8,128)(2,1)S(1)} %get-tuple-element.48), channel_id=1, source_target_pairs={{0,32},{16,48},{32,0},{48,16},{64,96},{80,112},{96,64},{112,80},{1... | collective-permute-start | bytes 589832 | tf_op jit(solution)/shard_map/ppermute | solution.py:286
  91.3 22.0 %collective-permute-start.26 = (bf16[128,768]{1,0:T(8,128)(2,1)S(1)}, bf16[128,768]{1,0:T(8,128)(2,1)S(1)}, u32[]{:S(2)}, u32[]{:S(2)}) collective-permute-start(bf16[128,768]{1,0:T(8,128)(2,1)S(1)} %get-tuple-element.49), channel_id=1, source_target_pairs={{0,48},{16,0},{32,16},{48,32},{64,112},{80,64},{96,80},{112,96},{1... | collective-permute-start | bytes 589832 | tf_op jit(solution)/shard_map/ppermute | solution.py:286
  93.9 14.2 %collective-permute-start.30 = (bf16[128,256]{1,0:T(8,128)(2,1)S(1)}, bf16[128,256]{1,0:T(8,128)(2,1)S(1)}, u32[]{:S(2)}, u32[]{:S(2)}) collective-permute-start(bf16[128,256]{1,0:T(8,128)(2,1)S(1)} %get-tuple-element.52), channel_id=1, source_target_pairs={{0,16},{16,32},{32,48},{48,0},{64,80},{80,96},{96,112},{112,64},{1... | collective-permute-start | bytes 196616 | tf_op jit(solution)/shard_map/ppermute | solution.py:286
  94.4 13.7 %collective-permute-start.31 = (bf16[128,256]{1,0:T(8,128)(2,1)S(1)}, bf16[128,256]{1,0:T(8,128)(2,1)S(1)}, u32[]{:S(2)}, u32[]{:S(2)}) collective-permute-start(bf16[128,256]{1,0:T(8,128)(2,1)S(1)} %get-tuple-element.53), channel_id=1, source_target_pairs={{0,32},{16,48},{32,0},{48,16},{64,96},{80,112},{96,64},{112,80},{1... | collective-permute-start | bytes 196616 | tf_op jit(solution)/shard_map/ppermute | solution.py:286
  (10 other events, 65.8 us)

commit v4 on v0

--- a/solution.py
+++ b/solution.py
@@ -289,10 +289,9 @@
     ctx = lax.axis_index("ctx")[None]
     section = lax.axis_index("section")[None]
     units = gather(keys, values)
-    slabs = [
-        turn(attention(span_map, ctx, section, queries[0], units, chunk))
-        for chunk in range(CHUNKS)
-    ]
+    raw = [attention(span_map, ctx, section, queries[0], units, c) for c in range(CHUNKS)]
+    slabs = [turn(r) for r in raw]
+    slabs[0], _ = lax.optimization_barrier((slabs[0], raw[1]))
     finished, sums = [], None
     for chunk in range(CHUNKS):
         total = row_total(slabs[chunk])

time: 107 us -> 105 us (0.981)
  waiting for transfers between devices: 30 us -> 23.5 us
  starting transfers between devices: 58.6 us -> 63 us
    ppermute x15, waiting for transfers between devices: 6.32 us -> 2.49 us  [ctx_move(): return lax.ppermute(unit, 'ctx', ctx_pairs(dx, dz, dc))]
    ppermute x6, starting transfers between devices: 8.12 us -> 10.8 us  [body(): lax.ppermute(total, 'section', climb_pairs(s))]
    ppermute x6, waiting for transfers between devices: 2.25 us -> 0.02 us  [body(): lax.ppermute(total, 'section', climb_pairs(s))]
  transfers between devices with their start and end apart: 33 -> 33, of which waited for: 9 -> 7; matrix products, arithmetic and copies ran while one was open for 0% -> 0% of each run, Pallas kernels for 7% -> 8%
where the time goes in v4:
time: 105 us; the launch traced here: 104 us
  starting transfers between devices  63 us (60%)
  waiting for transfers between devices  23.5 us (22%)
  Pallas kernels  17.9 us (17%)
    ppermute x12, starting transfers between devices, turn(): lax.ppermute(slabs[steps], 'section', turn_pairs(steps))  27.8 us
    ppermute x15, starting transfers between devices, ctx_move(): return lax.ppermute(unit, 'ctx', ctx_pairs(dx, dz, dc))  24.4 us
    ppermute x12, waiting for transfers between devices, turn(): lax.ppermute(slabs[steps], 'section', turn_pairs(steps))  21 us
    pallas_call x2, Pallas kernels, attention(): pl.pallas_call(functools.partial(attention_kernel, chunk), in_specs=[smem...  15.1 us
    ppermute x6, starting transfers between devices, body(): lax.ppermute(total, 'section', climb_pairs(s))  10.8 us
    ppermute x15, waiting for transfers between devices, ctx_move(): return lax.ppermute(unit, 'ctx', ctx_pairs(dx, dz, dc))  2.49 us
  transfers between devices with their start and end apart: 33, of which 7 were waited for; matrix products, arithmetic and copies ran while one was open for 0% of the time, Pallas kernels for 8%

profile of v4, /device:TPU:1, one launch (start us, length us, event | category | flops | bytes accessed | tf_op | source)
XLA Modules:
  0.0 104.5 jit_solution(9708739233020147663)
XLA Ops:
  1.0 2.1 %collective-permute-start = (bf16[128,1024]{1,0:T(8,128)(2,1)S(1)}, bf16[128,1024]{1,0:T(8,128)(2,1)S(1)}, u32[]{:S(2)}, u32[]{:S(2)}) collective-permute-start(bf16[128,1024]{1,0:T(8,128)(2,1)S(1)} %join.1.refs_0_), channel_id=1, source_target_pairs={{0,4},{1,5},{2,6},{3,7},{4,8},{5,9},{6,10},{7,11},{8,12},{9,13},{1... | collective-permute-start | bytes 786440 | tf_op jit(solution)/shard_map/ppermute | solution.py:40
  10.0 1.9 %collective-permute-start.4 = (bf16[128,1024]{1,0:T(8,128)(2,1)S(1)}, bf16[128,1024]{1,0:T(8,128)(2,1)S(1)}, u32[]{:S(2)}, u32[]{:S(2)}) collective-permute-start(bf16[128,1024]{1,0:T(8,128)(2,1)S(1)} %collective-permute-done.refs_1_), channel_id=1, source_target_pairs={{0,2},{1,3},{2,0},{3,1},{4,6},{5,7},{6,4},{7,5},{8,10},{9,11},{10,... | collective-permute-start | bytes 786440 | tf_op jit(solution)/shard_map/ppermute | solution.py:40
  11.9 2.7 %collective-permute-start.6 = (bf16[128,1024]{1,0:T(8,128)(2,1)S(1)}, bf16[128,1024]{1,0:T(8,128)(2,1)S(1)}, u32[]{:S(2)}, u32[]{:S(2)}) collective-permute-start(bf16[128,1024]{1,0:T(8,128)(2,1)S(1)} %collective-permute-done.3.refs_4_), channel_id=1, source_target_pairs={{0,12},{1,13},{2,14},{3,15},{4,0},{5,1},{6,2},{7,3},{8,4},{9,5},{1... | collective-permute-start | bytes 786440 | tf_op jit(solution)/shard_map/ppermute | solution.py:40
  14.6 2.4 %collective-permute-start.8 = (bf16[128,1024]{1,0:T(8,128)(2,1)S(1)}, bf16[128,1024]{1,0:T(8,128)(2,1)S(1)}, u32[]{:S(2)}, u32[]{:S(2)}) collective-permute-start(bf16[128,1024]{1,0:T(8,128)(2,1)S(1)} %collective-permute-done.refs_1_), channel_id=1, source_target_pairs={{0,1},{1,0},{2,3},{3,2},{4,5},{5,4},{6,7},{7,6},{8,9},{9,8},{10,11... | collective-permute-start | bytes 786440 | tf_op jit(solution)/shard_map/ppermute | solution.py:40
  17.1 2.3 %collective-permute-start.5 = (bf16[128,1024]{1,0:T(8,128)(2,1)S(1)}, bf16[128,1024]{1,0:T(8,128)(2,1)S(1)}, u32[]{:S(2)}, u32[]{:S(2)}) collective-permute-start(bf16[128,1024]{1,0:T(8,128)(2,1)S(1)} %collective-permute-done.1.refs_2_), channel_id=1, source_target_pairs={{0,2},{1,3},{2,0},{3,1},{4,6},{5,7},{6,4},{7,5},{8,10},{9,11},{10,... | collective-permute-start | bytes 786440 | tf_op jit(solution)/shard_map/ppermute | solution.py:40
  19.4 2.7 %collective-permute-start.10 = (bf16[128,1024]{1,0:T(8,128)(2,1)S(1)}, bf16[128,1024]{1,0:T(8,128)(2,1)S(1)}, u32[]{:S(2)}, u32[]{:S(2)}) collective-permute-start(bf16[128,1024]{1,0:T(8,128)(2,1)S(1)} %collective-permute-done.2.refs_3_), channel_id=1, source_target_pairs={{0,1},{1,0},{2,3},{3,2},{4,5},{5,4},{6,7},{7,6},{8,9},{9,8},{10,11... | collective-permute-start | bytes 786440 | tf_op jit(solution)/shard_map/ppermute | solution.py:40
  23.5 3.1 %collective-permute-start.13 = (bf16[128,1024]{1,0:T(8,128)(2,1)S(1)}, bf16[128,1024]{1,0:T(8,128)(2,1)}, u32[]{:S(2)}, u32[]{:S(2)}) collective-permute-start(bf16[128,1024]{1,0:T(8,128)(2,1)S(1)} %collective-permute-done.5.refs_6_), channel_id=1, source_target_pairs={{0,1},{1,0},{2,3},{3,2},{4,5},{5,4},{6,7},{7,6},{8,9},{9,8},{10,11... | collective-permute-start | bytes 786440 | tf_op jit(solution)/shard_map/ppermute | solution.py:40
  27.9 7.6 %attention.3 = (bf16[128,512]{1,0:T(8,128)(2,1)S(1)}, bf16[128,512]{1,0:T(8,128)(2,1)S(1)}, bf16[128,512]{1,0:T(8,128)(2,1)S(1)}, bf16[128,512]{1,0:T(8,128)(2,1)S(1)}) custom-call(s32[16]{0:T(128)} %span_map.3, s32[1]{0:T(128)} %bitcast.1.ctx, s32[1]{0:T(128)} %bitcast.section, bf16[128,4096]{1,0:T(8,128)(2,1)} %bitcast.3, ...), custom_call_target="tpu_custom_call" | custom-call | flops 4294967296 | bytes 3145728 | tf_op jit(solution)/shard_map/attention/pallas_call | solution.py:180
  35.5 3.1 %collective-permute-start.18 = (bf16[128,512]{1,0:T(8,128)(2,1)S(1)}, bf16[128,512]{1,0:T(8,128)(2,1)S(1)}, u32[]{:S(2)}, u32[]{:S(2)}) collective-permute-start(bf16[128,512]{1,0:T(8,128)(2,1)S(1)} %get-tuple-element.35), channel_id=1, source_target_pairs={{0,16},{16,32},{32,48},{48,0},{64,80},{80,96},{96,112},{112,64},{1... | collective-permute-start | bytes 393224 | tf_op jit(solution)/shard_map/ppermute | solution.py:284
  38.6 5.1 %collective-permute-start.19 = (bf16[128,512]{1,0:T(8,128)(2,1)S(1)}, bf16[128,512]{1,0:T(8,128)(2,1)S(1)}, u32[]{:S(2)}, u32[]{:S(2)}) collective-permute-start(bf16[128,512]{1,0:T(8,128)(2,1)S(1)} %get-tuple-element.36), channel_id=1, source_target_pairs={{0,32},{16,48},{32,0},{48,16},{64,96},{80,112},{96,64},{112,80},{1... | collective-permute-start | bytes 393224 | tf_op jit(solution)/shard_map/ppermute | solution.py:284
  43.6 2.4 %collective-permute-start.20 = (bf16[128,512]{1,0:T(8,128)(2,1)S(1)}, bf16[128,512]{1,0:T(8,128)(2,1)S(1)}, u32[]{:S(2)}, u32[]{:S(2)}) collective-permute-start(bf16[128,512]{1,0:T(8,128)(2,1)S(1)} %get-tuple-element.37), channel_id=1, source_target_pairs={{0,48},{16,0},{32,16},{48,32},{64,112},{80,64},{96,80},{112,96},{1... | collective-permute-start | bytes 393224 | tf_op jit(solution)/shard_map/ppermute | solution.py:284
  46.0 7.6 %attention.2 = (bf16[128,512]{1,0:T(8,128)(2,1)S(1)}, bf16[128,512]{1,0:T(8,128)(2,1)S(1)}, bf16[128,512]{1,0:T(8,128)(2,1)S(1)}, bf16[128,512]{1,0:T(8,128)(2,1)S(1)}) custom-call(s32[16]{0:T(128)} %span_map.3, s32[1]{0:T(128)} %bitcast.1.ctx, s32[1]{0:T(128)} %bitcast.section, bf16[128,4096]{1,0:T(8,128)(2,1)} %bitcast.4, ...), custom_call_target="tpu_custom_call" | custom-call | flops 4294967296 | bytes 3145728 | tf_op jit(solution)/shard_map/attention/pallas_call | solution.py:180
  53.7 2.1 %collective-permute-start.16 = (bf16[128,512]{1,0:T(8,128)(2,1)S(1)}, bf16[128,512]{1,0:T(8,128)(2,1)S(1)}, u32[]{:S(2)}, u32[]{:S(2)}) collective-permute-start(bf16[128,512]{1,0:T(8,128)(2,1)S(1)} %get-tuple-element.32), channel_id=1, source_target_pairs={{0,32},{16,48},{32,0},{48,16},{64,96},{80,112},{96,64},{112,80},{1... | collective-permute-start | bytes 393224 | tf_op jit(solution)/shard_map/ppermute | solution.py:284
  55.8 2.5 %collective-permute-start.17 = (bf16[128,512]{1,0:T(8,128)(2,1)S(1)}, bf16[128,512]{1,0:T(8,128)(2,1)S(1)}, u32[]{:S(2)}, u32[]{:S(2)}) collective-permute-start(bf16[128,512]{1,0:T(8,128)(2,1)S(1)} %get-tuple-element.33), channel_id=1, source_target_pairs={{0,48},{16,0},{32,16},{48,32},{64,112},{80,64},{96,80},{112,96},{1... | collective-permute-start | bytes 393224 | tf_op jit(solution)/shard_map/ppermute | solution.py:284
  59.7 2.6 %collective-permute-start.22 = (bf16[128,512]{1,0:T(8,128)(2,1)S(1)}, bf16[128,512]{1,0:T(8,128)(2,1)S(1)}, u32[]{:S(2)}, u32[]{:S(2)}) collective-permute-start(bf16[128,512]{1,0:T(8,128)(2,1)S(1)} %row_total.3), channel_id=1, source_target_pairs={{0,128},{16,144},{32,160},{48,176},{64,192},{80,208},{96,224},{112... | collective-permute-start | bytes 393224 | tf_op jit(solution)/shard_map/ppermute | solution.py:301
  64.0 2.4 %collective-permute-done.16.c.refs_2_ = bf16[128,512]{1,0:T(8,128)(2,1)S(1)} collective-permute-done((bf16[128,512]{1,0:T(8,128)(2,1)S(1)}, bf16[128,512]{1,0:T(8,128)(2,1)S(1)}, u32[]{:S(2)}, u32[]{:S(2)}) %collective-permute-start.16) | collective-permute-done | bytes 131104 | tf_op jit(solution)/shard_map/ppermute | solution.py:284
  66.4 5.0 %collective-permute-done.17.d.refs_3_ = bf16[128,512]{1,0:T(8,128)(2,1)S(1)} collective-permute-done((bf16[128,512]{1,0:T(8,128)(2,1)S(1)}, bf16[128,512]{1,0:T(8,128)(2,1)S(1)}, u32[]{:S(2)}, u32[]{:S(2)}) %collective-permute-start.17) | collective-permute-done | bytes 131104 | tf_op jit(solution)/shard_map/ppermute | solution.py:284
  73.1 2.6 %collective-permute-start.28 = (bf16[128,512]{1,0:T(8,128)(2,1)S(1)}, bf16[128,512]{1,0:T(8,128)(2,1)S(1)}, u32[]{:S(2)}, u32[]{:S(2)}) collective-permute-start(bf16[128,512]{1,0:T(8,128)(2,1)S(1)} %row_total.2), channel_id=1, source_target_pairs={{0,128},{16,144},{32,160},{48,176},{64,192},{80,208},{96,224},{112... | collective-permute-start | bytes 393224 | tf_op jit(solution)/shard_map/ppermute | solution.py:301
  77.6 2.0 %collective-permute-start.25 = (bf16[128,512]{1,0:T(8,128)(2,1)S(1)}, bf16[128,512]{1,0:T(8,128)(2,1)S(1)}, u32[]{:S(2)}, u32[]{:S(2)}) collective-permute-start(bf16[128,512]{1,0:T(8,128)(2,1)S(1)} %get-tuple-element.48), channel_id=1, source_target_pairs={{0,32},{16,48},{32,0},{48,16},{64,96},{80,112},{96,64},{112,80},{1... | collective-permute-start | bytes 393224 | tf_op jit(solution)/shard_map/ppermute | solution.py:284
  79.6 2.6 %collective-permute-start.26 = (bf16[128,512]{1,0:T(8,128)(2,1)S(1)}, bf16[128,512]{1,0:T(8,128)(2,1)S(1)}, u32[]{:S(2)}, u32[]{:S(2)}) collective-permute-start(bf16[128,512]{1,0:T(8,128)(2,1)S(1)} %get-tuple-element.49), channel_id=1, source_target_pairs={{0,48},{16,0},{32,16},{48,32},{64,112},{80,64},{96,80},{112,96},{1... | collective-permute-start | bytes 393224 | tf_op jit(solution)/shard_map/ppermute | solution.py:284
  82.9 3.4 %collective-permute-start.31 = (bf16[128,512]{1,0:T(8,128)(2,1)S(1)}, bf16[128,512]{1,0:T(8,128)(2,1)S(1)}, u32[]{:S(2)}, u32[]{:S(2)}) collective-permute-start(bf16[128,512]{1,0:T(8,128)(2,1)S(1)} %get-tuple-element.53), channel_id=1, source_target_pairs={{0,32},{16,48},{32,0},{48,16},{64,96},{80,112},{96,64},{112,80},{1... | collective-permute-start | bytes 393224 | tf_op jit(solution)/shard_map/ppermute | solution.py:284
  86.2 3.5 %collective-permute-start.32 = (bf16[128,512]{1,0:T(8,128)(2,1)S(1)}, bf16[128,512]{1,0:T(8,128)(2,1)S(1)}, u32[]{:S(2)}, u32[]{:S(2)}) collective-permute-start(bf16[128,512]{1,0:T(8,128)(2,1)S(1)} %get-tuple-element.54), channel_id=1, source_target_pairs={{0,48},{16,0},{32,16},{48,32},{64,112},{80,64},{96,80},{112,96},{1... | collective-permute-start | bytes 393224 | tf_op jit(solution)/shard_map/ppermute | solution.py:284
  89.7 10.0 %collective-permute-done.26.refs_3_ = bf16[128,512]{1,0:T(8,128)(2,1)S(1)} collective-permute-done((bf16[128,512]{1,0:T(8,128)(2,1)S(1)}, bf16[128,512]{1,0:T(8,128)(2,1)S(1)}, u32[]{:S(2)}, u32[]{:S(2)}) %collective-permute-start.26) | collective-permute-done | bytes 131104 | tf_op jit(solution)/shard_map/ppermute | solution.py:284
  99.7 3.6 %collective-permute-done.32.refs_7_ = bf16[128,512]{1,0:T(8,128)(2,1)S(1)} collective-permute-done((bf16[128,512]{1,0:T(8,128)(2,1)S(1)}, bf16[128,512]{1,0:T(8,128)(2,1)S(1)}, u32[]{:S(2)}, u32[]{:S(2)}) %collective-permute-start.32) | collective-permute-done | bytes 131104 | tf_op jit(solution)/shard_map/ppermute | solution.py:284
  (52 shorter events, 19.2 us)
Async XLA Ops:
  3.1 8.8 %collective-permute-start.3 = (bf16[128,1024]{1,0:T(8,128)(2,1)S(1)}, bf16[128,1024]{1,0:T(8,128)(2,1)S(1)}, u32[]{:S(2)}, u32[]{:S(2)}) collective-permute-start(bf16[128,1024]{1,0:T(8,128)(2,1)S(1)} %join.1.refs_0_), channel_id=1, source_target_pairs={{0,2},{1,3},{2,0},{3,1},{4,6},{5,7},{6,4},{7,5},{8,10},{9,11},{10,... | collective-permute-start | bytes 786440 | tf_op jit(solution)/shard_map/ppermute | solution.py:40
  4.7 9.9 %collective-permute-start.2 = (bf16[128,1024]{1,0:T(8,128)(2,1)S(1)}, bf16[128,1024]{1,0:T(8,128)(2,1)S(1)}, u32[]{:S(2)}, u32[]{:S(2)}) collective-permute-start(bf16[128,1024]{1,0:T(8,128)(2,1)S(1)} %join.1.refs_0_), channel_id=1, source_target_pairs={{0,12},{1,13},{2,14},{3,15},{4,0},{5,1},{6,2},{7,3},{8,4},{9,5},{1... | collective-permute-start | bytes 786440 | tf_op jit(solution)/shard_map/ppermute | solution.py:40
  6.2 10.8 %collective-permute-start.7 = (bf16[128,1024]{1,0:T(8,128)(2,1)S(1)}, bf16[128,1024]{1,0:T(8,128)(2,1)S(1)}, u32[]{:S(2)}, u32[]{:S(2)}) collective-permute-start(bf16[128,1024]{1,0:T(8,128)(2,1)S(1)} %join.1.refs_0_), channel_id=1, source_target_pairs={{0,1},{1,0},{2,3},{3,2},{4,5},{5,4},{6,7},{7,6},{8,9},{9,8},{10,11... | collective-permute-start | bytes 786440 | tf_op jit(solution)/shard_map/ppermute | solution.py:40
  8.1 9.0 %collective-permute-start.1 = (bf16[128,1024]{1,0:T(8,128)(2,1)S(1)}, bf16[128,1024]{1,0:T(8,128)(2,1)S(1)}, u32[]{:S(2)}, u32[]{:S(2)}) collective-permute-start(bf16[128,1024]{1,0:T(8,128)(2,1)S(1)} %collective-permute-done.refs_1_), channel_id=1, source_target_pairs={{0,4},{1,5},{2,6},{3,7},{4,8},{5,9},{6,10},{7,11},{8,12},{9,13},{1... | collective-permute-start | bytes 786440 | tf_op jit(solution)/shard_map/ppermute | solution.py:40
  10.0 9.4 %collective-permute-start.4 = (bf16[128,1024]{1,0:T(8,128)(2,1)S(1)}, bf16[128,1024]{1,0:T(8,128)(2,1)S(1)}, u32[]{:S(2)}, u32[]{:S(2)}) collective-permute-start(bf16[128,1024]{1,0:T(8,128)(2,1)S(1)} %collective-permute-done.refs_1_), channel_id=1, source_target_pairs={{0,2},{1,3},{2,0},{3,1},{4,6},{5,7},{6,4},{7,5},{8,10},{9,11},{10,... | collective-permute-start | bytes 786440 | tf_op jit(solution)/shard_map/ppermute | solution.py:40
  11.9 10.2 %collective-permute-start.6 = (bf16[128,1024]{1,0:T(8,128)(2,1)S(1)}, bf16[128,1024]{1,0:T(8,128)(2,1)S(1)}, u32[]{:S(2)}, u32[]{:S(2)}) collective-permute-start(bf16[128,1024]{1,0:T(8,128)(2,1)S(1)} %collective-permute-done.3.refs_4_), channel_id=1, source_target_pairs={{0,12},{1,13},{2,14},{3,15},{4,0},{5,1},{6,2},{7,3},{8,4},{9,5},{1... | collective-permute-start | bytes 786440 | tf_op jit(solution)/shard_map/ppermute | solution.py:40
  14.6 7.6 %collective-permute-start.8 = (bf16[128,1024]{1,0:T(8,128)(2,1)S(1)}, bf16[128,1024]{1,0:T(8,128)(2,1)S(1)}, u32[]{:S(2)}, u32[]{:S(2)}) collective-permute-start(bf16[128,1024]{1,0:T(8,128)(2,1)S(1)} %collective-permute-done.refs_1_), channel_id=1, source_target_pairs={{0,1},{1,0},{2,3},{3,2},{4,5},{5,4},{6,7},{7,6},{8,9},{9,8},{10,11... | collective-permute-start | bytes 786440 | tf_op jit(solution)/shard_map/ppermute | solution.py:40
  35.5 20.3 %collective-permute-start.18 = (bf16[128,512]{1,0:T(8,128)(2,1)S(1)}, bf16[128,512]{1,0:T(8,128)(2,1)S(1)}, u32[]{:S(2)}, u32[]{:S(2)}) collective-permute-start(bf16[128,512]{1,0:T(8,128)(2,1)S(1)} %get-tuple-element.35), channel_id=1, source_target_pairs={{0,16},{16,32},{32,48},{48,0},{64,80},{80,96},{96,112},{112,64},{1... | collective-permute-start | bytes 393224 | tf_op jit(solution)/shard_map/ppermute | solution.py:284
  38.6 19.7 %collective-permute-start.19 = (bf16[128,512]{1,0:T(8,128)(2,1)S(1)}, bf16[128,512]{1,0:T(8,128)(2,1)S(1)}, u32[]{:S(2)}, u32[]{:S(2)}) collective-permute-start(bf16[128,512]{1,0:T(8,128)(2,1)S(1)} %get-tuple-element.36), channel_id=1, source_target_pairs={{0,32},{16,48},{32,0},{48,16},{64,96},{80,112},{96,64},{112,80},{1... | collective-permute-start | bytes 393224 | tf_op jit(solution)/shard_map/ppermute | solution.py:284
  43.6 14.6 %collective-permute-start.20 = (bf16[128,512]{1,0:T(8,128)(2,1)S(1)}, bf16[128,512]{1,0:T(8,128)(2,1)S(1)}, u32[]{:S(2)}, u32[]{:S(2)}) collective-permute-start(bf16[128,512]{1,0:T(8,128)(2,1)S(1)} %get-tuple-element.37), channel_id=1, source_target_pairs={{0,48},{16,0},{32,16},{48,32},{64,112},{80,64},{96,80},{112,96},{1... | collective-permute-start | bytes 393224 | tf_op jit(solution)/shard_map/ppermute | solution.py:284
  53.6 8.7 %collective-permute-start.15 = (bf16[128,512]{1,0:T(8,128)(2,1)S(1)}, bf16[128,512]{1,0:T(8,128)(2,1)S(1)}, u32[]{:S(2)}, u32[]{:S(2)}) collective-permute-start(bf16[128,512]{1,0:T(8,128)(2,1)S(1)} %get-tuple-element.31), channel_id=1, source_target_pairs={{0,16},{16,32},{32,48},{48,0},{64,80},{80,96},{96,112},{112,64},{1... | collective-permute-start | bytes 393224 | tf_op jit(solution)/shard_map/ppermute | solution.py:284
  53.7 12.7 %collective-permute-start.16 = (bf16[128,512]{1,0:T(8,128)(2,1)S(1)}, bf16[128,512]{1,0:T(8,128)(2,1)S(1)}, u32[]{:S(2)}, u32[]{:S(2)}) collective-permute-start(bf16[128,512]{1,0:T(8,128)(2,1)S(1)} %get-tuple-element.32), channel_id=1, source_target_pairs={{0,32},{16,48},{32,0},{48,16},{64,96},{80,112},{96,64},{112,80},{1... | collective-permute-start | bytes 393224 | tf_op jit(solution)/shard_map/ppermute | solution.py:284
  55.8 15.6 %collective-permute-start.17 = (bf16[128,512]{1,0:T(8,128)(2,1)S(1)}, bf16[128,512]{1,0:T(8,128)(2,1)S(1)}, u32[]{:S(2)}, u32[]{:S(2)}) collective-permute-start(bf16[128,512]{1,0:T(8,128)(2,1)S(1)} %get-tuple-element.33), channel_id=1, source_target_pairs={{0,48},{16,0},{32,16},{48,32},{64,112},{80,64},{96,80},{112,96},{1... | collective-permute-start | bytes 393224 | tf_op jit(solution)/shard_map/ppermute | solution.py:284
  58.3 13.1 %collective-permute-start.21 = (bf16[128,512]{1,0:T(8,128)(2,1)S(1)}, bf16[128,512]{1,0:T(8,128)(2,1)S(1)}, u32[]{:S(2)}, u32[]{:S(2)}) collective-permute-start(bf16[128,512]{1,0:T(8,128)(2,1)S(1)} %row_total.3), channel_id=1, source_target_pairs={{0,64},{16,80},{32,96},{48,112},{64,128},{80,144},{96,160},{112,17... | collective-permute-start | bytes 393224 | tf_op jit(solution)/shard_map/ppermute | solution.py:301
  59.7 11.7 %collective-permute-start.22 = (bf16[128,512]{1,0:T(8,128)(2,1)S(1)}, bf16[128,512]{1,0:T(8,128)(2,1)S(1)}, u32[]{:S(2)}, u32[]{:S(2)}) collective-permute-start(bf16[128,512]{1,0:T(8,128)(2,1)S(1)} %row_total.3), channel_id=1, source_target_pairs={{0,128},{16,144},{32,160},{48,176},{64,192},{80,208},{96,224},{112... | collective-permute-start | bytes 393224 | tf_op jit(solution)/shard_map/ppermute | solution.py:301
  62.3 9.1 %collective-permute-start.23 = (bf16[128,512]{1,0:T(8,128)(2,1)S(1)}, bf16[128,512]{1,0:T(8,128)(2,1)S(1)}, u32[]{:S(2)}, u32[]{:S(2)}) collective-permute-start(bf16[128,512]{1,0:T(8,128)(2,1)S(1)} %row_total.3), channel_id=1, source_target_pairs={{0,192},{16,208},{32,224},{48,240},{64,0},{80,16},{96,32},{112,48}... | collective-permute-start | bytes 393224 | tf_op jit(solution)/shard_map/ppermute | solution.py:301
  71.8 7.9 %collective-permute-start.27 = (bf16[128,512]{1,0:T(8,128)(2,1)S(1)}, bf16[128,512]{1,0:T(8,128)(2,1)S(1)}, u32[]{:S(2)}, u32[]{:S(2)}) collective-permute-start(bf16[128,512]{1,0:T(8,128)(2,1)S(1)} %row_total.2), channel_id=1, source_target_pairs={{0,64},{16,80},{32,96},{48,112},{64,128},{80,144},{96,160},{112,17... | collective-permute-start | bytes 393224 | tf_op jit(solution)/shard_map/ppermute | solution.py:301
  73.1 9.1 %collective-permute-start.28 = (bf16[128,512]{1,0:T(8,128)(2,1)S(1)}, bf16[128,512]{1,0:T(8,128)(2,1)S(1)}, u32[]{:S(2)}, u32[]{:S(2)}) collective-permute-start(bf16[128,512]{1,0:T(8,128)(2,1)S(1)} %row_total.2), channel_id=1, source_target_pairs={{0,128},{16,144},{32,160},{48,176},{64,192},{80,208},{96,224},{112... | collective-permute-start | bytes 393224 | tf_op jit(solution)/shard_map/ppermute | solution.py:301
  76.8 9.4 %collective-permute-start.24 = (bf16[128,512]{1,0:T(8,128)(2,1)S(1)}, bf16[128,512]{1,0:T(8,128)(2,1)S(1)}, u32[]{:S(2)}, u32[]{:S(2)}) collective-permute-start(bf16[128,512]{1,0:T(8,128)(2,1)S(1)} %get-tuple-element.47), channel_id=1, source_target_pairs={{0,16},{16,32},{32,48},{48,0},{64,80},{80,96},{96,112},{112,64},{1... | collective-permute-start | bytes 393224 | tf_op jit(solution)/shard_map/ppermute | solution.py:284
  77.6 12.1 %collective-permute-start.25 = (bf16[128,512]{1,0:T(8,128)(2,1)S(1)}, bf16[128,512]{1,0:T(8,128)(2,1)S(1)}, u32[]{:S(2)}, u32[]{:S(2)}) collective-permute-start(bf16[128,512]{1,0:T(8,128)(2,1)S(1)} %get-tuple-element.48), channel_id=1, source_target_pairs={{0,32},{16,48},{32,0},{48,16},{64,96},{80,112},{96,64},{112,80},{1... | collective-permute-start | bytes 393224 | tf_op jit(solution)/shard_map/ppermute | solution.py:284
  79.6 20.1 %collective-permute-start.26 = (bf16[128,512]{1,0:T(8,128)(2,1)S(1)}, bf16[128,512]{1,0:T(8,128)(2,1)S(1)}, u32[]{:S(2)}, u32[]{:S(2)}) collective-permute-start(bf16[128,512]{1,0:T(8,128)(2,1)S(1)} %get-tuple-element.49), channel_id=1, source_target_pairs={{0,48},{16,0},{32,16},{48,32},{64,112},{80,64},{96,80},{112,96},{1... | collective-permute-start | bytes 393224 | tf_op jit(solution)/shard_map/ppermute | solution.py:284
  82.5 17.3 %collective-permute-start.30 = (bf16[128,512]{1,0:T(8,128)(2,1)S(1)}, bf16[128,512]{1,0:T(8,128)(2,1)S(1)}, u32[]{:S(2)}, u32[]{:S(2)}) collective-permute-start(bf16[128,512]{1,0:T(8,128)(2,1)S(1)} %get-tuple-element.52), channel_id=1, source_target_pairs={{0,16},{16,32},{32,48},{48,0},{64,80},{80,96},{96,112},{112,64},{1... | collective-permute-start | bytes 393224 | tf_op jit(solution)/shard_map/ppermute | solution.py:284
  82.9 16.9 %collective-permute-start.31 = (bf16[128,512]{1,0:T(8,128)(2,1)S(1)}, bf16[128,512]{1,0:T(8,128)(2,1)S(1)}, u32[]{:S(2)}, u32[]{:S(2)}) collective-permute-start(bf16[128,512]{1,0:T(8,128)(2,1)S(1)} %get-tuple-element.53), channel_id=1, source_target_pairs={{0,32},{16,48},{32,0},{48,16},{64,96},{80,112},{96,64},{112,80},{1... | collective-permute-start | bytes 393224 | tf_op jit(solution)/shard_map/ppermute | solution.py:284
  86.2 17.1 %collective-permute-start.32 = (bf16[128,512]{1,0:T(8,128)(2,1)S(1)}, bf16[128,512]{1,0:T(8,128)(2,1)S(1)}, u32[]{:S(2)}, u32[]{:S(2)}) collective-permute-start(bf16[128,512]{1,0:T(8,128)(2,1)S(1)} %get-tuple-element.54), channel_id=1, source_target_pairs={{0,48},{16,0},{32,16},{48,32},{64,112},{80,64},{96,80},{112,96},{1... | collective-permute-start | bytes 393224 | tf_op jit(solution)/shard_map/ppermute | solution.py:284
  (10 other events, 68.2 us)

commit v5 on v4

--- a/solution.py
+++ b/solution.py
@@ -16,6 +16,7 @@
 TRACE = SPANS * TOK
 WIDTH = KEY_VALUE_HEADS * HEAD_SIZE
 RING = 4
+OUTWARD = (0, 2, 1, 3)
 PAIR = 2 * HEAD_SIZE
 EXP2_SCALE = math.log2(math.e) / math.sqrt(HEAD_SIZE)
 HIDDEN = -1e30
@@ -213,7 +214,7 @@
         out_shape=jax.ShapeDtypeStruct((TOK, PART * PAIR), jnp.bfloat16),
         compiler_params=pltpu.CompilerParams(vmem_limit_bytes=4 * 2**20),
         name="row_total",
-    )(*slabs)
+    )(*(slabs[steps] for steps in OUTWARD))
 
 
 def prefix_kernel(chunk, section, residual_ref, *refs):
@@ -221,7 +222,7 @@
     ordered, summed = refs[3 * RING - 1 :]
     place, row = section[0] % RING, section[0] // RING
     for steps in range(RING):
-        ordered[(place + RING - steps) % RING] = slabs[steps][...]
+        ordered[(place + RING - steps) % RING] = slabs[OUTWARD.index(steps)][...]
     for part in range(PART):
         columns = slice(part * PAIR, (part + 1) * PAIR)
         first = (chunk * PART + part) * GROUP * HEAD_SIZE + place * PAIR
@@ -250,7 +251,7 @@
         ],
         compiler_params=pltpu.CompilerParams(vmem_limit_bytes=8 * 2**20),
         name="prefix",
-    )(section, residual, *slabs, *below)
+    )(section, residual, *(slabs[steps] for steps in OUTWARD), *below)
 
 
 def assemble_kernel(section, *refs):
@@ -258,7 +259,7 @@
     place = section[0] % RING
     for chunk in range(CHUNKS):
         for steps in range(RING):
-            column = (place + RING - steps) % RING * PAIR
+            column = (place + RING - OUTWARD[steps]) % RING * PAIR
             for part in range(PART):
                 first = (chunk * PART + part) * GROUP * HEAD_SIZE + column
                 o_ref[0, :, pl.ds(pl.multiple_of(first, PAIR), PAIR)] = slabs[
@@ -276,7 +277,7 @@
         out_shape=jax.ShapeDtypeStruct((1, TOK, width), jnp.bfloat16),
         compiler_params=pltpu.CompilerParams(vmem_limit_bytes=8 * 2**20),
         name="assemble",
-    )(section, *slabs)
+    )(section, *(slabs[c * RING + steps] for c in range(CHUNKS) for steps in OUTWARD))
 
 
 def turn(slabs):

time: 105 us -> 103 us (0.981)
  waiting for transfers between devices: 23.5 us -> 21 us
  starting transfers between devices: 63 us -> 64.1 us
    ppermute x12, waiting for transfers between devices: 21 us -> 18.4 us  [turn(): lax.ppermute(slabs[steps], 'section', turn_pairs(steps))]
    ppermute x6, starting transfers between devices: 10.8 us -> 11.9 us  [body(): lax.ppermute(total, 'section', climb_pairs(s))]
  transfers between devices with their start and end apart: 33 -> 33, of which waited for: 7 -> 9; matrix products, arithmetic and copies ran while one was open for 0% -> 0% of each run, Pallas kernels for 8% -> 8%
where the time goes in v5:
time: 103 us
  starting transfers between devices  64.1 us (62%)
  waiting for transfers between devices  21 us (20%)
  Pallas kernels  17.9 us (17%)
    ppermute x12, starting transfers between devices, turn(): lax.ppermute(slabs[steps], 'section', turn_pairs(steps))  27.8 us
    ppermute x15, starting transfers between devices, ctx_move(): return lax.ppermute(unit, 'ctx', ctx_pairs(dx, dz, dc))  24.4 us
    ppermute x12, waiting for transfers between devices, turn(): lax.ppermute(slabs[steps], 'section', turn_pairs(steps))  18.4 us
    pallas_call x2, Pallas kernels, attention(): pl.pallas_call(functools.partial(attention_kernel, chunk), in_specs=[smem...  15.1 us
    ppermute x6, starting transfers between devices, body(): lax.ppermute(total, 'section', climb_pairs(s))  11.9 us
    ppermute x15, waiting for transfers between devices, ctx_move(): return lax.ppermute(unit, 'ctx', ctx_pairs(dx, dz, dc))  2.49 us
  transfers between devices with their start and end apart: 33, of which 9 were waited for; matrix products, arithmetic and copies ran while one was open for 0% of the time, Pallas kernels for 8%

profile of v5, /device:TPU:1, one launch (start us, length us, event | category | flops | bytes accessed | tf_op | source)
XLA Modules:
  0.0 103.1 jit_solution(4324793933714295930)
XLA Ops:
  1.0 2.1 %collective-permute-start = (bf16[128,1024]{1,0:T(8,128)(2,1)S(1)}, bf16[128,1024]{1,0:T(8,128)(2,1)S(1)}, u32[]{:S(2)}, u32[]{:S(2)}) collective-permute-start(bf16[128,1024]{1,0:T(8,128)(2,1)S(1)} %join.1.refs_0_), channel_id=1, source_target_pairs={{0,4},{1,5},{2,6},{3,7},{4,8},{5,9},{6,10},{7,11},{8,12},{9,13},{1... | collective-permute-start | bytes 786440 | tf_op jit(solution)/shard_map/ppermute | solution.py:41
  10.0 1.9 %collective-permute-start.4 = (bf16[128,1024]{1,0:T(8,128)(2,1)S(1)}, bf16[128,1024]{1,0:T(8,128)(2,1)S(1)}, u32[]{:S(2)}, u32[]{:S(2)}) collective-permute-start(bf16[128,1024]{1,0:T(8,128)(2,1)S(1)} %collective-permute-done.refs_1_), channel_id=1, source_target_pairs={{0,2},{1,3},{2,0},{3,1},{4,6},{5,7},{6,4},{7,5},{8,10},{9,11},{10,... | collective-permute-start | bytes 786440 | tf_op jit(solution)/shard_map/ppermute | solution.py:41
  11.9 2.7 %collective-permute-start.6 = (bf16[128,1024]{1,0:T(8,128)(2,1)S(1)}, bf16[128,1024]{1,0:T(8,128)(2,1)S(1)}, u32[]{:S(2)}, u32[]{:S(2)}) collective-permute-start(bf16[128,1024]{1,0:T(8,128)(2,1)S(1)} %collective-permute-done.3.refs_4_), channel_id=1, source_target_pairs={{0,12},{1,13},{2,14},{3,15},{4,0},{5,1},{6,2},{7,3},{8,4},{9,5},{1... | collective-permute-start | bytes 786440 | tf_op jit(solution)/shard_map/ppermute | solution.py:41
  14.6 2.4 %collective-permute-start.8 = (bf16[128,1024]{1,0:T(8,128)(2,1)S(1)}, bf16[128,1024]{1,0:T(8,128)(2,1)S(1)}, u32[]{:S(2)}, u32[]{:S(2)}) collective-permute-start(bf16[128,1024]{1,0:T(8,128)(2,1)S(1)} %collective-permute-done.refs_1_), channel_id=1, source_target_pairs={{0,1},{1,0},{2,3},{3,2},{4,5},{5,4},{6,7},{7,6},{8,9},{9,8},{10,11... | collective-permute-start | bytes 786440 | tf_op jit(solution)/shard_map/ppermute | solution.py:41
  17.1 2.3 %collective-permute-start.5 = (bf16[128,1024]{1,0:T(8,128)(2,1)S(1)}, bf16[128,1024]{1,0:T(8,128)(2,1)S(1)}, u32[]{:S(2)}, u32[]{:S(2)}) collective-permute-start(bf16[128,1024]{1,0:T(8,128)(2,1)S(1)} %collective-permute-done.1.refs_2_), channel_id=1, source_target_pairs={{0,2},{1,3},{2,0},{3,1},{4,6},{5,7},{6,4},{7,5},{8,10},{9,11},{10,... | collective-permute-start | bytes 786440 | tf_op jit(solution)/shard_map/ppermute | solution.py:41
  19.4 2.7 %collective-permute-start.10 = (bf16[128,1024]{1,0:T(8,128)(2,1)S(1)}, bf16[128,1024]{1,0:T(8,128)(2,1)S(1)}, u32[]{:S(2)}, u32[]{:S(2)}) collective-permute-start(bf16[128,1024]{1,0:T(8,128)(2,1)S(1)} %collective-permute-done.2.refs_3_), channel_id=1, source_target_pairs={{0,1},{1,0},{2,3},{3,2},{4,5},{5,4},{6,7},{7,6},{8,9},{9,8},{10,11... | collective-permute-start | bytes 786440 | tf_op jit(solution)/shard_map/ppermute | solution.py:41
  23.5 3.1 %collective-permute-start.13 = (bf16[128,1024]{1,0:T(8,128)(2,1)S(1)}, bf16[128,1024]{1,0:T(8,128)(2,1)}, u32[]{:S(2)}, u32[]{:S(2)}) collective-permute-start(bf16[128,1024]{1,0:T(8,128)(2,1)S(1)} %collective-permute-done.5.refs_6_), channel_id=1, source_target_pairs={{0,1},{1,0},{2,3},{3,2},{4,5},{5,4},{6,7},{7,6},{8,9},{9,8},{10,11... | collective-permute-start | bytes 786440 | tf_op jit(solution)/shard_map/ppermute | solution.py:41
  27.9 7.6 %attention.3 = (bf16[128,512]{1,0:T(8,128)(2,1)S(1)}, bf16[128,512]{1,0:T(8,128)(2,1)S(1)}, bf16[128,512]{1,0:T(8,128)(2,1)S(1)}, bf16[128,512]{1,0:T(8,128)(2,1)S(1)}) custom-call(s32[16]{0:T(128)} %span_map.3, s32[1]{0:T(128)} %bitcast.1.ctx, s32[1]{0:T(128)} %bitcast.section, bf16[128,4096]{1,0:T(8,128)(2,1)} %bitcast.3, ...), custom_call_target="tpu_custom_call" | custom-call | flops 4294967296 | bytes 3145728 | tf_op jit(solution)/shard_map/attention/pallas_call | solution.py:181
  35.5 3.1 %collective-permute-start.18 = (bf16[128,512]{1,0:T(8,128)(2,1)S(1)}, bf16[128,512]{1,0:T(8,128)(2,1)S(1)}, u32[]{:S(2)}, u32[]{:S(2)}) collective-permute-start(bf16[128,512]{1,0:T(8,128)(2,1)S(1)} %get-tuple-element.35), channel_id=1, source_target_pairs={{0,16},{16,32},{32,48},{48,0},{64,80},{80,96},{96,112},{112,64},{1... | collective-permute-start | bytes 393224 | tf_op jit(solution)/shard_map/ppermute | solution.py:285
  38.6 5.1 %collective-permute-start.19 = (bf16[128,512]{1,0:T(8,128)(2,1)S(1)}, bf16[128,512]{1,0:T(8,128)(2,1)S(1)}, u32[]{:S(2)}, u32[]{:S(2)}) collective-permute-start(bf16[128,512]{1,0:T(8,128)(2,1)S(1)} %get-tuple-element.36), channel_id=1, source_target_pairs={{0,32},{16,48},{32,0},{48,16},{64,96},{80,112},{96,64},{112,80},{1... | collective-permute-start | bytes 393224 | tf_op jit(solution)/shard_map/ppermute | solution.py:285
  43.6 2.4 %collective-permute-start.20 = (bf16[128,512]{1,0:T(8,128)(2,1)S(1)}, bf16[128,512]{1,0:T(8,128)(2,1)S(1)}, u32[]{:S(2)}, u32[]{:S(2)}) collective-permute-start(bf16[128,512]{1,0:T(8,128)(2,1)S(1)} %get-tuple-element.37), channel_id=1, source_target_pairs={{0,48},{16,0},{32,16},{48,32},{64,112},{80,64},{96,80},{112,96},{1... | collective-permute-start | bytes 393224 | tf_op jit(solution)/shard_map/ppermute | solution.py:285
  46.0 7.6 %attention.2 = (bf16[128,512]{1,0:T(8,128)(2,1)S(1)}, bf16[128,512]{1,0:T(8,128)(2,1)S(1)}, bf16[128,512]{1,0:T(8,128)(2,1)S(1)}, bf16[128,512]{1,0:T(8,128)(2,1)S(1)}) custom-call(s32[16]{0:T(128)} %span_map.3, s32[1]{0:T(128)} %bitcast.1.ctx, s32[1]{0:T(128)} %bitcast.section, bf16[128,4096]{1,0:T(8,128)(2,1)} %bitcast.4, ...), custom_call_target="tpu_custom_call" | custom-call | flops 4294967296 | bytes 3145728 | tf_op jit(solution)/shard_map/attention/pallas_call | solution.py:181
  55.8 2.5 %collective-permute-start.17 = (bf16[128,512]{1,0:T(8,128)(2,1)S(1)}, bf16[128,512]{1,0:T(8,128)(2,1)S(1)}, u32[]{:S(2)}, u32[]{:S(2)}) collective-permute-start(bf16[128,512]{1,0:T(8,128)(2,1)S(1)} %get-tuple-element.33), channel_id=1, source_target_pairs={{0,48},{16,0},{32,16},{48,32},{64,112},{80,64},{96,80},{112,96},{1... | collective-permute-start | bytes 393224 | tf_op jit(solution)/shard_map/ppermute | solution.py:285
  59.7 2.6 %collective-permute-start.22 = (bf16[128,512]{1,0:T(8,128)(2,1)S(1)}, bf16[128,512]{1,0:T(8,128)(2,1)S(1)}, u32[]{:S(2)}, u32[]{:S(2)}) collective-permute-start(bf16[128,512]{1,0:T(8,128)(2,1)S(1)} %row_total.3), channel_id=1, source_target_pairs={{0,128},{16,144},{32,160},{48,176},{64,192},{80,208},{96,224},{112... | collective-permute-start | bytes 393224 | tf_op jit(solution)/shard_map/ppermute | solution.py:302
  64.0 2.8 %collective-permute-start.23 = (bf16[128,512]{1,0:T(8,128)(2,1)S(1)}, bf16[128,512]{1,0:T(8,128)(2,1)S(1)}, u32[]{:S(2)}, u32[]{:S(2)}) collective-permute-start(bf16[128,512]{1,0:T(8,128)(2,1)S(1)} %row_total.3), channel_id=1, source_target_pairs={{0,192},{16,208},{32,224},{48,240},{64,0},{80,16},{96,32},{112,48}... | collective-permute-start | bytes 393224 | tf_op jit(solution)/shard_map/ppermute | solution.py:302
  66.8 2.0 %collective-permute-done.17.d.refs_3_ = bf16[128,512]{1,0:T(8,128)(2,1)S(1)} collective-permute-done((bf16[128,512]{1,0:T(8,128)(2,1)S(1)}, bf16[128,512]{1,0:T(8,128)(2,1)S(1)}, u32[]{:S(2)}, u32[]{:S(2)}) %collective-permute-start.17) | collective-permute-done | bytes 131104 | tf_op jit(solution)/shard_map/ppermute | solution.py:285
  70.7 2.6 %collective-permute-start.28 = (bf16[128,512]{1,0:T(8,128)(2,1)S(1)}, bf16[128,512]{1,0:T(8,128)(2,1)S(1)}, u32[]{:S(2)}, u32[]{:S(2)}) collective-permute-start(bf16[128,512]{1,0:T(8,128)(2,1)S(1)} %row_total.2), channel_id=1, source_target_pairs={{0,128},{16,144},{32,160},{48,176},{64,192},{80,208},{96,224},{112... | collective-permute-start | bytes 393224 | tf_op jit(solution)/shard_map/ppermute | solution.py:302
  74.2 4.2 %collective-permute-start.24 = (bf16[128,512]{1,0:T(8,128)(2,1)S(1)}, bf16[128,512]{1,0:T(8,128)(2,1)S(1)}, u32[]{:S(2)}, u32[]{:S(2)}) collective-permute-start(bf16[128,512]{1,0:T(8,128)(2,1)S(1)} %get-tuple-element.47), channel_id=1, source_target_pairs={{0,32},{16,48},{32,0},{48,16},{64,96},{80,112},{96,64},{112,80},{1... | collective-permute-start | bytes 393224 | tf_op jit(solution)/shard_map/ppermute | solution.py:285
  78.5 3.4 %collective-permute-start.26 = (bf16[128,512]{1,0:T(8,128)(2,1)S(1)}, bf16[128,512]{1,0:T(8,128)(2,1)S(1)}, u32[]{:S(2)}, u32[]{:S(2)}) collective-permute-start(bf16[128,512]{1,0:T(8,128)(2,1)S(1)} %get-tuple-element.49), channel_id=1, source_target_pairs={{0,48},{16,0},{32,16},{48,32},{64,112},{80,64},{96,80},{112,96},{1... | collective-permute-start | bytes 393224 | tf_op jit(solution)/shard_map/ppermute | solution.py:285
  83.6 2.4 %collective-permute-start.31 = (bf16[128,512]{1,0:T(8,128)(2,1)S(1)}, bf16[128,512]{1,0:T(8,128)(2,1)S(1)}, u32[]{:S(2)}, u32[]{:S(2)}) collective-permute-start(bf16[128,512]{1,0:T(8,128)(2,1)S(1)} %get-tuple-element.53), channel_id=1, source_target_pairs={{0,16},{16,32},{32,48},{48,0},{64,80},{80,96},{96,112},{112,64},{1... | collective-permute-start | bytes 393224 | tf_op jit(solution)/shard_map/ppermute | solution.py:285
  87.1 2.3 %collective-permute-done.25.refs_2_ = bf16[128,512]{1,0:T(8,128)(2,1)S(1)} collective-permute-done((bf16[128,512]{1,0:T(8,128)(2,1)S(1)}, bf16[128,512]{1,0:T(8,128)(2,1)S(1)}, u32[]{:S(2)}, u32[]{:S(2)}) %collective-permute-start.25) | collective-permute-done | bytes 131104 | tf_op jit(solution)/shard_map/ppermute | solution.py:285
  89.4 4.6 %collective-permute-done.26.refs_3_ = bf16[128,512]{1,0:T(8,128)(2,1)S(1)} collective-permute-done((bf16[128,512]{1,0:T(8,128)(2,1)S(1)}, bf16[128,512]{1,0:T(8,128)(2,1)S(1)}, u32[]{:S(2)}, u32[]{:S(2)}) %collective-permute-start.26) | collective-permute-done | bytes 131104 | tf_op jit(solution)/shard_map/ppermute | solution.py:285
  94.1 5.4 %collective-permute-done.31.refs_6_ = bf16[128,512]{1,0:T(8,128)(2,1)S(1)} collective-permute-done((bf16[128,512]{1,0:T(8,128)(2,1)S(1)}, bf16[128,512]{1,0:T(8,128)(2,1)S(1)}, u32[]{:S(2)}, u32[]{:S(2)}) %collective-permute-start.31) | collective-permute-done | bytes 131104 | tf_op jit(solution)/shard_map/ppermute | solution.py:285
  99.5 2.5 %collective-permute-done.32.refs_7_ = bf16[128,512]{1,0:T(8,128)(2,1)S(1)} collective-permute-done((bf16[128,512]{1,0:T(8,128)(2,1)S(1)}, bf16[128,512]{1,0:T(8,128)(2,1)S(1)}, u32[]{:S(2)}, u32[]{:S(2)}) %collective-permute-start.32) | collective-permute-done | bytes 131104 | tf_op jit(solution)/shard_map/ppermute | solution.py:285
  (52 shorter events, 22.7 us)
Async XLA Ops:
  3.1 8.8 %collective-permute-start.3 = (bf16[128,1024]{1,0:T(8,128)(2,1)S(1)}, bf16[128,1024]{1,0:T(8,128)(2,1)S(1)}, u32[]{:S(2)}, u32[]{:S(2)}) collective-permute-start(bf16[128,1024]{1,0:T(8,128)(2,1)S(1)} %join.1.refs_0_), channel_id=1, source_target_pairs={{0,2},{1,3},{2,0},{3,1},{4,6},{5,7},{6,4},{7,5},{8,10},{9,11},{10,... | collective-permute-start | bytes 786440 | tf_op jit(solution)/shard_map/ppermute | solution.py:41
  4.7 9.9 %collective-permute-start.2 = (bf16[128,1024]{1,0:T(8,128)(2,1)S(1)}, bf16[128,1024]{1,0:T(8,128)(2,1)S(1)}, u32[]{:S(2)}, u32[]{:S(2)}) collective-permute-start(bf16[128,1024]{1,0:T(8,128)(2,1)S(1)} %join.1.refs_0_), channel_id=1, source_target_pairs={{0,12},{1,13},{2,14},{3,15},{4,0},{5,1},{6,2},{7,3},{8,4},{9,5},{1... | collective-permute-start | bytes 786440 | tf_op jit(solution)/shard_map/ppermute | solution.py:41
  6.2 10.8 %collective-permute-start.7 = (bf16[128,1024]{1,0:T(8,128)(2,1)S(1)}, bf16[128,1024]{1,0:T(8,128)(2,1)S(1)}, u32[]{:S(2)}, u32[]{:S(2)}) collective-permute-start(bf16[128,1024]{1,0:T(8,128)(2,1)S(1)} %join.1.refs_0_), channel_id=1, source_target_pairs={{0,1},{1,0},{2,3},{3,2},{4,5},{5,4},{6,7},{7,6},{8,9},{9,8},{10,11... | collective-permute-start | bytes 786440 | tf_op jit(solution)/shard_map/ppermute | solution.py:41
  8.1 9.0 %collective-permute-start.1 = (bf16[128,1024]{1,0:T(8,128)(2,1)S(1)}, bf16[128,1024]{1,0:T(8,128)(2,1)S(1)}, u32[]{:S(2)}, u32[]{:S(2)}) collective-permute-start(bf16[128,1024]{1,0:T(8,128)(2,1)S(1)} %collective-permute-done.refs_1_), channel_id=1, source_target_pairs={{0,4},{1,5},{2,6},{3,7},{4,8},{5,9},{6,10},{7,11},{8,12},{9,13},{1... | collective-permute-start | bytes 786440 | tf_op jit(solution)/shard_map/ppermute | solution.py:41
  10.0 9.4 %collective-permute-start.4 = (bf16[128,1024]{1,0:T(8,128)(2,1)S(1)}, bf16[128,1024]{1,0:T(8,128)(2,1)S(1)}, u32[]{:S(2)}, u32[]{:S(2)}) collective-permute-start(bf16[128,1024]{1,0:T(8,128)(2,1)S(1)} %collective-permute-done.refs_1_), channel_id=1, source_target_pairs={{0,2},{1,3},{2,0},{3,1},{4,6},{5,7},{6,4},{7,5},{8,10},{9,11},{10,... | collective-permute-start | bytes 786440 | tf_op jit(solution)/shard_map/ppermute | solution.py:41
  11.9 10.2 %collective-permute-start.6 = (bf16[128,1024]{1,0:T(8,128)(2,1)S(1)}, bf16[128,1024]{1,0:T(8,128)(2,1)S(1)}, u32[]{:S(2)}, u32[]{:S(2)}) collective-permute-start(bf16[128,1024]{1,0:T(8,128)(2,1)S(1)} %collective-permute-done.3.refs_4_), channel_id=1, source_target_pairs={{0,12},{1,13},{2,14},{3,15},{4,0},{5,1},{6,2},{7,3},{8,4},{9,5},{1... | collective-permute-start | bytes 786440 | tf_op jit(solution)/shard_map/ppermute | solution.py:41
  14.6 7.6 %collective-permute-start.8 = (bf16[128,1024]{1,0:T(8,128)(2,1)S(1)}, bf16[128,1024]{1,0:T(8,128)(2,1)S(1)}, u32[]{:S(2)}, u32[]{:S(2)}) collective-permute-start(bf16[128,1024]{1,0:T(8,128)(2,1)S(1)} %collective-permute-done.refs_1_), channel_id=1, source_target_pairs={{0,1},{1,0},{2,3},{3,2},{4,5},{5,4},{6,7},{7,6},{8,9},{9,8},{10,11... | collective-permute-start | bytes 786440 | tf_op jit(solution)/shard_map/ppermute | solution.py:41
  35.5 20.3 %collective-permute-start.18 = (bf16[128,512]{1,0:T(8,128)(2,1)S(1)}, bf16[128,512]{1,0:T(8,128)(2,1)S(1)}, u32[]{:S(2)}, u32[]{:S(2)}) collective-permute-start(bf16[128,512]{1,0:T(8,128)(2,1)S(1)} %get-tuple-element.35), channel_id=1, source_target_pairs={{0,16},{16,32},{32,48},{48,0},{64,80},{80,96},{96,112},{112,64},{1... | collective-permute-start | bytes 393224 | tf_op jit(solution)/shard_map/ppermute | solution.py:285
  38.6 19.7 %collective-permute-start.19 = (bf16[128,512]{1,0:T(8,128)(2,1)S(1)}, bf16[128,512]{1,0:T(8,128)(2,1)S(1)}, u32[]{:S(2)}, u32[]{:S(2)}) collective-permute-start(bf16[128,512]{1,0:T(8,128)(2,1)S(1)} %get-tuple-element.36), channel_id=1, source_target_pairs={{0,32},{16,48},{32,0},{48,16},{64,96},{80,112},{96,64},{112,80},{1... | collective-permute-start | bytes 393224 | tf_op jit(solution)/shard_map/ppermute | solution.py:285
  43.6 14.6 %collective-permute-start.20 = (bf16[128,512]{1,0:T(8,128)(2,1)S(1)}, bf16[128,512]{1,0:T(8,128)(2,1)S(1)}, u32[]{:S(2)}, u32[]{:S(2)}) collective-permute-start(bf16[128,512]{1,0:T(8,128)(2,1)S(1)} %get-tuple-element.37), channel_id=1, source_target_pairs={{0,48},{16,0},{32,16},{48,32},{64,112},{80,64},{96,80},{112,96},{1... | collective-permute-start | bytes 393224 | tf_op jit(solution)/shard_map/ppermute | solution.py:285
  53.6 10.4 %collective-permute-start.15 = (bf16[128,512]{1,0:T(8,128)(2,1)S(1)}, bf16[128,512]{1,0:T(8,128)(2,1)S(1)}, u32[]{:S(2)}, u32[]{:S(2)}) collective-permute-start(bf16[128,512]{1,0:T(8,128)(2,1)S(1)} %get-tuple-element.31), channel_id=1, source_target_pairs={{0,32},{16,48},{32,0},{48,16},{64,96},{80,112},{96,64},{112,80},{1... | collective-permute-start | bytes 393224 | tf_op jit(solution)/shard_map/ppermute | solution.py:285
  54.7 12.1 %collective-permute-start.16 = (bf16[128,512]{1,0:T(8,128)(2,1)S(1)}, bf16[128,512]{1,0:T(8,128)(2,1)S(1)}, u32[]{:S(2)}, u32[]{:S(2)}) collective-permute-start(bf16[128,512]{1,0:T(8,128)(2,1)S(1)} %get-tuple-element.32), channel_id=1, source_target_pairs={{0,16},{16,32},{32,48},{48,0},{64,80},{80,96},{96,112},{112,64},{1... | collective-permute-start | bytes 393224 | tf_op jit(solution)/shard_map/ppermute | solution.py:285
  55.8 13.0 %collective-permute-start.17 = (bf16[128,512]{1,0:T(8,128)(2,1)S(1)}, bf16[128,512]{1,0:T(8,128)(2,1)S(1)}, u32[]{:S(2)}, u32[]{:S(2)}) collective-permute-start(bf16[128,512]{1,0:T(8,128)(2,1)S(1)} %get-tuple-element.33), channel_id=1, source_target_pairs={{0,48},{16,0},{32,16},{48,32},{64,112},{80,64},{96,80},{112,96},{1... | collective-permute-start | bytes 393224 | tf_op jit(solution)/shard_map/ppermute | solution.py:285
  58.3 10.5 %collective-permute-start.21 = (bf16[128,512]{1,0:T(8,128)(2,1)S(1)}, bf16[128,512]{1,0:T(8,128)(2,1)S(1)}, u32[]{:S(2)}, u32[]{:S(2)}) collective-permute-start(bf16[128,512]{1,0:T(8,128)(2,1)S(1)} %row_total.3), channel_id=1, source_target_pairs={{0,64},{16,80},{32,96},{48,112},{64,128},{80,144},{96,160},{112,17... | collective-permute-start | bytes 393224 | tf_op jit(solution)/shard_map/ppermute | solution.py:302
  59.7 9.1 %collective-permute-start.22 = (bf16[128,512]{1,0:T(8,128)(2,1)S(1)}, bf16[128,512]{1,0:T(8,128)(2,1)S(1)}, u32[]{:S(2)}, u32[]{:S(2)}) collective-permute-start(bf16[128,512]{1,0:T(8,128)(2,1)S(1)} %row_total.3), channel_id=1, source_target_pairs={{0,128},{16,144},{32,160},{48,176},{64,192},{80,208},{96,224},{112... | collective-permute-start | bytes 393224 | tf_op jit(solution)/shard_map/ppermute | solution.py:302
  69.1 9.4 %collective-permute-start.27 = (bf16[128,512]{1,0:T(8,128)(2,1)S(1)}, bf16[128,512]{1,0:T(8,128)(2,1)S(1)}, u32[]{:S(2)}, u32[]{:S(2)}) collective-permute-start(bf16[128,512]{1,0:T(8,128)(2,1)S(1)} %row_total.2), channel_id=1, source_target_pairs={{0,64},{16,80},{32,96},{48,112},{64,128},{80,144},{96,160},{112,17... | collective-permute-start | bytes 393224 | tf_op jit(solution)/shard_map/ppermute | solution.py:302
  70.7 11.3 %collective-permute-start.28 = (bf16[128,512]{1,0:T(8,128)(2,1)S(1)}, bf16[128,512]{1,0:T(8,128)(2,1)S(1)}, u32[]{:S(2)}, u32[]{:S(2)}) collective-permute-start(bf16[128,512]{1,0:T(8,128)(2,1)S(1)} %row_total.2), channel_id=1, source_target_pairs={{0,128},{16,144},{32,160},{48,176},{64,192},{80,208},{96,224},{112... | collective-permute-start | bytes 393224 | tf_op jit(solution)/shard_map/ppermute | solution.py:302
  73.3 8.7 %collective-permute-start.29 = (bf16[128,512]{1,0:T(8,128)(2,1)S(1)}, bf16[128,512]{1,0:T(8,128)(2,1)S(1)}, u32[]{:S(2)}, u32[]{:S(2)}) collective-permute-start(bf16[128,512]{1,0:T(8,128)(2,1)S(1)} %row_total.2), channel_id=1, source_target_pairs={{0,192},{16,208},{32,224},{48,240},{64,0},{80,16},{96,32},{112,48}... | collective-permute-start | bytes 393224 | tf_op jit(solution)/shard_map/ppermute | solution.py:302
  74.2 11.7 %collective-permute-start.24 = (bf16[128,512]{1,0:T(8,128)(2,1)S(1)}, bf16[128,512]{1,0:T(8,128)(2,1)S(1)}, u32[]{:S(2)}, u32[]{:S(2)}) collective-permute-start(bf16[128,512]{1,0:T(8,128)(2,1)S(1)} %get-tuple-element.47), channel_id=1, source_target_pairs={{0,32},{16,48},{32,0},{48,16},{64,96},{80,112},{96,64},{112,80},{1... | collective-permute-start | bytes 393224 | tf_op jit(solution)/shard_map/ppermute | solution.py:285
  78.4 11.0 %collective-permute-start.25 = (bf16[128,512]{1,0:T(8,128)(2,1)S(1)}, bf16[128,512]{1,0:T(8,128)(2,1)S(1)}, u32[]{:S(2)}, u32[]{:S(2)}) collective-permute-start(bf16[128,512]{1,0:T(8,128)(2,1)S(1)} %get-tuple-element.48), channel_id=1, source_target_pairs={{0,16},{16,32},{32,48},{48,0},{64,80},{80,96},{96,112},{112,64},{1... | collective-permute-start | bytes 393224 | tf_op jit(solution)/shard_map/ppermute | solution.py:285
  78.5 15.5 %collective-permute-start.26 = (bf16[128,512]{1,0:T(8,128)(2,1)S(1)}, bf16[128,512]{1,0:T(8,128)(2,1)S(1)}, u32[]{:S(2)}, u32[]{:S(2)}) collective-permute-start(bf16[128,512]{1,0:T(8,128)(2,1)S(1)} %get-tuple-element.49), channel_id=1, source_target_pairs={{0,48},{16,0},{32,16},{48,32},{64,112},{80,64},{96,80},{112,96},{1... | collective-permute-start | bytes 393224 | tf_op jit(solution)/shard_map/ppermute | solution.py:285
  82.3 11.8 %collective-permute-start.30 = (bf16[128,512]{1,0:T(8,128)(2,1)S(1)}, bf16[128,512]{1,0:T(8,128)(2,1)S(1)}, u32[]{:S(2)}, u32[]{:S(2)}) collective-permute-start(bf16[128,512]{1,0:T(8,128)(2,1)S(1)} %get-tuple-element.52), channel_id=1, source_target_pairs={{0,32},{16,48},{32,0},{48,16},{64,96},{80,112},{96,64},{112,80},{1... | collective-permute-start | bytes 393224 | tf_op jit(solution)/shard_map/ppermute | solution.py:285
  83.6 15.9 %collective-permute-start.31 = (bf16[128,512]{1,0:T(8,128)(2,1)S(1)}, bf16[128,512]{1,0:T(8,128)(2,1)S(1)}, u32[]{:S(2)}, u32[]{:S(2)}) collective-permute-start(bf16[128,512]{1,0:T(8,128)(2,1)S(1)} %get-tuple-element.53), channel_id=1, source_target_pairs={{0,16},{16,32},{32,48},{48,0},{64,80},{80,96},{96,112},{112,64},{1... | collective-permute-start | bytes 393224 | tf_op jit(solution)/shard_map/ppermute | solution.py:285
  85.9 16.0 %collective-permute-start.32 = (bf16[128,512]{1,0:T(8,128)(2,1)S(1)}, bf16[128,512]{1,0:T(8,128)(2,1)S(1)}, u32[]{:S(2)}, u32[]{:S(2)}) collective-permute-start(bf16[128,512]{1,0:T(8,128)(2,1)S(1)} %get-tuple-element.54), channel_id=1, source_target_pairs={{0,48},{16,0},{32,16},{48,32},{64,112},{80,64},{96,80},{112,96},{1... | collective-permute-start | bytes 393224 | tf_op jit(solution)/shard_map/ppermute | solution.py:285
  (10 other events, 64.0 us)
